TPU v7x, 128 devices: a whole 4x4x4 slice. The times are simulated.
128 devices in a mesh: ctx: 32 (over x, z_lo, y), head: 4 (over z_hi, core).
Axes of the slice: x: 4, y: 4, z: 4 (z_hi: 2, z_lo: 2; z = z_hi * 2 + z_lo), core: 2. Of those that a mesh axis runs over, the one named last changes fastest.
Arguments:
- raw_values: bfloat16 [8192, 16384], P('ctx', 'head'), may hold values from -3 to 3
- state_ports: bfloat16 [8192, 2, 2048], P('ctx', None, 'head'), may hold values from -0.75 to 0.75
- step_raw: float32 [8192, 256], P('ctx', 'head')
- decay_log: float32 [256], P('head')
- skip_gain: float32 [256], P('head'), may hold values from 0.5 to 1.5
- conv_values: bfloat16 [4, 16384], P(None, 'head'), may hold values from -3 to 3
- conv_ports: bfloat16 [4, 2, 2048], P(None, None, 'head'), may hold values from -3 to 3
- prompt_slot: int32 [32], P('ctx'), may hold values from 0 to 1
- row_slot: int32 [256], P('ctx'), may hold values from 0 to 1, as said below
- cache_states: bfloat16 [64, 256, 64, 256], P('ctx', 'head'), may hold values from -6 to 6
- cache_values: bfloat16 [64, 3, 16384], P('ctx', None, 'head'), may hold values from -3 to 3
- cache_ports: bfloat16 [64, 3, 2, 2048], P('ctx', None, None, 'head'), may hold values from -0.75 to 0.75
- new_values: bfloat16 [4, 256, 16384], P(None, 'ctx', 'head'), may hold values from -3 to 3
- new_ports: bfloat16 [4, 256, 2, 2048], P(None, 'ctx', None, 'head'), may hold values from -0.75 to 0.75
- new_steps: float32 [4, 256, 256], P(None, 'ctx', 'head'), may hold values from -2 to 60
- out_weight: bfloat16 [16384, 8192], P('head', 'ctx'), may hold values from -0.046875 to 0.046875
Outputs:
- scan_out: bfloat16 [8192, 16384], P('ctx', 'head')
- decoded_out: bfloat16 [4, 256, 8192], P(None, 'head', 'ctx')
Inputs may be any that keep to these rules, and one draw needn't show every extreme that they name: `row_slot`: every slot of a group is read by one or more of the group's 8 rows.
All inputs are finite; a program needn't handle non-finite values.
Results may differ from a plain program's by a relative error of at most 0.013.
Values may be sent and summed in bfloat16 or wider, within the bound.
No kernel may reach another device: no remote copies, remote signals or barrier semaphores. Data moves between devices by JAX's collectives and lax.ppermute only.
A program may use at most 320 MiB of HBM per device.

v0:
```python
import jax
import jax.numpy as jnp
from jax import lax
from jax.sharding import PartitionSpec as P

P_SIZE = 64
N = 256
CONV = 4
SPAN = 256


def from_behind(value, axis, by):
    devices = lax.axis_size(axis)
    pairs = [(i, i + by) for i in range(devices) if 0 <= i + by < devices]
    return lax.ppermute(value, axis, pairs)


def carried_in(part, axis, combine, identity):
    place = lax.axis_index(axis)
    gathered = jax.tree.map(lambda a: lax.all_gather(a, axis), part)
    state = jax.tree.map(lambda a, e: jnp.zeros_like(a) + jnp.asarray(e, a.dtype), part, identity)

    def one(turn, state):
        return combine(
            state, jax.tree.map(lambda a: lax.dynamic_index_in_dim(a, turn, 0, False), gathered)
        )

    return lax.fori_loop(0, place, one, state)


def spread(value, axis, source):
    kept = jnp.where(lax.axis_index(axis) == source, value, 0).astype(value.dtype)
    return lax.psum(kept, axis)


def window_mix(windows, weights):
    mixture = weights[0].astype(jnp.float32) * windows[0].astype(jnp.float32)
    for position in range(1, len(windows)):
        mixture = mixture + weights[position].astype(jnp.float32) * windows[position].astype(
            jnp.float32
        )
    return jax.nn.silu(mixture).astype(jnp.bfloat16)


def chain_join(earlier, later):
    return (earlier[0] + later[0], jnp.exp(later[0])[:, None, None] * earlier[1] + later[1])


def shards(
    raw_values,
    state_ports,
    step_raw,
    decay_log,
    skip_gain,
    conv_values,
    conv_ports,
    prompt_slot,
    row_slot,
    cache_states,
    cache_values,
    cache_ports,
    new_values,
    new_ports,
    new_steps,
    out_weight,
):
    length = raw_values.shape[0]
    width_dev = raw_values.shape[1]
    head_dev = decay_log.shape[0]
    group_dev = state_ports.shape[2] // N
    per_group = head_dev // group_dev
    rim_rows = CONV - 1
    blocks = length // SPAN
    tail_values = raw_values[length - rim_rows :]
    tail_ports = state_ports[length - rim_rows :]
    rim_values, rim_ports = from_behind((tail_values, tail_ports), "ctx", 1)
    padded_values = jnp.concatenate([rim_values, raw_values], axis=0)
    padded_ports = jnp.concatenate([rim_ports, state_ports], axis=0)
    value_mix = window_mix(
        [padded_values[position : position + length] for position in range(CONV)], conv_values
    )
    port_mix = window_mix(
        [padded_ports[position : position + length] for position in range(CONV)], conv_ports
    )
    decay_rate = -jnp.exp(decay_log)
    step_sizes = jax.nn.softplus(step_raw)
    step_blocks = step_sizes.reshape(blocks, SPAN, head_dev)
    running = jnp.cumsum(step_blocks * decay_rate[None, None, :], axis=1)
    endings = running[:, -1]
    value_blocks = value_mix.reshape(blocks, SPAN, group_dev, per_group, P_SIZE)
    write_rows = port_mix[:, 0].reshape(blocks, SPAN, group_dev, N)
    read_rows = port_mix[:, 1].reshape(blocks, SPAN, group_dev, N)
    factors = (step_blocks * jnp.exp(endings[:, None, :] - running)).reshape(
        blocks, SPAN, group_dev, per_group
    )
    scaled = (value_blocks.astype(jnp.float32) * factors[..., None]).astype(jnp.bfloat16)
    fresh_states = jnp.einsum(
        "kqgjp,kqgn->kgjpn", scaled, write_rows, preferred_element_type=jnp.float32
    )
    carry_local = jnp.zeros(fresh_states.shape[1:], jnp.float32)
    local_in = [carry_local]
    carry_local = (
        jnp.exp(endings[0]).reshape(group_dev, per_group)[:, :, None, None] * carry_local
        + fresh_states[0]
    )
    total_log = jnp.sum(endings, axis=0)
    local_state = carry_local.reshape(head_dev, P_SIZE, N)
    before_log, before_state = carried_in(
        (total_log, local_state),
        "ctx",
        chain_join,
        (jnp.zeros_like(total_log), jnp.zeros_like(local_state)),
    )
    leading = jnp.cumsum(endings, axis=0) - endings
    incoming = (
        jnp.stack(local_in)
        + jnp.exp(leading).reshape(blocks, group_dev, per_group)[..., None, None]
        * before_state.reshape(group_dev, per_group, P_SIZE, N)[None]
    )
    skip_heads = skip_gain.reshape(group_dev, per_group)
    causal = jnp.arange(SPAN)[:, None] >= jnp.arange(SPAN)[None, :]

    def block_out(bundle):
        block_values, write_block, read_block, step_block, run_block, state_block = bundle
        scores = jnp.einsum(
            "tgn,sgn->gts", read_block, write_block, preferred_element_type=jnp.float32
        )
        run_heads = run_block.reshape(SPAN, group_dev, per_group).transpose(1, 2, 0)
        log_gaps = run_heads[..., :, None] - run_heads[..., None, :]
        decays = jnp.where(causal, jnp.exp(jnp.where(causal, log_gaps, 0.0)), 0.0)
        step_heads = step_block.reshape(SPAN, group_dev, per_group).transpose(1, 2, 0)
        weights = (scores[:, None] * decays * step_heads[..., None, :]).astype(jnp.bfloat16)
        within = jnp.einsum(
            "gjts,sgjp->tgjp", weights, block_values, preferred_element_type=jnp.float32
        )
        carried = jnp.exp(run_block).reshape(SPAN, group_dev, per_group)[..., None] * jnp.einsum(
            "tgn,gjpn->tgjp",
            read_block.astype(jnp.float32),
            state_block,
            precision=lax.Precision.HIGHEST,
        )
        return (
            within + carried + skip_heads[None, :, :, None] * block_values.astype(jnp.float32)
        ).astype(jnp.bfloat16)

    outputs = lax.map(
        block_out, (value_blocks, write_rows, read_rows, step_blocks, running, incoming)
    )
    scan_out = outputs.reshape(length, width_dev)
    last_index = lax.axis_size("ctx") - 1
    final_state = (jnp.exp(total_log)[:, None, None] * before_state + local_state).astype(
        jnp.bfloat16
    )
    carried_state, home_values, home_ports = (
        spread(final_state, "ctx", last_index),
        spread(tail_values, "ctx", last_index),
        spread(tail_ports, "ctx", last_index),
    )
    rows_dev = row_slot.shape[0]
    chosen = row_slot == prompt_slot[0]
    start_state = jnp.where(
        chosen[:, None, None, None], carried_state[None], jnp.take(cache_states, row_slot, axis=0)
    ).astype(jnp.float32)
    state_rows = start_state.reshape(rows_dev, group_dev, per_group, P_SIZE, N)
    conv_rows = jnp.where(
        chosen[:, None, None], home_values[None], jnp.take(cache_values, row_slot, axis=0)
    )
    conv_pairs = jnp.where(
        chosen[:, None, None, None], home_ports[None], jnp.take(cache_ports, row_slot, axis=0)
    )
    rates_grouped = decay_rate.reshape(group_dev, per_group)
    results = []
    for step_index in range(new_values.shape[0]):
        window_values = jnp.concatenate([conv_rows, new_values[step_index][:, None]], axis=1)
        window_ports = jnp.concatenate([conv_pairs, new_ports[step_index][:, None]], axis=1)
        value_now = window_mix(
            [window_values[:, position] for position in range(CONV)], conv_values
        )
        ports_now = window_mix([window_ports[:, position] for position in range(CONV)], conv_ports)
        write_now = ports_now[:, 0].reshape(rows_dev, group_dev, N).astype(jnp.float32)
        read_now = ports_now[:, 1].reshape(rows_dev, group_dev, N).astype(jnp.float32)
        size_now = jax.nn.softplus(new_steps[step_index]).reshape(rows_dev, group_dev, per_group)
        decay_now = jnp.exp(size_now * rates_grouped[None])
        value_heads = value_now.astype(jnp.float32).reshape(rows_dev, group_dev, per_group, P_SIZE)
        state_rows = (
            decay_now[..., None, None] * state_rows
            + (size_now[..., None] * value_heads)[..., None] * write_now[:, :, None, None, :]
        )
        readout = jnp.einsum(
            "rgjpn,rgn->rgjp", state_rows, read_now, precision=lax.Precision.HIGHEST
        )
        results.append(
            (readout + skip_heads[None, :, :, None] * value_heads)
            .astype(jnp.bfloat16)
            .reshape(rows_dev, width_dev)
        )
        conv_rows = window_values[:, 1:]
        conv_pairs = window_ports[:, 1:]
    decoded = jnp.stack(results)
    partials = jnp.einsum(
        "srk,kd->srd",
        lax.all_gather(decoded, "ctx", axis=1, tiled=True),
        out_weight,
        preferred_element_type=jnp.float32,
    )
    decoded_out = lax.psum_scatter(partials, "head", scatter_dimension=1, tiled=True).astype(
        jnp.bfloat16
    )
    return (scan_out, decoded_out)


def solution(mesh):
    in_specs = (
        P("ctx", "head"),
        P("ctx", None, "head"),
        P("ctx", "head"),
        P("head"),
        P("head"),
        P(None, "head"),
        P(None, None, "head"),
        P("ctx"),
        P("ctx"),
        P("ctx", "head", None, None),
        P("ctx", None, "head"),
        P("ctx", None, None, "head"),
        P(None, "ctx", "head"),
        P(None, "ctx", None, "head"),
        P(None, "ctx", "head"),
        P("head", "ctx"),
    )
    out_specs = (P("ctx", "head"), P(None, "head", "ctx"))
    return jax.shard_map(shards, mesh=mesh, in_specs=in_specs, out_specs=out_specs, check_vma=False)
```

profile of v0, /device:TPU:1, one launch (start us, length us, event | category | flops | bytes accessed | tf_op | source)
XLA Modules:
  0.0 2315.9 jit_solution(6753883359378057287)
XLA Ops:
  8.2 4.0 collective-permute-start
  13.0 3.2 collective-permute-start.1
  20.8 1.7 exponential_reduce_fusion
  26.9 6.4 multiply_convert_fusion.2
  33.2 4.1 copy.86
  37.4 2.4 fusion.55
  39.8 2.0 copy-done.2
  41.7 2.3 bitcast_add_fusion.2
  46.2 140.4 %all-reduce = (bf16[3,2,512]{2,0,1:T(4,128)(2,1)S(1)}, bf16[3,4096]{1,0:T(4,128)(2,1)S(1)}) all-reduce(bf16[3,2,512]{2,0,1:T(4,128)(2,1)S(1)} %get-tuple-element.163, bf16[3,4096]{1,0:T(4,128)(2,1)S(1)} %get-tuple-element.128), channel_id=1, replica_groups=mesh['ctx'=32,'head'=4] {'ctx'}, use_global_device_ids=true, to_apply=%region_6.7 | all-reduce | flops 15360 | bytes 61440 | tf_op jit(solution)/shard_map/psum | solution.py:33
  188.9 5.3 fusion.96
  194.3 6.3 gather_fusion.3
  200.5 6.4 gather_fusion.2
  208.4 67.4 %all-gather = f32[32,1,64]{2,1,0:T(1,128)S(1)} all-gather(f32[1,1,64]{2,1,0:T(1,128)S(1)} %copy.96), channel_id=2, replica_groups=mesh['ctx'=32,'head'=4] {'ctx'}, dimensions={0}, use_global_device_ids=true | all-gather | bytes 8448 | tf_op jit(solution)/shard_map/all_gather | solution.py:20
  276.7 1182.4 %all-gather.4.cloned.1.call-done = f32[32,64,64,256]{3,2,1,0:T(8,128)} async-done(((f32[1,64,64,256]{3,2,1,0:T(8,128)}), f32[32,64,64,256]{3,2,1,0:T(8,128)}) %all-gather.4.cloned.1.call-update) | async-done | bytes 134217744 | tf_op jit(solution)/shard_map/all_gather | solution.py:20
  1459.0 2.5 broadcast_in_dim.127
  1462.2 5.5 fusion.54
  1476.2 1.7 reshape.718
  1485.8 2.7 convert_multiply_fusion.9
  1488.5 14.2 pad_maximum_fusion
  1502.7 435.0 %all-reduce.3.cloned.1.call-done = bf16[2,32,64,256]{3,2,1,0:T(8,128)(2,1)} async-done(((bf16[2,32,64,256]{3,2,1,0:T(8,128)(2,1)}), bf16[2,32,64,256]{3,2,1,0:T(8,128)(2,1)}) %all-reduce.3.cloned.1.call-update) | async-done | bytes 2097168 | tf_op jit(solution)/shard_map/psum | solution.py:33
  1937.8 9.0 select_select_fusion
  1946.8 26.7 %fusion.4 = f32[8,2,1,32,64]{4,2,3,1,0:T(1,128)S(1)} fusion(bf16[8,2,256,1,1]{2,3,4,1,0:T(2,128)(2,1)S(1)} %bitcast.194, bf16[8,2,32,64,256]{4,3,2,1,0:T(8,128)(2,1)S(1)} %select_select_fusion, f32[8,2,256]{2,1,0:T(2,128)S(1)} %copy-done.28, f32[8,2,32,64]{3,2,1,0:T(8,128)S(1)} %copy-done.14, f32[8,2,32]{2,1,0:T(2,128)S(1)} %copy-done.38), kind=kOutput, calls=%fused_computation.13 | convolution fusion | flops 134217728 | bytes 17065984 | tf_op jit(solution)/shard_map/rgjpn,rgn->rgjp/dot_general | solution.py:189
  1973.6 28.6 %fusion.5 = f32[8,2,1,32,64]{4,2,3,1,0:T(1,128)S(1)} fusion(bf16[8,2,256,1,1]{2,3,4,1,0:T(2,128)(2,1)S(1)} %bitcast.195, bf16[8,2,32,64,256]{4,3,2,1,0:T(8,128)(2,1)S(1)} %select_select_fusion, f32[8,2,256]{2,1,0:T(2,128)S(1)} %reshape.717, f32[8,2,32,64]{3,2,1,0:T(8,128)S(1)} %copy-done.15, f32[8,2,32]{2,1,0:T(2,128)S(1)} %copy-done.39, ...), kind=kOutput, calls=%fused_computation.14 | convolution fusion | flops 159383552 | bytes 17215488 | tf_op jit(solution)/shard_map/rgjpn,rgn->rgjp/dot_general | solution.py:189
  2002.2 32.0 %fusion.6 = f32[8,2,1,32,64]{4,2,3,1,0:T(1,128)S(1)} fusion(bf16[8,2,256,1,1]{2,3,4,1,0:T(2,128)(2,1)S(1)} %bitcast.196, bf16[8,2,32,64,256]{4,3,2,1,0:T(8,128)(2,1)S(1)} %select_select_fusion, f32[8,2,256]{2,1,0:T(2,128)S(1)} %copy-done.31, f32[8,2,32,64]{3,2,1,0:T(8,128)S(1)} %copy-done.16, f32[8,2,32]{2,1,0:T(2,128)S(1)} %copy-done.40, ...), kind=kOutput, calls=%fused_computation.15 | convolution fusion | flops 184549376 | bytes 17364992 | tf_op jit(solution)/shard_map/rgjpn,rgn->rgjp/dot_general | solution.py:189
  2034.4 41.9 %fusion = f32[8,2,1,32,64]{4,2,3,1,0:T(1,128)S(1)} fusion(bf16[8,2,256,1,1]{2,3,4,1,0:T(2,128)(2,1)S(1)} %bitcast.198, bf16[8,2,32,64,256]{4,3,2,1,0:T(8,128)(2,1)S(1)} %select_select_fusion, f32[8,2,256]{2,1,0:T(2,128)S(1)} %copy-done.33, f32[8,2,32,64]{3,2,1,0:T(8,128)S(1)} %copy-done.17, f32[8,2,32]{2,1,0:T(2,128)S(1)} %copy-done.41, ...), kind=kOutput, calls=%fused_computation.6 | convolution fusion | flops 209715200 | bytes 17514496 | tf_op jit(solution)/shard_map/rgjpn,rgn->rgjp/dot_general | solution.py:189
  2078.5 170.3 %all-gather.6.cloned.1.call-done = bf16[4,256,4096]{2,1,0:T(8,128)(2,1)} async-done(((bf16[4,8,4096]{2,1,0:T(8,128)(2,1)}), bf16[4,256,4096]{2,1,0:T(8,128)(2,1)}) %all-gather.6.cloned.1.call-update) | async-done | bytes 8388624 | tf_op jit(solution)/shard_map/all_gather | solution.py:202
  2248.8 6.7 fusion.57
  2255.8 4.5 fusion.50
  2260.4 6.8 fusion.46
  2267.2 4.1 copy.103
  2271.3 36.5 %reduce-scatter.2.cloned.1.call-done = f32[4,64,256]{2,1,0:T(8,128)} async-done(((f32[4,256,256]{2,1,0:T(8,128)}), f32[4,64,256]{2,1,0:T(8,128)}) %reduce-scatter.2.cloned.1.call-update) | async-done | bytes 262160 | tf_op jit(solution)/shard_map/reduce_scatter | solution.py:206
  2307.8 1.6 convert_element_type.503
  (185 shorter events, 36.1 us)
Async XLA Ops:
  7.2 2241.6 %copy-start = (bf16[4096,256]{1,0:T(8,128)(2,1)S(1)}, bf16[4096,256]{1,0:T(8,128)(2,1)}, u32[]{:S(2)}) copy-start(bf16[4096,256]{1,0:T(8,128)(2,1)} %param.33) | copy-start | bytes 6291460
  7.2 1451.9 %all-gather.4.cloned.1.call-start = ((), (), s32[]{:S(2)}) async-start(), calls=%async_computation.1 | async-start | bytes 138412032 | tf_op jit(solution)/shard_map/all_gather | solution.py:20
  8.2 18.6 collective-permute-start
  13.0 11.5 collective-permute-start.1
  20.4 167.1 %copy-start.22 = (f32[2,512]{1,0:T(2,128)}, f32[2,512]{1,0:T(2,128)S(1)}, u32[]{:S(2)}) copy-start(f32[2,512]{1,0:T(2,128)S(1)} %get-tuple-element.159) | copy-start | bytes 12292
  20.4 167.1 %copy-start.23 = (f32[2,512]{1,0:T(2,128)}, f32[2,512]{1,0:T(2,128)S(1)}, u32[]{:S(2)}) copy-start(f32[2,512]{1,0:T(2,128)S(1)} %get-tuple-element.160) | copy-start | bytes 12292
  20.4 167.1 %copy-start.24 = (f32[2,512]{1,0:T(2,128)}, f32[2,512]{1,0:T(2,128)S(1)}, u32[]{:S(2)}) copy-start(f32[2,512]{1,0:T(2,128)S(1)} %get-tuple-element.161) | copy-start | bytes 12292
  20.4 167.1 %copy-start.25 = (f32[2,512]{1,0:T(2,128)}, f32[2,512]{1,0:T(2,128)S(1)}, u32[]{:S(2)}) copy-start(f32[2,512]{1,0:T(2,128)S(1)} %get-tuple-element.162) | copy-start | bytes 12292
  37.4 149.3 %copy-start.47 = (s32[8]{0:T(128)S(1)}, s32[8]{0:T(128)}, u32[]{:S(2)}) copy-start(s32[8]{0:T(128)} %param.26) | copy-start | bytes 100
  37.4 149.3 %copy-start.21 = (bf16[2,3,2,512]{3,2,1,0:T(2,128)(2,1)S(1)}, bf16[2,3,2,512]{3,2,1,0:T(2,128)(2,1)}, u32[]{:S(2)}) copy-start(bf16[2,3,2,512]{3,2,1,0:T(2,128)(2,1)} %param.29) | copy-start | bytes 36868
  37.4 150.2 %copy-start.20 = (bf16[4,8,2,512]{3,2,1,0:T(2,128)(2,1)S(1)}, bf16[4,8,2,512]{3,2,1,0:T(2,128)(2,1)}, u32[]{:S(2)}) copy-start(bf16[4,8,2,512]{3,2,1,0:T(2,128)(2,1)} %param.31) | copy-start | bytes 196612
  44.1 1893.6 %all-reduce.3.cloned.1.call-start = ((), (), s32[]{:S(2)}) async-start(), calls=%async_computation.2 | async-start | bytes 4194304 | tf_op jit(solution)/shard_map/psum | solution.py:33
  187.3 88.5 %copy-start.34 = (pred[8]{0:T(512)(128)(4,1)}, pred[8]{0:T(512)(128)(4,1)S(1)}, u32[]{:S(2)}) copy-start(pred[8]{0:T(512)(128)(4,1)S(1)} %get-tuple-element.177) | copy-start | bytes 28
  187.3 88.5 %copy-start.36 = (pred[8]{0:T(512)(128)(4,1)}, pred[8]{0:T(512)(128)(4,1)S(1)}, u32[]{:S(2)}) copy-start(pred[8]{0:T(512)(128)(4,1)S(1)} %get-tuple-element.178) | copy-start | bytes 28
  200.5 75.4 %copy-start.13 = (bf16[4,8,4096]{2,1,0:T(8,128)(2,1)S(1)}, bf16[4,8,4096]{2,1,0:T(8,128)(2,1)}, u32[]{:S(2)}) copy-start(bf16[4,8,4096]{2,1,0:T(8,128)(2,1)} %param.30) | copy-start | bytes 786436
  1467.7 781.0 %all-gather.6.cloned.1.call-start = ((), (), s32[]{:S(2)}) async-start(), calls=%async_computation.3 | async-start | bytes 8650752 | tf_op jit(solution)/shard_map/all_gather | solution.py:202
  1488.5 449.3 %copy-start.35 = (pred[8]{0:T(512)(128)(4,1)S(1)}, pred[8]{0:T(512)(128)(4,1)}, u32[]{:S(2)}) copy-start(pred[8]{0:T(512)(128)(4,1)} %copy-done.34) | copy-start | bytes 28
  1488.5 449.3 %copy-start.37 = (pred[8]{0:T(512)(128)(4,1)S(1)}, pred[8]{0:T(512)(128)(4,1)}, u32[]{:S(2)}) copy-start(pred[8]{0:T(512)(128)(4,1)} %copy-done.36) | copy-start | bytes 28
  1973.5 28.7 %copy-start.16 = (f32[8,2,32,64]{3,2,1,0:T(8,128)S(1)}, f32[8,2,32,64]{3,2,1,0:T(8,128)}, u32[]{:S(2)}) copy-start(f32[8,2,32,64]{3,2,1,0:T(8,128)} %get-tuple-element.132) | copy-start | bytes 393220
  2002.2 32.1 %copy-start.17 = (f32[8,2,32,64]{3,2,1,0:T(8,128)S(1)}, f32[8,2,32,64]{3,2,1,0:T(8,128)}, u32[]{:S(2)}) copy-start(f32[8,2,32,64]{3,2,1,0:T(8,128)} %get-tuple-element.134) | copy-start | bytes 393220
  2002.2 32.1 %copy-start.32 = (bf16[8,1,512]{2,1,0:T(2,128)(2,1)S(1)}, bf16[8,1,512]{2,1,0:T(2,128)(2,1)}, u32[]{:S(2)}) copy-start(bf16[8,1,512]{2,1,0:T(2,128)(2,1)} %slice.321) | copy-start | bytes 24580
  2002.2 32.1 %copy-start.33 = (f32[8,2,256]{2,1,0:T(2,128)S(1)}, f32[8,2,256]{2,1,0:T(2,128)}, u32[]{:S(2)}) copy-start(f32[8,2,256]{2,1,0:T(2,128)} %reshape.723) | copy-start | bytes 49156
  2002.2 32.1 %copy-start.41 = (f32[8,2,32]{2,1,0:T(2,128)S(1)}, f32[8,2,32]{2,1,0:T(2,128)}, u32[]{:S(2)}) copy-start(f32[8,2,32]{2,1,0:T(2,128)} %get-tuple-element.173) | copy-start | bytes 6148
  2034.3 42.0 %copy-start.9 = (bf16[8,2,32,64]{3,2,1,0:T(8,128)(2,1)S(1)}, bf16[8,2,32,64]{3,2,1,0:T(8,128)(2,1)}, u32[]{:S(2)}) copy-start(bf16[8,2,32,64]{3,2,1,0:T(8,128)(2,1)} %get-tuple-element.131) | copy-start | bytes 196612
  2034.3 42.0 %copy-start.10 = (bf16[8,2,32,64]{3,2,1,0:T(8,128)(2,1)S(1)}, bf16[8,2,32,64]{3,2,1,0:T(8,128)(2,1)}, u32[]{:S(2)}) copy-start(bf16[8,2,32,64]{3,2,1,0:T(8,128)(2,1)} %get-tuple-element.133) | copy-start | bytes 196612
  2034.3 42.0 %copy-start.11 = (bf16[8,2,32,64]{3,2,1,0:T(8,128)(2,1)S(1)}, bf16[8,2,32,64]{3,2,1,0:T(8,128)(2,1)}, u32[]{:S(2)}) copy-start(bf16[8,2,32,64]{3,2,1,0:T(8,128)(2,1)} %get-tuple-element.135) | copy-start | bytes 196612
  2034.3 42.0 %copy-start.44 = (f32[2,32]{1,0:T(2,128)S(1)}, f32[2,32]{1,0:T(2,128)}, u32[]{:S(2)}) copy-start(f32[2,32]{1,0:T(2,128)} %mul.811) | copy-start | bytes 772
  2034.3 44.0 %copy-start.8 = (f32[1,256,64]{1,0,2:T(1,128)S(1)}, f32[1,256,64]{1,0,2:T(1,128)}, u32[]{:S(2)}) copy-start(f32[1,256,64]{1,0,2:T(1,128)} %copy-done.7) | copy-start | bytes 196612
  2034.4 44.0 %copy-start.45 = (f32[64]{0:T(128)S(1)}, f32[64]{0:T(128)}, u32[]{:S(2)}) copy-start(f32[64]{0:T(128)} %get-tuple-element.92) | copy-start | bytes 772
  2078.1 177.5 %copy-start.4 = (bf16[256,1,512]{0,2,1:T(8,128)(2,1)S(1)}, bf16[256,1,512]{0,2,1:T(8,128)(2,1)}, u32[]{:S(2)}) copy-start(bf16[256,1,512]{0,2,1:T(8,128)(2,1)} %get-tuple-element.137) | copy-start | bytes 786436
  2078.1 177.5 %copy-start.6 = (bf16[256,1,512]{0,2,1:T(8,128)(2,1)S(1)}, bf16[256,1,512]{0,2,1:T(8,128)(2,1)}, u32[]{:S(2)}) copy-start(bf16[256,1,512]{0,2,1:T(8,128)(2,1)} %copy-done.5) | copy-start | bytes 786436
  2078.1 229.7 %reduce-scatter.2.cloned.1.call-start = ((), (), s32[]{:S(2)}) async-start(), calls=%async_computation.4 | async-start | bytes 1310720 | tf_op jit(solution)/shard_map/reduce_scatter | solution.py:206
  (23 other events, 285.9 us)
Sparse Core Ops, SparseCore 0:
  44.2 1414.7 all-gather.3
  1467.8 469.8 all-reduce.2
  2078.2 170.5 all-gather.5
  2255.6 52.0 reduce-scatter.1
where the time goes:
time: 2320 us
  waiting for transfers between devices  1820 us (78%)
  blocking collectives  208 us (9%)
  matrix products  150 us (6%)
  other arithmetic  57.2 us (2%)
  local copies, waits for them, and re-layouts  53.7 us (2%)
    all_gather x1, waiting for transfers between devices, carried_in(): gathered = jax.tree.map(lambda a: lax.all_gather(a, axis), part)  1180 us
    psum x1, waiting for transfers between devices, spread(): return lax.psum(kept, axis)  435 us
    all_gather x1, waiting for transfers between devices, shards(): lax.all_gather(decoded, 'ctx', axis=1, tiled=True)  170 us
    psum x1, blocking collectives, spread(): return lax.psum(kept, axis)  140 us
    dot_general x4, matrix products, shards(): jnp.einsum('rgjpn,rgn->rgjp', state_rows, read_now, precision=lax.Precisi...  129 us
    all_gather x1, blocking collectives, carried_in(): gathered = jax.tree.map(lambda a: lax.all_gather(a, axis), part)  67.4 us
  transfers between devices with their start and end apart: 6, of which 4 were waited for; matrix products, arithmetic and copies ran while one was open for 4% of the time, Pallas kernels for 0%

commit v1 on v0

v1 whole, which is shorter than its diff:
```python
import functools

import jax
import jax.numpy as jnp
from jax import lax
from jax.experimental import pallas as pl
from jax.experimental.pallas import tpu as pltpu
from jax.sharding import PartitionSpec as P

P_SIZE = 64
N = 256
CONV = 4
SPAN = 256
X, Z, Y = 4, 2, 4
F32 = jnp.float32
BF16 = jnp.bfloat16
SMEM = pl.BlockSpec(memory_space=pltpu.SMEM)
VMEM = pl.BlockSpec(memory_space=pltpu.VMEM)
VMEM_BYTES = 48 * 2**20


def place(x, z, y):
    return (x % X * Z + z % Z) * Y + y % Y


def shifted(value, dx=0, dz=0, dy=0):
    pairs = [
        (place(x, z, y), place(x + dx, z + dz, y + dy))
        for x in range(X)
        for z in range(Z)
        for y in range(Y)
    ]
    return lax.ppermute(value, "ctx", pairs)


def call(kernel, out_shape, scratch=(), n_in=None, us=2.0, grid_spec=None, aliases=None):
    params = dict(
        out_shape=out_shape,
        compiler_params=pltpu.CompilerParams(vmem_limit_bytes=VMEM_BYTES),
        cost_estimate=pl.CostEstimate(
            flops=int(us * 1.0e9), bytes_accessed=int(us * 1.0e6), transcendentals=0
        ),
    )
    if grid_spec is not None:
        return pl.pallas_call(kernel, grid_spec=grid_spec, **params)
    outs = jax.tree.map(lambda _: VMEM, out_shape)
    return pl.pallas_call(
        kernel,
        in_specs=[SMEM] + [VMEM] * (n_in - 1),
        out_specs=outs,
        scratch_shapes=list(scratch),
        **params,
    )


def sds(shape, dtype):
    return jax.ShapeDtypeStruct(shape, dtype)


def silu(value):
    return value * (0.5 + 0.5 * jnp.tanh(0.5 * value))


def softplus(value):
    return jnp.maximum(value, 0.0) + jnp.log1p(jnp.exp(-jnp.abs(value)))


def halves(value):
    high = value.astype(BF16)
    return high, (value - high.astype(F32)).astype(BF16)


def paired(value):
    high, low = halves(value)
    return jnp.concatenate([high.astype(F32), low.astype(F32)], axis=1).astype(BF16)


def head_spread(quarter, heads, width):
    row = lax.broadcasted_iota(jnp.int32, (2 * heads, width), 0)
    col = lax.broadcasted_iota(jnp.int32, (2 * heads, width), 1)
    first = quarter * (width // P_SIZE)
    match = lax.rem(row, heads) == first + lax.div(col, P_SIZE)
    return jnp.where(match, 1.0, 0.0).astype(BF16)


def dot(a, b):
    return jnp.dot(a, b, preferred_element_type=F32)


def dot_nt(a, b):
    return lax.dot_general(a, b, (((1,), (1,)), ((), ())), preferred_element_type=F32)


def ports_kernel(
    ids, ports, rim, taps, steps, steps_t, log_row, log_col,
    read_out, write_t_out, run_out, row_out, factor_out, grow_out, scr,
):
    width = ports.shape[1]
    base = rim.shape[1] - width
    scr[0:8] = rim[:, base:]
    scr[8 : 8 + SPAN] = ports[...].astype(F32)
    half = width // 2
    for part in range(2):
        lanes = slice(part * half, (part + 1) * half)
        mixture = taps[0:1, base + part * half : base + (part + 1) * half] * scr[5 : 5 + SPAN, lanes]
        for position in range(1, CONV):
            mixture = mixture + taps[
                position : position + 1, base + part * half : base + (part + 1) * half
            ] * scr[5 + position : 5 + position + SPAN, lanes]
        mixed = silu(mixture)
        if part == 0:
            write_t_out[...] = mixed.astype(BF16).astype(F32).T.astype(BF16)
        else:
            read_out[...] = mixed.astype(BF16)
    rows = lax.broadcasted_iota(jnp.int32, (SPAN, SPAN), 0)
    cols = lax.broadcasted_iota(jnp.int32, (SPAN, SPAN), 1)
    lower = jnp.where(rows >= cols, 1.0, 0.0)
    upper = jnp.where(rows <= cols, 1.0, 0.0)
    size = softplus(steps[...])
    run = jnp.dot(
        lower, size * -jnp.exp(log_row[...]), precision=lax.Precision.HIGHEST,
        preferred_element_type=F32,
    )
    size_t = softplus(steps_t[...])
    run_t = jnp.dot(
        size_t * -jnp.exp(log_col[...]), upper, precision=lax.Precision.HIGHEST,
        preferred_element_type=F32,
    )
    heads = run.shape[1]
    quarter = heads // Y
    for index in range(Y):
        run_out[index] = run[:, index * quarter : (index + 1) * quarter]
    row_out[...] = run_t - jnp.log(size_t)
    ending = run[SPAN - 1 : SPAN]
    factor_out[0:SPAN] = paired(size * jnp.exp(ending - run))
    factor_out[SPAN : SPAN + 16] = paired(jnp.broadcast_to(jnp.exp(ending), (16, heads)))
    grow_out[...] = paired(jnp.exp(run))


def state_kernel(ids, raw, rim, taps, factor, write_t, payload, mixed_out, scr, wide, scaled):
    width = raw.shape[1]
    shift = ids[0]
    scr[0:8] = rim[...]
    scr[8 : 8 + SPAN] = raw[...].astype(F32)
    spread = head_spread(shift, factor.shape[1] // 2, width)
    wide[...] = dot(factor[...], spread)
    rows = 32
    for start in range(0, SPAN, rows):
        mixture = taps[0:1] * scr[start + 5 : start + 5 + rows]
        for position in range(1, CONV):
            at = start + 5 + position
            mixture = mixture + taps[position : position + 1] * scr[at : at + rows]
        mixed = silu(mixture).astype(BF16)
        mixed_out[start : start + rows] = mixed
        scaled[start : start + rows] = (mixed.astype(F32) * wide[start : start + rows]).astype(BF16)
    for start in range(0, width, 256):
        payload[0:N, start : start + 256] = dot(
            write_t[...], scaled[:, start : start + 256]
        ).astype(BF16)
    decay = wide[SPAN : SPAN + 16]
    high = decay.astype(BF16).astype(F32)
    at = lax.broadcasted_iota(jnp.int32, decay.shape, 0)
    tail = jnp.where(at == 0, high, jnp.where(at == 1, decay - high, 0.0))
    payload[N : N + 16] = tail.astype(BF16)


def state_call(quarter, raw, rim, taps, factor, write_t):
    width_dev = raw.shape[1]
    width = width_dev // Y
    per_group = write_t.shape[0] // N
    per = Y // per_group
    grid_spec = pltpu.PrefetchScalarGridSpec(
        num_scalar_prefetch=1,
        grid=(1,),
        in_specs=[
            pl.BlockSpec((SPAN, width), lambda i, s: (0, s[0])),
            pl.BlockSpec((8, width), lambda i, s: (0, s[0])),
            pl.BlockSpec((CONV, width), lambda i, s: (0, s[0])),
            pl.BlockSpec(factor.shape, lambda i, s: (0, 0)),
            pl.BlockSpec((N, SPAN), lambda i, s: (lax.div(s[0], per), 0)),
        ],
        out_specs=[
            pl.BlockSpec((N + 16, width), lambda i, s: (0, 0)),
            pl.BlockSpec((SPAN, width), lambda i, s: (0, 0)),
        ],
        scratch_shapes=[
            pltpu.VMEM((SPAN + 8, width), F32),
            pltpu.VMEM((SPAN + 16, width), F32),
            pltpu.VMEM((SPAN, width), BF16),
        ],
    )
    return call(
        state_kernel,
        (sds((N + 16, width), BF16), sds((SPAN, width), BF16)),
        grid_spec=grid_spec,
        us=3.0,
    )(quarter, raw, rim, taps, factor, write_t)


def within_kernel(ids, read, write_t, run, row, mixed, skip, out, scores):
    scores[...] = dot(read[...], write_t[...])
    half = SPAN // 2
    rows = lax.broadcasted_iota(jnp.int32, (half, half), 0)
    cols = lax.broadcasted_iota(jnp.int32, (half, half), 1)
    causal = rows >= cols
    left = lax.broadcasted_iota(jnp.int32, (half, 2 * P_SIZE), 1) < P_SIZE
    for pair in range(mixed.shape[1] // (2 * P_SIZE)):
        lanes = slice(pair * 2 * P_SIZE, (pair + 1) * 2 * P_SIZE)
        upper, lower = mixed[0:half, lanes], mixed[half:SPAN, lanes]
        tops, bottoms = [], []
        for member in range(2):
            head = 2 * pair + member
            col = run[0, :, head : head + 1]
            line = row[head : head + 1, :]
            w00 = jnp.where(
                causal, scores[0:half, 0:half] * jnp.exp(col[0:half] - line[:, 0:half]), 0.0
            ).astype(BF16)
            w10 = (scores[half:SPAN, 0:half] * jnp.exp(col[half:SPAN] - line[:, 0:half])).astype(BF16)
            w11 = jnp.where(
                causal,
                scores[half:SPAN, half:SPAN] * jnp.exp(col[half:SPAN] - line[:, half:SPAN]),
                0.0,
            ).astype(BF16)
            tops.append(dot(w00, upper))
            bottoms.append(dot(w10, upper) + dot(w11, lower))
        gain = skip[0:1, lanes]
        out[0:half, lanes] = jnp.where(left, tops[0], tops[1]) + gain * upper.astype(F32)
        out[half:SPAN, lanes] = jnp.where(left, bottoms[0], bottoms[1]) + gain * lower.astype(F32)


def within_call(quarter, read, write_t, run, row, mixed, skip):
    width = mixed.shape[1]
    per = Y // (write_t.shape[0] // N)
    heads = width // P_SIZE
    grid_spec = pltpu.PrefetchScalarGridSpec(
        num_scalar_prefetch=1,
        grid=(1,),
        in_specs=[
            pl.BlockSpec((SPAN, N), lambda i, s: (0, lax.div(s[0], per))),
            pl.BlockSpec((N, SPAN), lambda i, s: (lax.div(s[0], per), 0)),
            pl.BlockSpec((1, SPAN, heads), lambda i, s: (s[0], 0, 0)),
            pl.BlockSpec((heads, SPAN), lambda i, s: (s[0], 0)),
            pl.BlockSpec((SPAN, width), lambda i, s: (0, 0)),
            pl.BlockSpec((1, width), lambda i, s: (0, s[0])),
        ],
        out_specs=pl.BlockSpec((SPAN, width), lambda i, s: (0, 0)),
        scratch_shapes=[pltpu.VMEM((SPAN, SPAN), F32)],
    )
    return call(within_kernel, sds((SPAN, width), F32), grid_spec=grid_spec, us=4.0)(
        quarter, read, write_t, run, row, mixed, skip
    )


def carried_kernel(ids, grow, read, *refs):
    withins, states, out = refs[0:Y], refs[Y : 2 * Y], refs[2 * Y]
    width = withins[0].shape[1]
    groups = read.shape[1] // N
    per = Y // groups
    for index in range(Y):
        quarter = lax.rem(ids[2] + index, Y)
        group = lax.div(quarter, per)
        spread = head_spread(quarter, grow.shape[1] // 2, width)
        reads = read[:, pl.ds(pl.multiple_of(group * N, N), N)]
        for start in range(0, width, 256):
            lanes = slice(start, start + 256)
            carried = dot(grow[...], spread[:, lanes]) * dot(reads, states[index][:, lanes])
            out[:, pl.ds(pl.multiple_of(quarter * width + start, 256), 256)] = (
                withins[index][:, lanes] + carried
            ).astype(BF16)


def decay_row(payload):
    tail = payload[N : N + 16].astype(F32)
    return tail[0:1] + tail[1:2]


def row_total_kernel(ids, *refs):
    states, out = refs[0:Y], refs[Y]
    spots = [lax.rem(ids[2] + index, Y) for index in range(Y)]
    decays = [decay_row(state) for state in states]
    width = states[0].shape[1]
    weights = []
    for mine in range(Y):
        weight = jnp.ones((1, width), F32)
        for other in range(Y):
            if other != mine:
                weight = weight * jnp.where(spots[other] > spots[mine], decays[other], 1.0)
        weights.append(weight)
    whole = decays[0] * decays[1] * decays[2] * decays[3]
    at = lax.broadcasted_iota(jnp.int32, (16, width), 0)
    high = whole.astype(BF16).astype(F32)
    tail = jnp.where(at == 0, high, jnp.where(at == 1, whole - high, 0.0)).astype(BF16)
    lanes_each = out.shape[2]
    for owner in range(out.shape[0]):
        lanes = slice(owner * lanes_each, (owner + 1) * lanes_each)
        total = weights[0][:, lanes] * states[0][0:N, lanes].astype(F32)
        for index in range(1, Y):
            total = total + weights[index][:, lanes] * states[index][0:N, lanes].astype(F32)
        out[owner, 0:N] = total.astype(BF16)
        out[owner, N : N + 16] = tail[:, lanes]


def chain_kernel(ids, totals, out):
    carry = jnp.zeros((N, totals.shape[2]), F32)
    for turn in range(totals.shape[0]):
        out[turn, 0:N] = carry.astype(BF16)
        tail = totals[turn, N : N + 16].astype(F32)
        carry = (tail[0:1] + tail[1:2]) * carry + totals[turn, 0:N].astype(F32)
    final = carry.astype(BF16)
    for turn in range(totals.shape[0]):
        out[turn, N : 2 * N] = final


def prefix_kernel(ids, back, *refs):
    states, outs = refs[0:Y], refs[Y : 2 * Y]
    spots = [lax.rem(ids[2] + index, Y) for index in range(Y)]
    decays = [decay_row(state) for state in states]
    lanes_each = back.shape[2]

    def between(low, high):
        weight = jnp.ones(decays[0].shape, F32)
        for other in range(Y):
            inside = spots[other] < high
            if low is not None:
                inside = jnp.logical_and(inside, spots[other] > low)
            weight = weight * jnp.where(inside, decays[other], 1.0)
        return weight

    for target in range(Y):
        base = between(None, spots[target])
        weights = [
            jnp.where(spots[mine] < spots[target], between(spots[mine], spots[target]), 0.0)
            for mine in range(Y)
        ]
        for owner in range(back.shape[0]):
            lanes = slice(owner * lanes_each, (owner + 1) * lanes_each)
            total = base[:, lanes] * back[owner, 0:N].astype(F32)
            for mine in range(Y):
                if mine != target:
                    total = total + weights[mine][:, lanes] * states[mine][0:N, lanes].astype(F32)
            outs[target][:, lanes] = total.astype(BF16)


def decode_kernel(ids, masks, recent, fresh, taps, steps, log_row, skip, cache, out):
    count, rows_dev, channels = fresh.shape
    heads = steps.shape[1]
    width_dev = heads * P_SIZE
    group_dev = (channels - width_dev) // (2 * N)
    chosen = masks[0, :, 0:1] > 0.5
    second = masks[1, :, 0:1] > 0.5
    chosen_rows, second_rows = chosen[0:rows_dev], second[0:rows_dev]
    rim_rows = CONV - 1
    piece = 1024

    def mixes(start):
        lanes = slice(start, start + piece)
        line = []
        for position in range(rim_rows):
            first = recent[position : position + 1, lanes]
            other = recent[rim_rows + position : rim_rows + position + 1, lanes]
            home = recent[2 * rim_rows + position : 2 * rim_rows + position + 1, lanes]
            line.append(jnp.where(chosen_rows, home, jnp.where(second_rows, other, first)))
        line += [fresh[index, :, lanes].astype(F32) for index in range(count)]
        results = []
        for index in range(count):
            mixture = taps[0:1, lanes] * line[index]
            for position in range(1, CONV):
                mixture = mixture + taps[position : position + 1, lanes] * line[index + position]
            results.append(silu(mixture).astype(BF16).astype(F32))
        return results

    ports = mixes(width_dev)
    half = group_dev * N
    size = softplus(steps[...])
    log_decay = size * -jnp.exp(log_row[...])
    sizes = [size[index * rows_dev : (index + 1) * rows_dev] for index in range(count)]
    logs = [log_decay[index * rows_dev : (index + 1) * rows_dev] for index in range(count)]
    lane = lax.broadcasted_iota(jnp.int32, (rows_dev, heads), 1)
    per_group = heads // group_dev
    stack, spots = [], {}
    total = None
    starts = []
    for index in range(count):
        total = logs[index] if total is None else total + logs[index]
        starts.append(jnp.exp(total))
    start_all = jnp.concatenate(starts, axis=0)
    kept = jnp.where(chosen, 0.0, start_all)
    given = jnp.where(chosen, start_all, 0.0)
    for index in range(count):
        gap = None
        for earlier in range(index, -1, -1):
            product = ports[index][:, half : 2 * half] * ports[earlier][:, 0:half]
            meets = jnp.zeros((rows_dev, heads), F32)
            for group in range(group_dev):
                met = jnp.sum(product[:, group * N : (group + 1) * N], axis=1, keepdims=True)
                meets = jnp.where(lax.div(lane, per_group) == group, met, meets)
            weight = meets * sizes[earlier]
            if earlier == index:
                weight = weight + skip[...]
            else:
                gap = logs[earlier + 1] if gap is None else gap + logs[earlier + 1]
                weight = weight * jnp.exp(gap)
            spots[index, earlier] = count * rows_dev + len(stack) * rows_dev
            stack.append(weight)
    coefficients = paired(jnp.concatenate([kept] + stack, axis=0))
    shared = paired(given)
    reads = jnp.concatenate([port[:, half : 2 * half] for port in ports], axis=0).astype(BF16)
    quarters = width_dev // piece
    per = quarters // group_dev
    for quarter in range(quarters):
        lanes = slice(quarter * piece, (quarter + 1) * piece)
        group = quarter // per
        read = reads[:, group * N : (group + 1) * N]
        wide = dot(coefficients, head_spread(quarter, heads, piece))
        values = mixes(quarter * piece)
        met = jnp.where(
            second, dot_nt(read, cache[1, lanes, :]), dot_nt(read, cache[0, lanes, :])
        )
        results = []
        for index in range(count):
            at = index * rows_dev
            line = wide[at : at + rows_dev] * met[at : at + rows_dev]
            for earlier in range(index + 1):
                spot = spots[index, earlier]
                line = line + wide[spot : spot + rows_dev] * values[earlier]
            results.append(line)
        out[quarter, :, 0:piece] = jnp.concatenate(results, axis=0).astype(BF16)
        out[quarter, :, piece : piece + N] = read
        out[quarter, :, piece + N : piece + N + 2 * heads] = shared


def project_kernel(ids, back, *refs):
    pieces, blocks = refs[0:X], refs[X : X + Y]
    keep, send, final, joined = refs[X + Y : X + Y + 4]
    width = joined.shape[1]
    each = back.shape[2]
    for owner in range(back.shape[0]):
        final[:, owner * each : (owner + 1) * each] = back[owner, N : 2 * N]
    pairs = pieces[0].shape[1] - width - N
    spread = head_spread(ids[2], pairs // 2, width)
    for index in range(X):
        spot = lax.rem(ids[0] + index, X)
        same = lax.rem(spot, 2) == ids[3]
        row = lax.div(spot, 2)
        reads = pieces[index][:, width : width + N]
        given = pieces[index][:, width + N :]
        for start in range(0, width, 256):
            lanes = slice(start, start + 256)
            extra = dot(given, spread[:, lanes]) * dot(reads, final[:, lanes])
            joined[:, lanes] = (pieces[index][:, lanes].astype(F32) + extra).astype(BF16)
        for block in range(Y):
            part = dot(joined[...], blocks[block][...])

            @pl.when(same)
            def _():
                keep[block, row] = part

            @pl.when(jnp.logical_not(same))
            def _():
                send[block, row] = part.astype(BF16)


def shards(
    raw_values,
    state_ports,
    step_raw,
    decay_log,
    skip_gain,
    conv_values,
    conv_ports,
    prompt_slot,
    row_slot,
    cache_states,
    cache_values,
    cache_ports,
    new_values,
    new_ports,
    new_steps,
    out_weight,
):
    length, width_dev = raw_values.shape
    heads = decay_log.shape[0]
    ports_dev = 2 * state_ports.shape[2]
    rim_rows = CONV - 1
    width = width_dev // Y
    count, rows_dev = new_steps.shape[0:2]
    me = lax.axis_index("ctx").astype(jnp.int32)
    part = lax.axis_index("head").astype(jnp.int32)
    my_x, my_z, my_y = me // (Z * Y), me // Y % Z, me % Y
    my_core, my_high = part % 2, part // 2
    ids = jnp.stack([my_x, my_z, my_y, my_core])
    quarters = [(my_y + index) % Y for index in range(Y)]
    quarter_ids = [quarter.reshape(1) for quarter in quarters]

    ports_flat = state_ports.reshape(length, ports_dev)
    tails = jnp.concatenate([raw_values[length - rim_rows :], ports_flat[length - rim_rows :]], axis=1)
    devices = X * Z * Y
    rim = lax.ppermute(tails, "ctx", [(i, i + 1) for i in range(devices - 1)])
    rim = jnp.pad(rim.astype(F32), ((8 - rim_rows, 0), (0, 0)))

    last = devices - 1
    home = tails
    at_z = lax.ppermute(home, "ctx", [(last, place(X - 1, Z - 2, Y - 1))])
    home = jnp.where(my_z == Z - 1, home, at_z)
    moved = home
    for step in range(1, Y):
        moved_y = lax.ppermute(
            home, "ctx", [(place(X - 1, z, Y - 1), place(X - 1, z, Y - 1 - step)) for z in range(Z)]
        )
        moved = jnp.where(my_y == Y - 1 - step, moved_y, moved)
    home = moved
    for step in range(1, X):
        moved_x = lax.ppermute(
            home,
            "ctx",
            [(place(X - 1, z, y), place(X - 1 - step, z, y)) for z in range(Z) for y in range(Y)],
        )
        moved = jnp.where(my_x == X - 1 - step, moved_x, moved)
    home = moved

    taps = jnp.concatenate([conv_values, conv_ports.reshape(CONV, ports_dev)], axis=1).astype(F32)
    log_row = decay_log.reshape(1, heads)
    skip_row = skip_gain.reshape(1, heads)
    skip_wide = jnp.repeat(skip_gain, P_SIZE).reshape(1, width_dev)

    read, write_t, run, row, factor, grow = call(
        ports_kernel,
        (
            sds((SPAN, ports_dev // 2), BF16),
            sds((ports_dev // 2, SPAN), BF16),
            sds((Y, SPAN, heads // Y), F32),
            sds((heads, SPAN), F32),
            sds((SPAN + 16, 2 * heads), BF16),
            sds((SPAN, 2 * heads), BF16),
        ),
        scratch=[pltpu.VMEM((SPAN + 8, ports_dev), F32)],
        n_in=8,
        us=4.0,
    )(ids, ports_flat, rim, taps, step_raw, step_raw.T, log_row, decay_log.reshape(heads, 1))

    states, mixed = [None] * Y, [None] * Y
    for index in (1, 3, 2, 0):
        states[index], mixed[index] = state_call(
            quarter_ids[index], raw_values, rim, taps, factor, write_t
        )
    ring = [states[0], None, None, None]
    for index in (1, 3, 2):
        ring[Y - index] = shifted(states[index], dy=index)

    chosen = row_slot == prompt_slot[0]
    masks = jnp.stack([chosen, row_slot == 1]).astype(F32)
    masks = jnp.broadcast_to(jnp.tile(masks, (1, count))[:, :, None], (2, count * rows_dev, 128))
    slots = cache_values.shape[0]
    recent = jnp.concatenate(
        [
            jnp.concatenate(
                [
                    cache_values.reshape(slots * rim_rows, width_dev),
                    cache_ports.reshape(slots * rim_rows, ports_dev),
                ],
                axis=1,
            ),
            home,
        ],
        axis=0,
    ).astype(F32)
    fresh = jnp.concatenate([new_values, new_ports.reshape(count, rows_dev, ports_dev)], axis=2)
    packed_width = width + N + 2 * heads
    packed = call(
        decode_kernel,
        sds((Y, count * rows_dev, packed_width), BF16),
        n_in=9,
        us=6.0,
    )(
        ids,
        masks,
        recent,
        fresh,
        taps,
        new_steps.reshape(count * rows_dev, heads),
        log_row,
        skip_row,
        cache_states.reshape(slots, width_dev, N),
    )
    by_y = [lax.dynamic_index_in_dim(packed, quarters[0], 0, False), None, None, None]
    for index in range(1, Y):
        by_y[Y - index] = shifted(
            lax.dynamic_index_in_dim(packed, quarters[index], 0, False), dy=index
        )
    turned = jnp.concatenate(by_y + by_y[0 : Y - 1], axis=0)
    ordered = lax.dynamic_slice_in_dim(
        turned, (Y - my_y) % Y * count * rows_dev, Y * count * rows_dev, 0
    )
    both = jnp.concatenate([ordered, shifted(ordered, dz=1)], axis=0)
    pieces = [both] + [shifted(both, dx=-index) for index in range(1, X)]

    withins = [
        within_call(quarter_ids[index], read, write_t, run, row, mixed[index], skip_wide)
        for index in range(Y)
    ]

    owners = X * Z
    each = width // owners
    groups = [[place(x, z, y) for x in range(X) for z in range(Z)] for y in range(Y)]
    totals = call(row_total_kernel, sds((owners, N + 16, each), BF16), n_in=1 + Y, us=2.0)(ids, *ring)
    totals = lax.all_to_all(totals, "ctx", 0, 0, tiled=True, axis_index_groups=groups)
    back = call(chain_kernel, sds((owners, 2 * N, each), BF16), n_in=2, us=1.0)(ids, totals)
    back = lax.all_to_all(back, "ctx", 0, 0, tiled=True, axis_index_groups=groups)
    prefixes = call(
        prefix_kernel, tuple(sds((N, width), BF16) for _ in range(Y)), n_in=2 + Y, us=2.5
    )(ids, back, *ring)
    incoming = [prefixes[0], None, None, None]
    for index in (1, 3, 2):
        incoming[Y - index] = shifted(prefixes[index], dy=index)

    blocks = [lax.dynamic_slice_in_dim(out_weight, quarters[0] * width, width, 0), None, None, None]
    for index in (1, 3, 2):
        blocks[Y - index] = shifted(
            lax.dynamic_slice_in_dim(out_weight, quarters[index] * width, width, 0), dy=index
        )
    piece_rows = both.shape[0]
    cols = out_weight.shape[1]
    keep, send = call(
        project_kernel,
        (sds((Y, X // 2, piece_rows, cols), F32), sds((Y, X // 2, piece_rows, cols), BF16)),
        scratch=[pltpu.VMEM((N, width), BF16), pltpu.VMEM((piece_rows, width), BF16)],
        n_in=2 + X + Y,
        us=6.0,
    )(ids, back, *pieces, *blocks)
    other = lax.ppermute(send, "head", [(i, i ^ 1) for i in range(4)])
    joined = keep + other.astype(F32)
    sums = joined[0]
    for index in (1, 3, 2):
        sums = sums + shifted(joined[index].astype(BF16), dy=index).astype(F32)
    theirs = lax.dynamic_index_in_dim(sums, 1 - my_high, 0, False).astype(BF16)
    mine = lax.dynamic_index_in_dim(sums, my_high, 0, False)
    mine = mine + lax.ppermute(theirs, "head", [(i, i ^ 2) for i in range(4)]).astype(F32)
    mine = mine.astype(BF16).reshape(Z, Y, count, rows_dev, cols)
    mine = jnp.where(my_z == 0, mine, mine[::-1])
    decoded_out = mine.transpose(2, 0, 1, 3, 4).reshape(count, Z * Y * rows_dev, cols)

    scan_out = call(carried_kernel, sds((SPAN, width_dev), BF16), n_in=3 + 2 * Y, us=6.0)(
        ids, grow, read, *withins, *incoming
    )
    return scan_out, decoded_out


def solution(mesh):
    in_specs = (
        P("ctx", "head"),
        P("ctx", None, "head"),
        P("ctx", "head"),
        P("head"),
        P("head"),
        P(None, "head"),
        P(None, None, "head"),
        P("ctx"),
        P("ctx"),
        P("ctx", "head", None, None),
        P("ctx", None, "head"),
        P("ctx", None, None, "head"),
        P(None, "ctx", "head"),
        P(None, "ctx", None, "head"),
        P(None, "ctx", "head"),
        P("head", "ctx"),
    )
    out_specs = (P("ctx", "head"), P(None, "head", "ctx"))
    return jax.shard_map(shards, mesh=mesh, in_specs=in_specs, out_specs=out_specs, check_vma=False)
```

time: 2320 us -> 209 us (0.09)
  waiting for transfers between devices: 1820 us -> 85.1 us
  blocking collectives: 208 us -> 0 us
  matrix products: 150 us -> 0 us
  other arithmetic: 57.2 us -> 4.3 us
  starting transfers between devices: 7.8 us -> 51.7 us
  Pallas kernels: 0 us -> 35.8 us
  local copies, waits for them, and re-layouts: 53.7 us -> 28.2 us
    all_gather x2 -> x0, waiting for transfers between devices: 1350 us -> none  [the longest x1 1180 us: carried_in(): gathered = jax.tree.map(lambda a: lax.all_gather(a, axis), part)]
    psum x1 -> x0, waiting for transfers between devices: 435 us -> none  [spread(): return lax.psum(kept, axis)]
    dot_general x9 -> x0, matrix products: 150 us -> none  [the longest x4 129 us: shards(): jnp.einsum('rgjpn,rgn->rgjp', state_rows, read_now, precision=lax.Precisi...]
    psum x1 -> x0, blocking collectives: 140 us -> none  [spread(): return lax.psum(kept, axis)]
    ppermute x2 -> x29, waiting for transfers between devices: 0.01 us -> 84.5 us  [the longest x19 84.5 us: shifted(): return lax.ppermute(value, 'ctx', pairs)]
    all_gather x1 -> x0, blocking collectives: 67.4 us -> none  [carried_in(): gathered = jax.tree.map(lambda a: lax.all_gather(a, axis), part)]
    reduce_scatter x1 -> x0, waiting for transfers between devices: 36.5 us -> none  [shards(): lax.psum_scatter(partials, 'head', scatter_dimension=1, tiled=True)]
    pallas_call x0 -> x15, Pallas kernels: none -> 35.8 us  [the longest x1 10.4 us: shards(): call(project_kernel, (sds((Y, X // 2, piece_rows, cols), F32), sds((Y, X...]
  transfers between devices with their start and end apart: 6 -> 31, of which waited for: 4 -> 10; matrix products, arithmetic and copies ran while one was open for 4% -> 5% of each run, Pallas kernels for 0% -> 11%
where the time goes in v1:
time: 209 us; the launch traced here: 207 us
  waiting for transfers between devices  85.1 us (41%)
  starting transfers between devices  51.7 us (25%)
  Pallas kernels  35.8 us (17%)
  local copies, waits for them, and re-layouts  28.2 us (13%)
  other arithmetic  4.3 us (2%)
  between operations  2.18 us (1%)
    ppermute x19, waiting for transfers between devices, shifted(): return lax.ppermute(value, 'ctx', pairs)  84.5 us
    ppermute x19, starting transfers between devices, shifted(): return lax.ppermute(value, 'ctx', pairs)  23.6 us
    unnamed x107, local copies, waits for them, and re-layouts  21.5 us
    pallas_call x1, Pallas kernels, shards(): call(project_kernel, (sds((Y, X // 2, piece_rows, cols), F32), sds((Y, X...  10.4 us
    all_to_all x1, starting transfers between devices, shards(): lax.all_to_all(totals, 'ctx', 0, 0, tiled=True, axis_index_groups=groups)  9.7 us
    pallas_call x4, Pallas kernels, state_call(): call(state_kernel, (sds((N + 16, width), BF16), sds((SPAN, width), BF16))...  6.95 us
  transfers between devices with their start and end apart: 31, of which 10 were waited for; matrix products, arithmetic and copies ran while one was open for 5% of the time, Pallas kernels for 11%

profile of v1, /device:TPU:1, one launch (start us, length us, event | category | flops | bytes accessed | tf_op | source)
XLA Modules:
  0.0 207.4 jit_solution(1187301463787817371)
XLA Ops:
  2.3 4.0 %collective-permute-start = (bf16[3,5120]{1,0:T(4,128)(2,1)S(1)}, bf16[3,5120]{1,0:T(4,128)(2,1)S(1)}, u32[]{:S(2)}, u32[]{:S(2)}) collective-permute-start(bf16[3,5120]{1,0:T(4,128)(2,1)S(1)} %pad_maximum_fusion.2), channel_id=1, source_target_pairs={{0,4},{4,8},{8,12},{12,16},{16,20},{20,24},{24,28},{28,32},{32,36}... | collective-permute-start | bytes 92168 | tf_op jit(solution)/shard_map/ppermute | solution.py:498
  15.6 2.2 %shard_map.167 = (bf16[256,512]{1,0:T(8,128)(2,1)S(1)}, bf16[512,256]{1,0:T(8,128)(2,1)S(1)}, f32[4,256,16]{2,1,0:T(8,128)S(1)}, f32[64,256]{1,0:T(8,128)S(1)}, ...) custom-call(s32[4]{0:T(128)S(1)} %pad_add_fusion.ids, bf16[256,1024]{1,0:T(8,128)(2,1)S(1)} %bitcast.63, ...), custom_call_target="tpu_custom_call" | custom-call | flops 4000000000 | bytes 4000000 | tf_op jit(solution)/shard_map/pallas_call | solution.py:526
  17.9 1.7 shard_map.168
  19.6 1.7 shard_map.170
  21.4 1.7 shard_map.172
  25.9 1.7 shard_map.174
  27.7 2.8 %collective-permute-start.1 = (bf16[272,1024]{1,0:T(8,128)(2,1)S(1)}, bf16[272,1024]{1,0:T(8,128)(2,1)S(1)}, u32[]{:S(2)}, u32[]{:S(2)}) collective-permute-start(bf16[272,1024]{1,0:T(8,128)(2,1)S(1)} %get-tuple-element.33), channel_id=1, source_target_pairs={{0,12},{4,0},{8,4},{12,8},{16,28},{20,16},{24,20},{28,24},{32,44},... | collective-permute-start | bytes 1671176 | tf_op jit(solution)/shard_map/ppermute | solution.py:33
  31.5 2.4 %shard_map.180 = bf16[4,32,1408]{2,1,0:T(8,128)(2,1)S(1)} custom-call(s32[4]{0:T(128)S(1)} %pad_add_fusion.ids, f32[2,32,128]{2,1,0:T(8,128)S(1)} %broadcast_in_dim.9.masks, f32[9,5120]{1,0:T(8,128)S(1)} %maximum_convert_fusion.recent, bf16[4,8,5120]{2,1,0:T(8,128)(2,1)S(1)} %pad_maximum_fusion.1.fresh, f32[4,5120]{1,0:T(4,128)S(1)} %maximum_convert_fusion.1.taps, ...), custom_call_target="tpu_custom_call" | custom-call | flops 6000000000 | bytes 6000000 | tf_op jit(solution)/shard_map/pallas_call | solution.py:569
  34.0 2.8 %collective-permute-start.14 = (bf16[32,1408]{1,0:T(8,128)(2,1)S(1)}, bf16[32,1408]{1,0:T(8,128)(2,1)S(1)}, u32[]{:S(2)}, u32[]{:S(2)}) collective-permute-start(bf16[32,1408]{1,0:T(8,128)(2,1)S(1)} %get-tuple-element.53), channel_id=1, source_target_pairs={{0,12},{4,0},{8,4},{12,8},{16,28},{20,16},{24,20},{28,24},{32,44},... | collective-permute-start | bytes 270344 | tf_op jit(solution)/shard_map/ppermute | solution.py:33
  38.0 18.1 %collective-permute-done.14 = bf16[32,1408]{1,0:T(8,128)(2,1)S(1)} collective-permute-done((bf16[32,1408]{1,0:T(8,128)(2,1)S(1)}, bf16[32,1408]{1,0:T(8,128)(2,1)S(1)}, u32[]{:S(2)}, u32[]{:S(2)}) %collective-permute-start.14) | collective-permute-done | bytes 90144 | tf_op jit(solution)/shard_map/ppermute | solution.py:33
  56.2 2.3 %collective-permute-done.15 = bf16[32,1408]{1,0:T(8,128)(2,1)S(1)} collective-permute-done((bf16[32,1408]{1,0:T(8,128)(2,1)S(1)}, bf16[32,1408]{1,0:T(8,128)(2,1)S(1)}, u32[]{:S(2)}, u32[]{:S(2)}) %collective-permute-start.15) | collective-permute-done | bytes 90144 | tf_op jit(solution)/shard_map/ppermute | solution.py:33
  58.5 3.4 %collective-permute-done.16 = bf16[32,1408]{1,0:T(8,128)(2,1)S(1)} collective-permute-done((bf16[32,1408]{1,0:T(8,128)(2,1)S(1)}, bf16[32,1408]{1,0:T(8,128)(2,1)S(1)}, u32[]{:S(2)}, u32[]{:S(2)}) %collective-permute-start.16) | collective-permute-done | bytes 90144 | tf_op jit(solution)/shard_map/ppermute | solution.py:33
  62.1 1.9 shard_map.176
  64.8 9.7 %all-to-all-start = ((bf16[8,272,128]{2,1,0:T(8,128)(2,1)}), bf16[8,272,128]{2,1,0:T(8,128)(2,1)S(1)}, u32[]{:S(2)}, u32[]{:S(2)}) async-start(bf16[8,272,128]{2,1,0:T(8,128)(2,1)} %shard_map.176), calls=%async_computation | async-start | bytes 1114112 | tf_op jit(solution)/shard_map/all_to_all | solution.py:606
  75.5 1.5 collective-permute-start.17
  77.1 2.7 %constant_dynamic-slice_fusion = (bf16[1024,256]{1,0:T(8,128)(2,1)}, bf16[1024,256]{1,0:T(8,128)(2,1)}, bf16[1024,256]{1,0:T(8,128)(2,1)S(1)}, bf16[1024,256]{1,0:T(8,128)(2,1)}) fusion(bf16[4096,256]{1,0:T(8,128)(2,1)} %param.31, s32[]{:T(128)S(6)} %select_n.165, s32[]{:T(128)S(6)} %select_n.163, s32[]{:T(128)S(6)} %select_n.162, s32[]{:T(128)S(6)} %select_n.164), kind=kLoop, calls=%fused_computation.34 | loop fusion | bytes 4194320 | tf_op jit(solution)/shard_map/dynamic_slice | solution.py:619
  81.9 1.7 shard_map.177
  83.5 3.6 %all-to-all-start.1 = ((bf16[8,512,128]{2,1,0:T(8,128)(2,1)}), bf16[8,512,128]{2,1,0:T(8,128)(2,1)S(1)}, u32[]{:S(2)}, u32[]{:S(2)}) async-start(bf16[8,512,128]{2,1,0:T(8,128)(2,1)} %shard_map.177), calls=%async_computation.1 | async-start | bytes 2097152 | tf_op jit(solution)/shard_map/all_to_all | solution.py:608
  87.1 1.9 collective-permute-done.17
  90.0 3.1 %collective-permute-start.18 = (bf16[256,1408]{1,0:T(8,128)(2,1)S(1)}, bf16[256,1408]{1,0:T(8,128)(2,1)S(1)}, u32[]{:S(2)}, u32[]{:S(2)}) collective-permute-start(bf16[256,1408]{1,0:T(8,128)(2,1)S(1)} %pad_maximum_fusion.refs_0_), channel_id=1, source_target_pairs={{0,96},{4,100},{8,104},{12,108},{16,112},{20,116},{24,120},{28,124... | collective-permute-start | bytes 2162696 | tf_op jit(solution)/shard_map/ppermute | solution.py:33
  97.1 7.2 %collective-permute-done.22.refs_6_ = bf16[1024,256]{1,0:T(8,128)(2,1)S(1)} collective-permute-done((bf16[1024,256]{1,0:T(8,128)(2,1)}, bf16[1024,256]{1,0:T(8,128)(2,1)S(1)}, u32[]{:S(2)}, u32[]{:S(2)}) %collective-permute-start.22) | collective-permute-done | bytes 524320 | tf_op jit(solution)/shard_map/ppermute | solution.py:33
  105.1 11.2 %collective-permute-done.23.refs_7_ = bf16[1024,256]{1,0:T(8,128)(2,1)S(1)} collective-permute-done((bf16[1024,256]{1,0:T(8,128)(2,1)}, bf16[1024,256]{1,0:T(8,128)(2,1)S(1)}, u32[]{:S(2)}, u32[]{:S(2)}) %collective-permute-start.23) | collective-permute-done | bytes 524320 | tf_op jit(solution)/shard_map/ppermute | solution.py:33
  118.9 13.4 %collective-permute-done.20.refs_3_ = bf16[256,1408]{1,0:T(8,128)(2,1)S(1)} collective-permute-done((bf16[256,1408]{1,0:T(8,128)(2,1)S(1)}, bf16[256,1408]{1,0:T(8,128)(2,1)S(1)}, u32[]{:S(2)}, u32[]{:S(2)}) %collective-permute-start.20) | collective-permute-done | bytes 720928 | tf_op jit(solution)/shard_map/ppermute | solution.py:33
  140.5 10.4 %shard_map.181 = (f32[4,2,256,256]{3,2,1,0:T(8,128)}, bf16[4,2,256,256]{3,2,1,0:T(8,128)(2,1)S(1)}) custom-call(s32[4]{0:T(128)S(1)} %pad_add_fusion.ids, bf16[8,512,128]{2,1,0:T(8,128)(2,1)} %copy-done, bf16[256,1408]{1,0:T(8,128)(2,1)S(1)} %pad_maximum_fusion.refs_0_, bf16[256,1408]{1,0:T(8,128)(2,1)S(1)} %copy-done.8, bf16[256,1408]{1,0:T(8,128)(2,1)S(1)} %copy-done.10, ...), custom_call_target="tpu_custom_call" | custom-call | flops 6000000000 | bytes 6000000 | tf_op jit(solution)/shard_map/pallas_call | solution.py:623
  150.9 2.2 %collective-permute-start.24 = (bf16[4,2,256,256]{3,2,1,0:T(8,128)(2,1)S(1)}, bf16[4,2,256,256]{3,2,1,0:T(8,128)(2,1)S(1)}, u32[]{:S(2)}, u32[]{:S(2)}) collective-permute-start(bf16[4,2,256,256]{3,2,1,0:T(8,128)(2,1)S(1)} %get-tuple-element.41), channel_id=1, source_target_pairs={{0,1},{1,0},{2,3},{3,2},{4,5},{5,4},{6,7},{7,6},{8,9},{9,8},{10,11... | collective-permute-start | bytes 3145736 | tf_op jit(solution)/shard_map/ppermute | solution.py:630
  163.1 2.3 %shard_map.178 = (bf16[256,1024]{1,0:T(8,128)(2,1)S(1)}, bf16[256,1024]{1,0:T(8,128)(2,1)S(1)}, bf16[256,1024]{1,0:T(8,128)(2,1)S(1)}, bf16[256,1024]{1,0:T(8,128)(2,1)S(1)}) custom-call(s32[4]{0:T(128)S(1)} %pad_add_fusion.ids, bf16[8,512,128]{2,1,0:T(8,128)(2,1)S(1)} %copy-done.1, bf16[272,1024]{1,0:T(8,128)(2,1)S(1)} %copy-done.27, ...), custom_call_target="tpu_custom_call" | custom-call | flops 2500000000 | bytes 2500000 | tf_op jit(solution)/shard_map/pallas_call | solution.py:609
  166.9 1.6 collective-permute-start.5
  168.5 2.7 %collective-permute-start.26 = (bf16[2,256,256]{2,1,0:T(8,128)(2,1)S(1)}, bf16[2,256,256]{2,1,0:T(8,128)(2,1)S(1)}, u32[]{:S(2)}, u32[]{:S(2)}) collective-permute-start(bf16[2,256,256]{2,1,0:T(8,128)(2,1)S(1)} %get-tuple-element.50), channel_id=1, source_target_pairs={{0,12},{4,0},{8,4},{12,8},{16,28},{20,16},{24,20},{28,24},{32,44},... | collective-permute-start | bytes 786440 | tf_op jit(solution)/shard_map/ppermute | solution.py:33
  172.3 24.8 %collective-permute-done.26 = bf16[2,256,256]{2,1,0:T(8,128)(2,1)S(1)} collective-permute-done((bf16[2,256,256]{2,1,0:T(8,128)(2,1)S(1)}, bf16[2,256,256]{2,1,0:T(8,128)(2,1)S(1)}, u32[]{:S(2)}, u32[]{:S(2)}) %collective-permute-start.26) | collective-permute-done | bytes 262176 | tf_op jit(solution)/shard_map/ppermute | solution.py:33
  197.1 2.1 %collective-permute-done.25 = bf16[2,256,256]{2,1,0:T(8,128)(2,1)S(1)} collective-permute-done((bf16[2,256,256]{2,1,0:T(8,128)(2,1)S(1)}, bf16[2,256,256]{2,1,0:T(8,128)(2,1)S(1)}, u32[]{:S(2)}, u32[]{:S(2)}) %collective-permute-start.25) | collective-permute-done | bytes 262176 | tf_op jit(solution)/shard_map/ppermute | solution.py:33
  199.3 3.4 %collective-permute-start.28 = (bf16[256,256]{1,0:T(8,128)(2,1)S(1)}, bf16[256,256]{1,0:T(8,128)(2,1)S(1)}, u32[]{:S(2)}, u32[]{:S(2)}) collective-permute-start(bf16[256,256]{1,0:T(8,128)(2,1)S(1)} %fusion.5), channel_id=1, source_target_pairs={{0,2},{1,3},{2,0},{3,1},{4,6},{5,7},{6,4},{7,5},{8,10},{9,11},{10,... | collective-permute-start | bytes 393224 | tf_op jit(solution)/shard_map/ppermute | solution.py:637
  202.7 3.9 %shard_map.179 = bf16[256,4096]{1,0:T(8,128)(2,1)} custom-call(s32[4]{0:T(128)S(1)} %pad_add_fusion.ids, bf16[256,128]{1,0:T(8,128)(2,1)S(1)} %get-tuple-element.22.grow, bf16[256,512]{1,0:T(8,128)(2,1)S(1)} %copy-done.42, f32[256,1024]{1,0:T(8,128)S(1)} %shard_map.169.refs_0_, f32[256,1024]{1,0:T(8,128)S(1)} %shard_map.171.refs_1_, ...), custom_call_target="tpu_custom_call" | custom-call | flops 6000000000 | bytes 6000000 | tf_op jit(solution)/shard_map/pallas_call | solution.py:642
  (184 shorter events, 48.9 us)
Async XLA Ops:
  2.3 13.2 %collective-permute-start = (bf16[3,5120]{1,0:T(4,128)(2,1)S(1)}, bf16[3,5120]{1,0:T(4,128)(2,1)S(1)}, u32[]{:S(2)}, u32[]{:S(2)}) collective-permute-start(bf16[3,5120]{1,0:T(4,128)(2,1)S(1)} %pad_maximum_fusion.2), channel_id=1, source_target_pairs={{0,4},{4,8},{8,12},{12,16},{16,20},{20,24},{24,28},{28,32},{32,36}... | collective-permute-start | bytes 92168 | tf_op jit(solution)/shard_map/ppermute | solution.py:498
  6.4 7.1 %collective-permute-start.7 = (bf16[3,5120]{1,0:T(4,128)(2,1)S(1)}, bf16[3,5120]{1,0:T(4,128)(2,1)S(1)}, u32[]{:S(2)}, u32[]{:S(2)}) collective-permute-start(bf16[3,5120]{1,0:T(4,128)(2,1)S(1)} %pad_maximum_fusion.2), channel_id=1, source_target_pairs={{124,108},{125,109},{126,110},{127,111}} | collective-permute-start | bytes 92168 | tf_op jit(solution)/shard_map/ppermute | solution.py:503
  13.5 9.7 %collective-permute-start.8 = (bf16[3,5120]{1,0:T(4,128)(2,1)S(1)}, bf16[3,5120]{1,0:T(4,128)(2,1)S(1)}, u32[]{:S(2)}, u32[]{:S(2)}) collective-permute-start(bf16[3,5120]{1,0:T(4,128)(2,1)S(1)} %broadcast_select_fusion), channel_id=1, source_target_pairs={{108,96},{124,112},{109,97},{125,113},{110,98},{126,114},{111,99},... | collective-permute-start | bytes 92168 | tf_op jit(solution)/shard_map/ppermute | solution.py:507
  14.2 9.0 %collective-permute-start.9 = (bf16[3,5120]{1,0:T(4,128)(2,1)S(1)}, bf16[3,5120]{1,0:T(4,128)(2,1)S(1)}, u32[]{:S(2)}, u32[]{:S(2)}) collective-permute-start(bf16[3,5120]{1,0:T(4,128)(2,1)S(1)} %broadcast_select_fusion), channel_id=1, source_target_pairs={{108,100},{124,116},{109,101},{125,117},{110,102},{126,118},{111,1... | collective-permute-start | bytes 92168 | tf_op jit(solution)/shard_map/ppermute | solution.py:507
  14.9 8.3 %collective-permute-start.10 = (bf16[3,5120]{1,0:T(4,128)(2,1)S(1)}, bf16[3,5120]{1,0:T(4,128)(2,1)S(1)}, u32[]{:S(2)}, u32[]{:S(2)}) collective-permute-start(bf16[3,5120]{1,0:T(4,128)(2,1)S(1)} %broadcast_select_fusion), channel_id=1, source_target_pairs={{108,104},{124,120},{109,105},{125,121},{110,106},{126,122},{111,1... | collective-permute-start | bytes 92168 | tf_op jit(solution)/shard_map/ppermute | solution.py:507
  19.6 42.5 %copy-start.26 = (bf16[272,1024]{1,0:T(8,128)(2,1)}, bf16[272,1024]{1,0:T(8,128)(2,1)S(1)}, u32[]{:S(2)}) copy-start(bf16[272,1024]{1,0:T(8,128)(2,1)S(1)} %get-tuple-element.32.refs_0_) | copy-start | bytes 1671172
  23.2 7.6 %collective-permute-start.11 = (bf16[3,5120]{1,0:T(4,128)(2,1)S(1)}, bf16[3,5120]{1,0:T(4,128)(2,1)S(1)}, u32[]{:S(2)}, u32[]{:S(2)}) collective-permute-start(bf16[3,5120]{1,0:T(4,128)(2,1)S(1)} %select_select_fusion.1), channel_id=1, source_target_pairs={{96,0},{100,4},{104,8},{108,12},{112,16},{116,20},{120,24},{124,28... | collective-permute-start | bytes 92168 | tf_op jit(solution)/shard_map/ppermute | solution.py:513
  24.5 6.7 %collective-permute-start.12 = (bf16[3,5120]{1,0:T(4,128)(2,1)S(1)}, bf16[3,5120]{1,0:T(4,128)(2,1)S(1)}, u32[]{:S(2)}, u32[]{:S(2)}) collective-permute-start(bf16[3,5120]{1,0:T(4,128)(2,1)S(1)} %select_select_fusion.1), channel_id=1, source_target_pairs={{96,32},{100,36},{104,40},{108,44},{112,48},{116,52},{120,56},{124... | collective-permute-start | bytes 92168 | tf_op jit(solution)/shard_map/ppermute | solution.py:513
  25.2 6.0 %collective-permute-start.13 = (bf16[3,5120]{1,0:T(4,128)(2,1)S(1)}, bf16[3,5120]{1,0:T(4,128)(2,1)S(1)}, u32[]{:S(2)}, u32[]{:S(2)}) collective-permute-start(bf16[3,5120]{1,0:T(4,128)(2,1)S(1)} %select_select_fusion.1), channel_id=1, source_target_pairs={{96,64},{100,68},{104,72},{108,76},{112,80},{116,84},{120,88},{124... | collective-permute-start | bytes 92168 | tf_op jit(solution)/shard_map/ppermute | solution.py:513
  27.7 34.3 %collective-permute-start.1 = (bf16[272,1024]{1,0:T(8,128)(2,1)S(1)}, bf16[272,1024]{1,0:T(8,128)(2,1)S(1)}, u32[]{:S(2)}, u32[]{:S(2)}) collective-permute-start(bf16[272,1024]{1,0:T(8,128)(2,1)S(1)} %get-tuple-element.33), channel_id=1, source_target_pairs={{0,12},{4,0},{8,4},{12,8},{16,28},{20,16},{24,20},{28,24},{32,44},... | collective-permute-start | bytes 1671176 | tf_op jit(solution)/shard_map/ppermute | solution.py:33
  30.5 31.5 %collective-permute-start.2 = (bf16[272,1024]{1,0:T(8,128)(2,1)S(1)}, bf16[272,1024]{1,0:T(8,128)(2,1)S(1)}, u32[]{:S(2)}, u32[]{:S(2)}) collective-permute-start(bf16[272,1024]{1,0:T(8,128)(2,1)S(1)} %get-tuple-element.34), channel_id=1, source_target_pairs={{0,8},{4,12},{8,0},{12,4},{16,24},{20,28},{24,16},{28,20},{32,40},... | collective-permute-start | bytes 1671176 | tf_op jit(solution)/shard_map/ppermute | solution.py:33
  30.9 31.2 %collective-permute-start.3 = (bf16[272,1024]{1,0:T(8,128)(2,1)S(1)}, bf16[272,1024]{1,0:T(8,128)(2,1)S(1)}, u32[]{:S(2)}, u32[]{:S(2)}) collective-permute-start(bf16[272,1024]{1,0:T(8,128)(2,1)S(1)} %get-tuple-element.35), channel_id=1, source_target_pairs={{0,4},{4,8},{8,12},{12,0},{16,20},{20,24},{24,28},{28,16},{32,36},... | collective-permute-start | bytes 1671176 | tf_op jit(solution)/shard_map/ppermute | solution.py:33
  34.0 22.2 %collective-permute-start.14 = (bf16[32,1408]{1,0:T(8,128)(2,1)S(1)}, bf16[32,1408]{1,0:T(8,128)(2,1)S(1)}, u32[]{:S(2)}, u32[]{:S(2)}) collective-permute-start(bf16[32,1408]{1,0:T(8,128)(2,1)S(1)} %get-tuple-element.53), channel_id=1, source_target_pairs={{0,12},{4,0},{8,4},{12,8},{16,28},{20,16},{24,20},{28,24},{32,44},... | collective-permute-start | bytes 270344 | tf_op jit(solution)/shard_map/ppermute | solution.py:33
  36.8 21.8 %collective-permute-start.15 = (bf16[32,1408]{1,0:T(8,128)(2,1)S(1)}, bf16[32,1408]{1,0:T(8,128)(2,1)S(1)}, u32[]{:S(2)}, u32[]{:S(2)}) collective-permute-start(bf16[32,1408]{1,0:T(8,128)(2,1)S(1)} %get-tuple-element.52), channel_id=1, source_target_pairs={{0,8},{4,12},{8,0},{12,4},{16,24},{20,28},{24,16},{28,20},{32,40},... | collective-permute-start | bytes 270344 | tf_op jit(solution)/shard_map/ppermute | solution.py:33
  56.2 5.8 %collective-permute-start.16 = (bf16[32,1408]{1,0:T(8,128)(2,1)S(1)}, bf16[32,1408]{1,0:T(8,128)(2,1)S(1)}, u32[]{:S(2)}, u32[]{:S(2)}) collective-permute-start(bf16[32,1408]{1,0:T(8,128)(2,1)S(1)} %get-tuple-element.51), channel_id=1, source_target_pairs={{0,4},{4,8},{8,12},{12,0},{16,20},{20,24},{24,28},{28,16},{32,36},... | collective-permute-start | bytes 270344 | tf_op jit(solution)/shard_map/ppermute | solution.py:33
  64.8 17.1 %all-to-all-start = ((bf16[8,272,128]{2,1,0:T(8,128)(2,1)}), bf16[8,272,128]{2,1,0:T(8,128)(2,1)S(1)}, u32[]{:S(2)}, u32[]{:S(2)}) async-start(bf16[8,272,128]{2,1,0:T(8,128)(2,1)} %shard_map.176), calls=%async_computation | async-start | bytes 1114112 | tf_op jit(solution)/shard_map/all_to_all | solution.py:606
  75.5 13.4 %collective-permute-start.17 = (bf16[128,1408]{1,0:T(8,128)(2,1)S(1)}, bf16[128,1408]{1,0:T(8,128)(2,1)}, u32[]{:S(2)}, u32[]{:S(2)}) collective-permute-start(bf16[128,1408]{1,0:T(8,128)(2,1)S(1)} %constant_dynamic-slice_fusion.4), channel_id=1, source_target_pairs={{0,16},{4,20},{8,24},{12,28},{16,0},{20,4},{24,8},{28,12},{32,48},... | collective-permute-start | bytes 1081352 | tf_op jit(solution)/shard_map/ppermute | solution.py:33
  79.8 15.6 %collective-permute-start.21 = (bf16[1024,256]{1,0:T(8,128)(2,1)}, bf16[1024,256]{1,0:T(8,128)(2,1)S(1)}, u32[]{:S(2)}, u32[]{:S(2)}) collective-permute-start(bf16[1024,256]{1,0:T(8,128)(2,1)} %get-tuple-element.45), channel_id=1, source_target_pairs={{0,12},{4,0},{8,4},{12,8},{16,28},{20,16},{24,20},{28,24},{32,44},... | collective-permute-start | bytes 1572872 | tf_op jit(solution)/shard_map/ppermute | solution.py:33
  83.5 49.6 %all-to-all-start.1 = ((bf16[8,512,128]{2,1,0:T(8,128)(2,1)}), bf16[8,512,128]{2,1,0:T(8,128)(2,1)S(1)}, u32[]{:S(2)}, u32[]{:S(2)}) async-start(bf16[8,512,128]{2,1,0:T(8,128)(2,1)} %shard_map.177), calls=%async_computation.1 | async-start | bytes 2097152 | tf_op jit(solution)/shard_map/all_to_all | solution.py:608
  90.0 27.1 %collective-permute-start.18 = (bf16[256,1408]{1,0:T(8,128)(2,1)S(1)}, bf16[256,1408]{1,0:T(8,128)(2,1)S(1)}, u32[]{:S(2)}, u32[]{:S(2)}) collective-permute-start(bf16[256,1408]{1,0:T(8,128)(2,1)S(1)} %pad_maximum_fusion.refs_0_), channel_id=1, source_target_pairs={{0,96},{4,100},{8,104},{12,108},{16,112},{20,116},{24,120},{28,124... | collective-permute-start | bytes 2162696 | tf_op jit(solution)/shard_map/ppermute | solution.py:33
  93.1 24.9 %collective-permute-start.19 = (bf16[256,1408]{1,0:T(8,128)(2,1)S(1)}, bf16[256,1408]{1,0:T(8,128)(2,1)S(1)}, u32[]{:S(2)}, u32[]{:S(2)}) collective-permute-start(bf16[256,1408]{1,0:T(8,128)(2,1)S(1)} %pad_maximum_fusion.refs_0_), channel_id=1, source_target_pairs={{0,64},{4,68},{8,72},{12,76},{16,80},{20,84},{24,88},{28,92},{32,9... | collective-permute-start | bytes 2162696 | tf_op jit(solution)/shard_map/ppermute | solution.py:33
  94.5 37.8 %collective-permute-start.20 = (bf16[256,1408]{1,0:T(8,128)(2,1)S(1)}, bf16[256,1408]{1,0:T(8,128)(2,1)S(1)}, u32[]{:S(2)}, u32[]{:S(2)}) collective-permute-start(bf16[256,1408]{1,0:T(8,128)(2,1)S(1)} %pad_maximum_fusion.refs_0_), channel_id=1, source_target_pairs={{0,32},{4,36},{8,40},{12,44},{16,48},{20,52},{24,56},{28,60},{32,6... | collective-permute-start | bytes 2162696 | tf_op jit(solution)/shard_map/ppermute | solution.py:33
  94.5 9.9 %collective-permute-start.22 = (bf16[1024,256]{1,0:T(8,128)(2,1)}, bf16[1024,256]{1,0:T(8,128)(2,1)S(1)}, u32[]{:S(2)}, u32[]{:S(2)}) collective-permute-start(bf16[1024,256]{1,0:T(8,128)(2,1)} %get-tuple-element.47), channel_id=1, source_target_pairs={{0,8},{4,12},{8,0},{12,4},{16,24},{20,28},{24,16},{28,20},{32,40},... | collective-permute-start | bytes 1572872 | tf_op jit(solution)/shard_map/ppermute | solution.py:33
  96.1 20.2 %collective-permute-start.23 = (bf16[1024,256]{1,0:T(8,128)(2,1)}, bf16[1024,256]{1,0:T(8,128)(2,1)S(1)}, u32[]{:S(2)}, u32[]{:S(2)}) collective-permute-start(bf16[1024,256]{1,0:T(8,128)(2,1)} %get-tuple-element.44), channel_id=1, source_target_pairs={{0,4},{4,8},{8,12},{12,0},{16,20},{20,24},{24,28},{28,16},{32,36},... | collective-permute-start | bytes 1572872 | tf_op jit(solution)/shard_map/ppermute | solution.py:33
  150.9 8.4 %collective-permute-start.24 = (bf16[4,2,256,256]{3,2,1,0:T(8,128)(2,1)S(1)}, bf16[4,2,256,256]{3,2,1,0:T(8,128)(2,1)S(1)}, u32[]{:S(2)}, u32[]{:S(2)}) collective-permute-start(bf16[4,2,256,256]{3,2,1,0:T(8,128)(2,1)S(1)} %get-tuple-element.41), channel_id=1, source_target_pairs={{0,1},{1,0},{2,3},{3,2},{4,5},{5,4},{6,7},{7,6},{8,9},{9,8},{10,11... | collective-permute-start | bytes 3145736 | tf_op jit(solution)/shard_map/ppermute | solution.py:630
  160.3 10.9 %collective-permute-start.27 = (bf16[2,256,256]{2,1,0:T(8,128)(2,1)S(1)}, bf16[2,256,256]{2,1,0:T(8,128)(2,1)S(1)}, u32[]{:S(2)}, u32[]{:S(2)}) collective-permute-start(bf16[2,256,256]{2,1,0:T(8,128)(2,1)S(1)} %get-tuple-element.49), channel_id=1, source_target_pairs={{0,8},{4,12},{8,0},{12,4},{16,24},{20,28},{24,16},{28,20},{32,40},... | collective-permute-start | bytes 786440 | tf_op jit(solution)/shard_map/ppermute | solution.py:33
  165.5 37.2 %collective-permute-start.4 = (bf16[256,1024]{1,0:T(8,128)(2,1)S(1)}, bf16[256,1024]{1,0:T(8,128)(2,1)S(1)}, u32[]{:S(2)}, u32[]{:S(2)}) collective-permute-start(bf16[256,1024]{1,0:T(8,128)(2,1)S(1)} %get-tuple-element.37), channel_id=1, source_target_pairs={{0,12},{4,0},{8,4},{12,8},{16,28},{20,16},{24,20},{28,24},{32,44},... | collective-permute-start | bytes 1572872 | tf_op jit(solution)/shard_map/ppermute | solution.py:33
  166.9 35.8 %collective-permute-start.5 = (bf16[256,1024]{1,0:T(8,128)(2,1)S(1)}, bf16[256,1024]{1,0:T(8,128)(2,1)S(1)}, u32[]{:S(2)}, u32[]{:S(2)}) collective-permute-start(bf16[256,1024]{1,0:T(8,128)(2,1)S(1)} %get-tuple-element.38), channel_id=1, source_target_pairs={{0,8},{4,12},{8,0},{12,4},{16,24},{20,28},{24,16},{28,20},{32,40},... | collective-permute-start | bytes 1572872 | tf_op jit(solution)/shard_map/ppermute | solution.py:33
  168.5 34.2 %collective-permute-start.6 = (bf16[256,1024]{1,0:T(8,128)(2,1)S(1)}, bf16[256,1024]{1,0:T(8,128)(2,1)S(1)}, u32[]{:S(2)}, u32[]{:S(2)}) collective-permute-start(bf16[256,1024]{1,0:T(8,128)(2,1)S(1)} %get-tuple-element.39), channel_id=1, source_target_pairs={{0,4},{4,8},{8,12},{12,0},{16,20},{20,24},{24,28},{28,16},{32,36},... | collective-permute-start | bytes 1572872 | tf_op jit(solution)/shard_map/ppermute | solution.py:33
  168.5 28.5 %collective-permute-start.26 = (bf16[2,256,256]{2,1,0:T(8,128)(2,1)S(1)}, bf16[2,256,256]{2,1,0:T(8,128)(2,1)S(1)}, u32[]{:S(2)}, u32[]{:S(2)}) collective-permute-start(bf16[2,256,256]{2,1,0:T(8,128)(2,1)S(1)} %get-tuple-element.50), channel_id=1, source_target_pairs={{0,12},{4,0},{8,4},{12,8},{16,28},{20,16},{24,20},{28,24},{32,44},... | collective-permute-start | bytes 786440 | tf_op jit(solution)/shard_map/ppermute | solution.py:33
  171.2 27.9 %collective-permute-start.25 = (bf16[2,256,256]{2,1,0:T(8,128)(2,1)S(1)}, bf16[2,256,256]{2,1,0:T(8,128)(2,1)S(1)}, u32[]{:S(2)}, u32[]{:S(2)}) collective-permute-start(bf16[2,256,256]{2,1,0:T(8,128)(2,1)S(1)} %get-tuple-element.48), channel_id=1, source_target_pairs={{0,4},{4,8},{8,12},{12,0},{16,20},{20,24},{24,28},{28,16},{32,36},... | collective-permute-start | bytes 786440 | tf_op jit(solution)/shard_map/ppermute | solution.py:33
  199.3 7.3 %collective-permute-start.28 = (bf16[256,256]{1,0:T(8,128)(2,1)S(1)}, bf16[256,256]{1,0:T(8,128)(2,1)S(1)}, u32[]{:S(2)}, u32[]{:S(2)}) collective-permute-start(bf16[256,256]{1,0:T(8,128)(2,1)S(1)} %fusion.5), channel_id=1, source_target_pairs={{0,2},{1,3},{2,0},{3,1},{4,6},{5,7},{6,4},{7,5},{8,10},{9,11},{10,... | collective-permute-start | bytes 393224 | tf_op jit(solution)/shard_map/ppermute | solution.py:637
  (46 other events, 169.0 us)

commit v2 on v1

v2 whole, which is shorter than its diff:
```python
import functools

import jax
import jax.numpy as jnp
from jax import lax
from jax.experimental import pallas as pl
from jax.experimental.pallas import tpu as pltpu
from jax.sharding import PartitionSpec as P

P_SIZE = 64
N = 256
CONV = 4
SPAN = 256
X, Z, Y = 4, 2, 4
F32 = jnp.float32
BF16 = jnp.bfloat16
VMEM_BYTES = 48 * 2**20


def place(x, z, y):
    return (x % X * Z + z % Z) * Y + y % Y


def shifted(value, dx=0, dz=0, dy=0):
    pairs = [
        (place(x, z, y), place(x + dx, z + dz, y + dy))
        for x in range(X)
        for z in range(Z)
        for y in range(Y)
    ]
    return lax.ppermute(value, "ctx", pairs)


def whole(shape):
    return pl.BlockSpec(shape, lambda i, s: (0,) * len(shape))


def call(kernel, ids, ins, outs, scratch=(), after=(), into=None, turns=1):
    def split(entry):
        return entry if isinstance(entry, tuple) else (entry, None, None)

    def spec(entry):
        value, block, at = split(entry)
        if block is None:
            return whole(value.shape)
        return pl.BlockSpec(block, lambda i, s: at(s, i))

    extra = list(after) + ([] if into is None else [into])
    count = len(ins)

    def body(*refs):
        kernel(*refs[: 1 + count], *refs[1 + count + len(extra) :])

    aliases = {} if into is None else {count + len(extra): 0}
    return pl.pallas_call(
        body,
        grid_spec=pltpu.PrefetchScalarGridSpec(
            num_scalar_prefetch=1,
            grid=(turns,),
            in_specs=[spec(entry) for entry in ins]
            + [pl.BlockSpec(memory_space=pl.ANY)] * len(extra),
            out_specs=[spec(entry) for entry in outs],
            scratch_shapes=list(scratch),
        ),
        out_shape=[split(entry)[0] for entry in outs],
        input_output_aliases=aliases,
        compiler_params=pltpu.CompilerParams(vmem_limit_bytes=VMEM_BYTES),
        cost_estimate=pl.CostEstimate(
            flops=10**6, bytes_accessed=10**4, transcendentals=0
        ),
    )(ids, *[split(entry)[0] for entry in ins], *extra)


def sds(shape, dtype):
    return jax.ShapeDtypeStruct(shape, dtype)


def silu(value):
    return value * (0.5 + 0.5 * jnp.tanh(0.5 * value))


def softplus(value):
    return jnp.maximum(value, 0.0) + jnp.log1p(jnp.exp(-jnp.abs(value)))


def halves(value):
    high = value.astype(BF16)
    return high, (value - high.astype(F32)).astype(BF16)


def paired(value):
    high, low = halves(value)
    return jnp.concatenate([high.astype(F32), low.astype(F32)], axis=1).astype(BF16)


def head_spread(quarter, heads, width):
    row = lax.broadcasted_iota(jnp.int32, (2 * heads, width), 0)
    col = lax.broadcasted_iota(jnp.int32, (2 * heads, width), 1)
    first = quarter * (width // P_SIZE)
    match = lax.rem(row, heads) == first + lax.div(col, P_SIZE)
    return jnp.where(match, 1.0, 0.0).astype(BF16)


def dot(a, b):
    return jnp.dot(a, b, preferred_element_type=F32)


def dot_nt(a, b):
    return lax.dot_general(a, b, (((1,), (1,)), ((), ())), preferred_element_type=F32)


def wrapped(ids, index):
    return lax.rem(ids[2] + index, Y)


def tails_kernel(ids, raw, ports, out):
    rim_rows, channels = out.shape
    width_dev = raw.shape[1]
    first = raw.shape[0] - rim_rows
    half = ports.shape[2]
    out[:, 0:width_dev] = raw[...].astype(F32)[first:].astype(BF16)
    both = ports[...].astype(F32)
    for part in range(2):
        at = width_dev + part * half
        out[:, at : at + half] = both[first:, part, :].astype(BF16)


def span_kernel(
    ids, raw, ports, rim, value_taps, port_taps, steps_t, log_row, skip_row,
    read_out, write_t_out, run_out, row_out, grow_out, mixed_out, *refs,
):
    payloads = refs[0:Y]
    done, scr, wide, scaled = refs[Y : Y + 4]
    done[...] = jnp.zeros(done.shape, F32)
    width_dev = raw.shape[1]
    half = ports.shape[1] // 2
    heads = log_row.shape[1]
    width = width_dev // Y
    tap = port_taps[...].astype(F32)
    scr[5:8] = rim[:, width_dev:].astype(F32)
    scr[8 : 8 + SPAN] = ports[...].astype(F32)
    for part in range(2):
        lanes = slice(part * half, (part + 1) * half)
        line = tap[:, part, :]
        mixture = line[0:1] * scr[5 : 5 + SPAN, lanes]
        for position in range(1, CONV):
            mixture = mixture + line[position : position + 1] * scr[
                5 + position : 5 + position + SPAN, lanes
            ]
        mixed = silu(mixture)
        if part == 0:
            write_t_out[...] = mixed.astype(BF16).astype(F32).T.astype(BF16)
        else:
            read_out[...] = mixed.astype(BF16)
    rows = lax.broadcasted_iota(jnp.int32, (SPAN, SPAN), 0)
    cols = lax.broadcasted_iota(jnp.int32, (SPAN, SPAN), 1)
    lower = jnp.where(rows >= cols, 1.0, 0.0)
    size_t = softplus(steps_t[...])
    size = size_t.T
    run = jnp.dot(
        lower, size * -jnp.exp(log_row[...]), precision=lax.Precision.HIGHEST,
        preferred_element_type=F32,
    )
    quarter = heads // Y
    for index in range(Y):
        run_out[index] = run[:, index * quarter : (index + 1) * quarter]
    row_out[...] = run.T - jnp.log(size_t)
    ending = run[SPAN - 1 : SPAN]
    factor = jnp.concatenate(
        [
            paired(size * jnp.exp(ending - run)),
            paired(jnp.broadcast_to(jnp.exp(ending), (16, heads))),
        ],
        axis=0,
    )
    grow_out[0:SPAN] = paired(jnp.exp(run))
    grow_out[SPAN : SPAN + 16] = paired(jnp.broadcast_to(skip_row[...], (16, heads)))
    per = Y * N // half
    step = 32
    for index in (1, 3, 2, 0):
        spot = wrapped(ids, index)
        lanes = pl.ds(pl.multiple_of(spot * width, width), width)
        group = lax.div(spot, per)
        write_t = write_t_out[pl.ds(pl.multiple_of(group * N, N), N), :]
        tap = value_taps[:, lanes].astype(F32)
        scr[5:8] = rim[:, lanes].astype(F32)
        scr[8 : 8 + SPAN] = raw[:, lanes].astype(F32)
        wide[...] = dot(factor, head_spread(spot, heads, width))
        for start in range(0, SPAN, step):
            mixture = tap[0:1] * scr[start + 5 : start + 5 + step]
            for position in range(1, CONV):
                at = start + 5 + position
                mixture = mixture + tap[position : position + 1] * scr[at : at + step]
            mixed = silu(mixture).astype(BF16)
            mixed_out[index, start : start + step] = mixed
            scaled[start : start + step] = (
                mixed.astype(F32) * wide[start : start + step]
            ).astype(BF16)
        for start in range(0, width, 256):
            payloads[index][0:N, start : start + 256] = dot(
                write_t, scaled[:, start : start + 256]
            ).astype(BF16)
        decay = wide[SPAN : SPAN + 16]
        high = decay.astype(BF16).astype(F32)
        at = lax.broadcasted_iota(jnp.int32, decay.shape, 0)
        tail = jnp.where(at == 0, high, jnp.where(at == 1, decay - high, 0.0))
        payloads[index][N : N + 16] = tail.astype(BF16)


def scan_kernel(indices, ids, reads, writes_t, runs, row_lines, grow, mixes, *refs):
    states = refs[0 : len(indices)]
    out, scores, wide = refs[len(indices) :]
    for turn, index in enumerate(indices):

        @pl.when(pl.program_id(0) == turn)
        def _():
            scan_quarter(
                index, ids, reads, writes_t, runs, row_lines, mixes, grow, states[turn], out,
                scores, wide,
            )


def scan_quarter(index, ids, reads, writes_t, runs, row_lines, mixes, grow, state, out, scores, wide):
    mixed = mixes.at[index]
    width = mixed.shape[1]
    spot = wrapped(ids, index)
    group = pl.ds(pl.multiple_of(lax.div(spot * reads.shape[1], Y * N) * N, N), N)
    read = reads[:, group]
    heads = width // P_SIZE
    run = runs[pl.ds(spot, 1)]
    row = row_lines[pl.ds(pl.multiple_of(spot * heads, heads), heads), :]
    scores[...] = dot(read, writes_t[group, :])
    wide[...] = dot(grow[...], head_spread(spot, grow.shape[1] // 2, width))
    for start in range(0, width, 256):
        lanes = slice(start, start + 256)
        wide[0:SPAN, lanes] = wide[0:SPAN, lanes] * dot(read, state[:, lanes])
    half = SPAN // 2
    rows = lax.broadcasted_iota(jnp.int32, (half, half), 0)
    cols = lax.broadcasted_iota(jnp.int32, (half, half), 1)
    causal = rows >= cols
    left = lax.broadcasted_iota(jnp.int32, (half, 2 * P_SIZE), 1) < P_SIZE
    for pair in range(width // (2 * P_SIZE)):
        lanes = slice(pair * 2 * P_SIZE, (pair + 1) * 2 * P_SIZE)
        upper, lower = mixed[0:half, lanes], mixed[half:SPAN, lanes]
        tops, bottoms = [], []
        for member in range(2):
            head = 2 * pair + member
            col = run[0, :, head : head + 1]
            line = row[head : head + 1, :]
            w00 = jnp.where(
                causal, scores[0:half, 0:half] * jnp.exp(col[0:half] - line[:, 0:half]), 0.0
            ).astype(BF16)
            w10 = (scores[half:SPAN, 0:half] * jnp.exp(col[half:SPAN] - line[:, 0:half])).astype(BF16)
            w11 = jnp.where(
                causal,
                scores[half:SPAN, half:SPAN] * jnp.exp(col[half:SPAN] - line[:, half:SPAN]),
                0.0,
            ).astype(BF16)
            tops.append(dot(w00, upper))
            bottoms.append(dot(w10, upper) + dot(w11, lower))
        gain = wide[SPAN : SPAN + 1, lanes]
        out[0:half, lanes] = (
            jnp.where(left, tops[0], tops[1]) + wide[0:half, lanes] + gain * upper.astype(F32)
        ).astype(BF16)
        out[half:SPAN, lanes] = (
            jnp.where(left, bottoms[0], bottoms[1]) + wide[half:SPAN, lanes]
            + gain * lower.astype(F32)
        ).astype(BF16)


def decay_row(payload):
    tail = payload[N : N + 16].astype(F32)
    return tail[0:1] + tail[1:2]


def row_total_kernel(ids, *refs):
    states, out, done = refs[0:Y], refs[Y], refs[Y + 1]
    done[...] = jnp.zeros(done.shape, F32)
    spots = [lax.rem(ids[2] + index, Y) for index in range(Y)]
    decays = [decay_row(state) for state in states]
    width = states[0].shape[1]
    weights = []
    for mine in range(Y):
        weight = jnp.ones((1, width), F32)
        for other in range(Y):
            if other != mine:
                weight = weight * jnp.where(spots[other] > spots[mine], decays[other], 1.0)
        weights.append(weight)
    whole = decays[0] * decays[1] * decays[2] * decays[3]
    at = lax.broadcasted_iota(jnp.int32, (16, width), 0)
    high = whole.astype(BF16).astype(F32)
    tail = jnp.where(at == 0, high, jnp.where(at == 1, whole - high, 0.0)).astype(BF16)
    lanes_each = out.shape[2]
    for owner in range(out.shape[0]):
        lanes = slice(owner * lanes_each, (owner + 1) * lanes_each)
        total = weights[0][:, lanes] * states[0][0:N, lanes].astype(F32)
        for index in range(1, Y):
            total = total + weights[index][:, lanes] * states[index][0:N, lanes].astype(F32)
        out[owner, 0:N] = total.astype(BF16)
        out[owner, N : N + 16] = tail[:, lanes]


def chain_kernel(ids, totals, out):
    carry = jnp.zeros((N, totals.shape[2]), F32)
    for turn in range(totals.shape[0]):
        out[turn, 0:N] = carry.astype(BF16)
        tail = totals[turn, N : N + 16].astype(F32)
        carry = (tail[0:1] + tail[1:2]) * carry + totals[turn, 0:N].astype(F32)
    final = carry.astype(BF16)
    for turn in range(totals.shape[0]):
        out[turn, N : 2 * N] = final


def prefix_kernel(ids, back, *refs):
    states, outs = refs[0:Y], refs[Y : 2 * Y]
    spots = [lax.rem(ids[2] + index, Y) for index in range(Y)]
    decays = [decay_row(state) for state in states]
    lanes_each = back.shape[2]

    def between(low, high):
        weight = jnp.ones(decays[0].shape, F32)
        for other in range(Y):
            inside = spots[other] < high
            if low is not None:
                inside = jnp.logical_and(inside, spots[other] > low)
            weight = weight * jnp.where(inside, decays[other], 1.0)
        return weight

    for target in range(Y):
        base = between(None, spots[target])
        weights = [
            jnp.where(spots[mine] < spots[target], between(spots[mine], spots[target]), 0.0)
            for mine in range(Y)
        ]
        for owner in range(back.shape[0]):
            lanes = slice(owner * lanes_each, (owner + 1) * lanes_each)
            total = base[:, lanes] * back[owner, 0:N].astype(F32)
            for mine in range(Y):
                if mine != target:
                    total = total + weights[mine][:, lanes] * states[mine][0:N, lanes].astype(F32)
            outs[target][:, lanes] = total.astype(BF16)


def decode_kernel(
    ids, home, home_1, home_2, home_3, old_values, old_ports, new_values, new_ports,
    value_taps, port_taps, steps, log_row, skip, cache, out,
):
    count, rows_dev, width_dev = new_values.shape
    heads = steps.shape[1]
    group_dev = new_ports.shape[3] // N
    rim_rows = CONV - 1
    piece = out.shape[2] - N - 2 * heads
    at = lax.broadcasted_iota(jnp.int32, (count * rows_dev, 1), 0)
    slot = jnp.zeros(at.shape, jnp.int32)
    for spot in range(rows_dev):
        slot = jnp.where(lax.rem(at, rows_dev) == spot, ids[6 + spot], slot)
    chosen = slot == ids[5]
    second = slot == 1
    chosen_rows, second_rows = chosen[0:rows_dev], second[0:rows_dev]
    tails = home[...].astype(F32)
    for back, other in ((1, home_1), (2, home_2), (3, home_3)):
        tails = jnp.where(ids[0] == X - 1 - back, other[...].astype(F32), tails)

    def mix(tap, lines):
        results = []
        for index in range(count):
            mixture = tap[0:1] * lines[index]
            for position in range(1, CONV):
                mixture = mixture + tap[position : position + 1] * lines[index + position]
            results.append(silu(mixture).astype(BF16).astype(F32))
        return results

    def pick(first, other, prompt):
        return jnp.where(chosen_rows, prompt, jnp.where(second_rows, other, first))

    def value_mixes(lanes):
        lines = []
        for position in range(rim_rows):
            old = old_values[position, :, lanes].astype(F32)
            lines.append(pick(old[0:1], old[1:2], tails[position : position + 1, lanes]))
        lines += [new_values[index, :, lanes].astype(F32) for index in range(count)]
        return mix(value_taps[:, lanes].astype(F32), lines)

    def port_mixes(part):
        lines = []
        width = group_dev * N
        lanes = slice(width_dev + part * width, width_dev + (part + 1) * width)
        for position in range(rim_rows):
            old = [old_ports[member, position].astype(F32)[part : part + 1] for member in range(2)]
            lines.append(pick(old[0], old[1], tails[position : position + 1, lanes]))
        lines += [new_ports[index].astype(F32)[:, part, :] for index in range(count)]
        return mix(port_taps[...].astype(F32)[:, part, :], lines)

    writes, read_rows = port_mixes(0), port_mixes(1)
    size = softplus(steps[...])
    log_decay = size * -jnp.exp(log_row[...])
    sizes = [size[index * rows_dev : (index + 1) * rows_dev] for index in range(count)]
    logs = [log_decay[index * rows_dev : (index + 1) * rows_dev] for index in range(count)]
    lane = lax.broadcasted_iota(jnp.int32, (rows_dev, heads), 1)
    per_group = heads // group_dev
    stack, spots = [], {}
    total = None
    starts = []
    for index in range(count):
        total = logs[index] if total is None else total + logs[index]
        starts.append(jnp.exp(total))
    start_all = jnp.concatenate(starts, axis=0)
    kept = jnp.where(chosen, 0.0, start_all)
    given = jnp.where(chosen, start_all, 0.0)
    for index in range(count):
        gap = None
        for earlier in range(index, -1, -1):
            product = read_rows[index] * writes[earlier]
            meets = jnp.zeros((rows_dev, heads), F32)
            for group in range(group_dev):
                met = jnp.sum(product[:, group * N : (group + 1) * N], axis=1, keepdims=True)
                meets = jnp.where(lax.div(lane, per_group) == group, met, meets)
            weight = meets * sizes[earlier]
            if earlier == index:
                weight = weight + skip[...]
            else:
                gap = logs[earlier + 1] if gap is None else gap + logs[earlier + 1]
                weight = weight * jnp.exp(gap)
            spots[index, earlier] = count * rows_dev + len(stack) * rows_dev
            stack.append(weight)
    coefficients = paired(jnp.concatenate([kept] + stack, axis=0))
    shared = paired(given)
    reads = jnp.concatenate(read_rows, axis=0).astype(BF16)
    quarters = width_dev // piece
    per = quarters // group_dev
    for quarter in range(quarters):
        lanes = slice(quarter * piece, (quarter + 1) * piece)
        group = quarter // per
        read = reads[:, group * N : (group + 1) * N]
        wide = dot(coefficients, head_spread(quarter, heads, piece))
        values = value_mixes(lanes)
        met = jnp.where(
            second, dot_nt(read, cache[1, lanes, :]), dot_nt(read, cache[0, lanes, :])
        )
        results = []
        for index in range(count):
            at = index * rows_dev
            line = wide[at : at + rows_dev] * met[at : at + rows_dev]
            for earlier in range(index + 1):
                spot = spots[index, earlier]
                line = line + wide[spot : spot + rows_dev] * values[earlier]
            results.append(line)
        out[quarter, :, 0:piece] = jnp.concatenate(results, axis=0).astype(BF16)
        out[quarter, :, piece : piece + N] = read
        out[quarter, :, piece + N : piece + N + 2 * heads] = shared


def copy_kernel(ids, source, out):
    out[...] = source[...]


def order_kernel(ids, *refs):
    out, done = refs[Y : Y + 2]
    done[...] = jnp.zeros(done.shape, F32)
    for index in range(Y):
        out[wrapped(ids, index)] = refs[index][...]


def project_kernel(ids, back, *refs):
    pieces, blocks = refs[0 : Z * X], refs[Z * X : Z * X + Y]
    keep, send, final, joined = refs[Z * X + Y : Z * X + Y + 4]
    width = joined.shape[1]
    each = back.shape[2]
    rows = pieces[0].shape[0]
    for owner in range(back.shape[0]):
        final[:, owner * each : (owner + 1) * each] = back[owner, N : 2 * N]
    pairs = pieces[0].shape[1] - width - N
    spread = head_spread(ids[2], pairs // 2, width)
    for index in range(X):
        for member in range(Z):
            piece = pieces[member * X + index]
            at = (index * Z + member) * rows
            for start in range(0, width, 256):
                lanes = slice(start, start + 256)
                extra = dot(piece[:, width + N :], spread[:, lanes]) * dot(
                    piece[:, width : width + N], final[:, lanes]
                )
                joined[at : at + rows, lanes] = (piece[:, lanes].astype(F32) + extra).astype(BF16)
    for block in range(Y):
        part = dot(joined[...], blocks[block][...]).astype(BF16)
        for index in range(X):
            spot = lax.rem(ids[0] + index, X)
            same = lax.rem(spot, 2) == ids[3]
            row = lax.div(spot, 2)
            lines = part[index * Z * rows : (index + 1) * Z * rows]

            @pl.when(same)
            def _():
                keep[block, row] = lines

            @pl.when(jnp.logical_not(same))
            def _():
                send[block, row] = lines


def pair_sum_kernel(ids, keep, other, own, *outs):
    own[...] = keep[0].astype(F32) + other[0].astype(F32)
    for index in range(1, Y):
        outs[index - 1][...] = (keep[index].astype(F32) + other[index].astype(F32)).astype(BF16)


def ring_sum_kernel(ids, own, first, second, third, mine, theirs):
    high = ids[4]

    def total(at):
        return (
            own[at] + first[at].astype(F32) + second[at].astype(F32) + third[at].astype(F32)
        )

    mine[...] = total(high)
    theirs[...] = total(1 - high).astype(BF16)


def finish_kernel(ids, mine, other, out):
    total = mine[...] + other[...].astype(F32)
    count = out.shape[0]
    rows = out.shape[1] // (Z * Y)
    for member in range(Z):
        spot = lax.rem(ids[1] + member, Z)
        for index in range(count):
            lines = []
            for turn in range(Y):
                at = ((member * Y + turn) * count + index) * rows
                lines.append(total[at : at + rows])
            out[index, pl.ds(pl.multiple_of(spot * Y * rows, Y * rows), Y * rows), :] = (
                jnp.concatenate(lines, axis=0).astype(BF16)
            )


def shards(
    raw_values,
    state_ports,
    step_raw,
    decay_log,
    skip_gain,
    conv_values,
    conv_ports,
    prompt_slot,
    row_slot,
    cache_states,
    cache_values,
    cache_ports,
    new_values,
    new_ports,
    new_steps,
    out_weight,
):
    length, width_dev = raw_values.shape
    heads = decay_log.shape[0]
    ports_dev = 2 * state_ports.shape[2]
    rim_rows = CONV - 1
    width = width_dev // Y
    count, rows_dev = new_steps.shape[0:2]
    per = Y * N // state_ports.shape[2]
    me = lax.axis_index("ctx").astype(jnp.int32)
    part = lax.axis_index("head").astype(jnp.int32)
    my_x, my_z, my_y = me // (Z * Y), me // Y % Z, me % Y
    my_core, my_high = part % 2, part // 2
    ids = jnp.concatenate(
        [jnp.stack([my_x, my_z, my_y, my_core, my_high]), prompt_slot, row_slot]
    )
    devices = X * Z * Y
    log_row = decay_log.reshape(1, heads)
    skip_row = skip_gain.reshape(1, heads)

    def quarter_block(block, index, dim):
        def at(s, i):
            spot = [0] * len(block)
            spot[dim] = wrapped(s, index)
            return tuple(spot)

        return block, at

    edge = 16
    last_edge = length // edge - 1
    tails = call(
        tails_kernel,
        ids,
        [
            (raw_values, (edge, width_dev), lambda s, i: (last_edge, 0)),
            (state_ports, (edge,) + state_ports.shape[1:], lambda s, i: (last_edge, 0, 0)),
        ],
        [sds((rim_rows, width_dev + ports_dev), BF16)],
    )[0]
    rim = lax.ppermute(tails, "ctx", [(i, i + 1) for i in range(devices - 1)])
    last = devices - 1
    moved = tails
    for step in range(1, Y):
        at_y = lax.ppermute(tails, "ctx", [(last, last - step)])
        moved = jnp.where(my_y == Y - 1 - step, at_y, moved)
    home_y = moved
    at_z = lax.ppermute(
        home_y, "ctx", [(place(X - 1, Z - 1, y), place(X - 1, 0, y)) for y in range(Y)]
    )
    moved = jnp.where(my_z == Z - 1, home_y, at_z)
    homes = [moved]
    for step in range(1, X):
        homes.append(
            lax.ppermute(
                moved,
                "ctx",
                [(place(X - 1, z, y), place(X - 1 - step, z, y)) for z in range(Z) for y in range(Y)],
            )
        )

    span = call(
        span_kernel,
        ids,
        [
            raw_values,
            state_ports.reshape(length, ports_dev),
            rim,
            conv_values,
            conv_ports,
            step_raw.T,
            log_row,
            skip_row,
        ],
        [
            sds((SPAN, ports_dev // 2), BF16),
            sds((ports_dev // 2, SPAN), BF16),
            sds((Y, SPAN, heads // Y), F32),
            sds((heads, SPAN), F32),
            sds((SPAN + 16, 2 * heads), BF16),
            sds((Y, SPAN, width), BF16),
        ]
        + [sds((N + 16, width), BF16)] * Y
        + [sds((8, 128), F32)],
        scratch=[
            pltpu.VMEM((SPAN + 8, width), F32),
            pltpu.VMEM((SPAN + 16, width), F32),
            pltpu.VMEM((SPAN, width), BF16),
        ],
    )
    shared, states, spanned = span[0:6], span[6 : 6 + Y], span[6 + Y]
    ring = [states[0], None, None, None]
    for index in (1, 3, 2):
        ring[Y - index] = shifted(states[index], dy=index)

    packed_width = width + N + 2 * heads
    slots = cache_states.shape[0]
    packed = call(
        decode_kernel,
        ids,
        [
            *homes,
            cache_values.transpose(1, 0, 2),
            cache_ports,
            new_values,
            new_ports,
            conv_values,
            conv_ports,
            new_steps.reshape(count * rows_dev, heads),
            log_row,
            skip_row,
            cache_states.reshape(slots, width_dev, N),
        ],
        [sds((Y, count * rows_dev, packed_width), BF16)],
        after=[spanned],
    )[0]
    quarters = [(my_y + index) % Y for index in range(Y)]
    by_y = [lax.dynamic_index_in_dim(packed, quarters[0], 0, False), None, None, None]
    for index in range(1, Y):
        by_y[Y - index] = shifted(
            lax.dynamic_index_in_dim(packed, quarters[index], 0, False), dy=index
        )
    ordered, turned = call(
        order_kernel,
        ids,
        by_y,
        [sds((Y, count * rows_dev, packed_width), BF16), sds((8, 128), F32)],
    )
    piece_rows = Z * Y * count * rows_dev
    pieces = []
    for held in (ordered, shifted(ordered, dz=1)):
        held = held.reshape(Y * count * rows_dev, packed_width)
        pieces += [held] + [shifted(held, dx=-index) for index in range(1, X)]

    owners = X * Z
    each = width // owners
    groups = [[place(x, z, y) for x in range(X) for z in range(Z)] for y in range(Y)]
    totals, summed = call(
        row_total_kernel,
        ids,
        ring,
        [sds((owners, N + 16, each), BF16), sds((8, 128), F32)],
        after=[turned],
    )
    totals = lax.all_to_all(totals, "ctx", 0, 0, tiled=True, axis_index_groups=groups)
    back = call(chain_kernel, ids, [totals], [sds((owners, 2 * N, each), BF16)])[0]
    back = lax.all_to_all(back, "ctx", 0, 0, tiled=True, axis_index_groups=groups)
    prefixes = call(
        prefix_kernel,
        ids,
        [back, *ring],
        [sds((N, width), BF16) for _ in range(Y)],
    )
    incoming = [prefixes[0], None, None, None]
    for index in (1, 3, 2):
        incoming[Y - index] = shifted(prefixes[index], dy=index)

    def weight_block(index, after=()):
        return call(
            copy_kernel,
            ids,
            [(out_weight, *quarter_block((width, out_weight.shape[1]), index, 0))],
            [sds((width, out_weight.shape[1]), BF16)],
            after=after,
        )[0]

    blocks = [None] * Y
    for index in (1, 3, 2):
        blocks[Y - index] = shifted(weight_block(index, after=[summed]), dy=index)

    cols = out_weight.shape[1]
    keep, send = call(
        project_kernel,
        ids,
        [
            back,
            *pieces,
            (out_weight, *quarter_block((width, cols), 0, 0)),
            *blocks[1:],
        ],
        [sds((Y, X // 2, piece_rows, cols), BF16)] * 2,
        scratch=[pltpu.VMEM((N, width), BF16), pltpu.VMEM((X * piece_rows, width), BF16)],
        after=[incoming[1][0:16, 0:128], incoming[3][0:16, 0:128]],
    )
    other = lax.ppermute(send, "head", [(i, i ^ 1) for i in range(4)])
    half = (X // 2, piece_rows, cols)
    own, *outward = call(
        pair_sum_kernel,
        ids,
        [keep, other],
        [sds(half, F32)] + [sds(half, BF16)] * (Y - 1),
    )
    inward = [shifted(outward[index - 1], dy=index) for index in (1, 3, 2)]
    mine, theirs = call(
        ring_sum_kernel, ids, [own, *inward], [sds(half[1:], F32), sds(half[1:], BF16)]
    )
    other = lax.ppermute(theirs, "head", [(i, i ^ 2) for i in range(4)])
    decoded_out = call(
        finish_kernel, ids, [mine, other], [sds((count, Z * Y * rows_dev, cols), BF16)]
    )[0]

    def turn_block(indices):
        def at(s, i):
            index = indices[0]
            for turn in range(1, len(indices)):
                index = jnp.where(i == turn, indices[turn], index)
            return 0, wrapped(s, index)

        return at

    scan_out = None
    for indices in ((0, 1, 3), (2,)):
        scan_out = call(
            functools.partial(scan_kernel, indices),
            ids,
            [*shared, *[incoming[index] for index in indices]],
            [(sds((SPAN, width_dev), BF16), (SPAN, width), turn_block(indices))],
            scratch=[pltpu.VMEM((SPAN, SPAN), F32), pltpu.VMEM((SPAN + 16, width), F32)],
            into=scan_out,
            turns=len(indices),
        )[0]
    return scan_out, decoded_out


def solution(mesh):
    in_specs = (
        P("ctx", "head"),
        P("ctx", None, "head"),
        P("ctx", "head"),
        P("head"),
        P("head"),
        P(None, "head"),
        P(None, None, "head"),
        P("ctx"),
        P("ctx"),
        P("ctx", "head", None, None),
        P("ctx", None, "head"),
        P("ctx", None, None, "head"),
        P(None, "ctx", "head"),
        P(None, "ctx", None, "head"),
        P(None, "ctx", "head"),
        P("head", "ctx"),
    )
    out_specs = (P("ctx", "head"), P(None, "head", "ctx"))
    return jax.shard_map(shards, mesh=mesh, in_specs=in_specs, out_specs=out_specs, check_vma=False)
```

time: 209 us -> 195 us (0.933)
  waiting for transfers between devices: 85.1 us -> 66.4 us
  local copies, waits for them, and re-layouts: 28.2 us -> 13.5 us
  blocking collectives: 0 us -> 14.6 us
  Pallas kernels: 35.8 us -> 41.5 us
  starting transfers between devices: 51.7 us -> 56.8 us
  other arithmetic: 4.3 us -> 0.07 us
    ppermute x19 -> x22, waiting for transfers between devices: 84.5 us -> 52 us  [shifted(): return lax.ppermute(value, 'ctx', pairs)]
    all_to_all x0 -> x1, blocking collectives: none -> 14.6 us  [shards(): lax.all_to_all(totals, 'ctx', 0, 0, tiled=True, axis_index_groups=groups)]
    all_to_all x1 -> x0, starting transfers between devices: 9.7 us -> none  [shards(): lax.all_to_all(totals, 'ctx', 0, 0, tiled=True, axis_index_groups=groups)]
    ppermute x1, starting transfers between devices: 2.19 us -> 11.6 us  [shards(): other = lax.ppermute(send, 'head', [(i, i ^ 1) for i in range(4)])]
    unnamed x107 -> x65, local copies, waits for them, and re-layouts: 21.5 us -> 12.8 us
    ppermute x8, waiting for transfers between devices: 0.02 us -> 7.19 us  [the longest x3 7.18 us: shards(): lax.ppermute(moved, 'ctx', [(place(X - 1, z, y), place(X - 1 - step, z, y...]
    pallas_call x15 -> x16, Pallas kernels: 35.8 us -> 41.5 us  [call(): pl.pallas_call(body, grid_spec=pltpu.PrefetchScalarGridSpec(num_scalar_pr...]
    all_to_all x1, waiting for transfers between devices: 0.01 us -> 5.53 us  [shards(): lax.all_to_all(back, 'ctx', 0, 0, tiled=True, axis_index_groups=groups)]
  transfers between devices with their start and end apart: 31 -> 33, of which waited for: 10 -> 13; matrix products, arithmetic and copies ran while one was open for 5% -> 0% of each run, Pallas kernels for 11% -> 14%
where the time goes in v2:
time: 195 us
  waiting for transfers between devices  66.4 us (34%)
  starting transfers between devices  56.8 us (29%)
  Pallas kernels  41.5 us (21%)
  blocking collectives  14.6 us (7%)
  local copies, waits for them, and re-layouts  13.5 us (7%)
    ppermute x22, waiting for transfers between devices, shifted(): return lax.ppermute(value, 'ctx', pairs)  52 us
    pallas_call x16, Pallas kernels, call(): pl.pallas_call(body, grid_spec=pltpu.PrefetchScalarGridSpec(num_scalar_pr...  41.5 us
    ppermute x22, starting transfers between devices, shifted(): return lax.ppermute(value, 'ctx', pairs)  28.8 us
    all_to_all x1, blocking collectives, shards(): lax.all_to_all(totals, 'ctx', 0, 0, tiled=True, axis_index_groups=groups)  14.6 us
    unnamed x65, local copies, waits for them, and re-layouts  12.8 us
    ppermute x1, starting transfers between devices, shards(): other = lax.ppermute(send, 'head', [(i, i ^ 1) for i in range(4)])  11.6 us
    ppermute x3, waiting for transfers between devices, shards(): lax.ppermute(moved, 'ctx', [(place(X - 1, z, y), place(X - 1 - step, z, y...  7.18 us
    all_to_all x1, waiting for transfers between devices, shards(): lax.all_to_all(back, 'ctx', 0, 0, tiled=True, axis_index_groups=groups)  5.53 us
  transfers between devices with their start and end apart: 33, of which 13 were waited for; matrix products, arithmetic and copies ran while one was open for 0% of the time, Pallas kernels for 14%

profile of v2, /device:TPU:1, one launch (start us, length us, event | category | flops | bytes accessed | tf_op | source)
XLA Modules:
  0.0 194.7 jit_solution(13720971669727795900)
XLA Ops:
  7.4 4.0 %collective-permute-start = (bf16[3,5120]{1,0:T(4,128)(2,1)S(1)}, bf16[3,5120]{1,0:T(4,128)(2,1)S(1)}, u32[]{:S(2)}, u32[]{:S(2)}) collective-permute-start(bf16[3,5120]{1,0:T(4,128)(2,1)S(1)} %shard_map.167), channel_id=1, source_target_pairs={{0,4},{4,8},{8,12},{12,16},{16,20},{20,24},{24,28},{28,32},{32,36}... | collective-permute-start | bytes 92168 | tf_op jit(solution)/shard_map/ppermute | solution.py:590
  12.5 11.0 %shard_map.168 = (bf16[256,512]{1,0:T(8,128)(2,1)S(1)}, bf16[512,256]{1,0:T(8,128)(2,1)S(1)}, f32[4,256,16]{2,1,0:T(8,128)S(1)}, f32[64,256]{1,0:T(8,128)S(1)}, ...) custom-call(s32[14]{0:T(128)S(1)} %concatenate.3.refs_0_, ...), custom_call_target="tpu_custom_call" | custom-call | flops 1000000 | bytes 10000 | tf_op jit(solution)/shard_map/pallas_call | solution.py:55
  26.4 3.2 %collective-permute-start.1 = (bf16[272,1024]{1,0:T(8,128)(2,1)}, bf16[272,1024]{1,0:T(8,128)(2,1)S(1)}, u32[]{:S(2)}, u32[]{:S(2)}) collective-permute-start(bf16[272,1024]{1,0:T(8,128)(2,1)} %get-tuple-element.36), channel_id=1, source_target_pairs={{0,12},{4,0},{8,4},{12,8},{16,28},{20,16},{24,20},{28,24},{32,44},... | collective-permute-start | bytes 1671176 | tf_op jit(solution)/shard_map/ppermute | solution.py:31
  33.4 7.2 %collective-permute-done.10.refs_4_ = bf16[3,5120]{1,0:T(4,128)(2,1)S(1)} collective-permute-done((bf16[3,5120]{1,0:T(4,128)(2,1)S(1)}, bf16[3,5120]{1,0:T(4,128)(2,1)S(1)}, u32[]{:S(2)}, u32[]{:S(2)}) %collective-permute-start.10) | collective-permute-done | bytes 30752 | tf_op jit(solution)/shard_map/ppermute | solution.py:604
  40.6 2.2 %copy-done.5 = bf16[2,64,64,256]{3,2,1,0:T(8,128)(2,1)S(1)} copy-done((bf16[2,64,64,256]{3,2,1,0:T(8,128)(2,1)S(1)}, bf16[2,64,64,256]{3,2,1,0:T(8,128)(2,1)}, u32[]{:S(2)}) %copy-start.5) | copy-done | bytes 4194328
  42.8 2.4 %shard_map.169 = bf16[4,32,1408]{2,1,0:T(8,128)(2,1)S(1)} custom-call(s32[14]{0:T(128)S(1)} %concatenate.3.refs_0_, bf16[3,5120]{1,0:T(4,128)(2,1)S(1)} %broadcast_select_fusion.refs_1_, bf16[3,5120]{1,0:T(4,128)(2,1)S(1)} %collective-permute-done.8.refs_2_, bf16[3,5120]{1,0:T(4,128)(2,1)S(1)} %collective-permute-done.9.refs_3_, ...), custom_call_target="tpu_custom_call" | custom-call | flops 1000000 | bytes 10000 | tf_op jit(solution)/shard_map/pallas_call | solution.py:55
  45.2 2.5 %collective-permute-start.11 = (bf16[32,1408]{1,0:T(8,128)(2,1)S(1)}, bf16[32,1408]{1,0:T(8,128)(2,1)S(1)}, u32[]{:S(2)}, u32[]{:S(2)}) collective-permute-start(bf16[32,1408]{1,0:T(8,128)(2,1)S(1)} %get-tuple-element.58), channel_id=1, source_target_pairs={{0,12},{4,0},{8,4},{12,8},{16,28},{20,16},{24,20},{28,24},{32,44},... | collective-permute-start | bytes 270344 | tf_op jit(solution)/shard_map/ppermute | solution.py:31
  48.8 6.5 %collective-permute-done.11.refs_2_ = bf16[32,1408]{1,0:T(8,128)(2,1)S(1)} collective-permute-done((bf16[32,1408]{1,0:T(8,128)(2,1)S(1)}, bf16[32,1408]{1,0:T(8,128)(2,1)S(1)}, u32[]{:S(2)}, u32[]{:S(2)}) %collective-permute-start.11) | collective-permute-done | bytes 90144 | tf_op jit(solution)/shard_map/ppermute | solution.py:31
  55.3 3.3 %collective-permute-start.13 = (bf16[32,1408]{1,0:T(8,128)(2,1)S(1)}, bf16[32,1408]{1,0:T(8,128)(2,1)S(1)}, u32[]{:S(2)}, u32[]{:S(2)}) collective-permute-start(bf16[32,1408]{1,0:T(8,128)(2,1)S(1)} %get-tuple-element.56), channel_id=1, source_target_pairs={{0,4},{4,8},{8,12},{12,0},{16,20},{20,24},{24,28},{28,16},{32,36},... | collective-permute-start | bytes 270344 | tf_op jit(solution)/shard_map/ppermute | solution.py:31
  58.7 3.1 %collective-permute-done.13.refs_4_ = bf16[32,1408]{1,0:T(8,128)(2,1)S(1)} collective-permute-done((bf16[32,1408]{1,0:T(8,128)(2,1)S(1)}, bf16[32,1408]{1,0:T(8,128)(2,1)S(1)}, u32[]{:S(2)}, u32[]{:S(2)}) %collective-permute-start.13) | collective-permute-done | bytes 90144 | tf_op jit(solution)/shard_map/ppermute | solution.py:31
  64.2 14.6 %all_to_all.10.refs_1_ = bf16[8,272,128]{2,1,0:T(8,128)(2,1)S(1)} all-to-all(bf16[8,272,128]{2,1,0:T(8,128)(2,1)S(1)} %get-tuple-element.41), channel_id=1, replica_groups={{0,16,32,48,64,80,96,112},{4,20,36,52,68,84,100,116},{8,24,40,56,72,88,..., dimensions={0} | all-to-all | bytes 1114112 | tf_op jit(solution)/shard_map/all_to_all | solution.py:694
  78.8 1.7 shard_map.172
  80.5 3.6 %all-to-all-start.1 = ((bf16[8,512,128]{2,1,0:T(8,128)(2,1)}), bf16[8,512,128]{2,1,0:T(8,128)(2,1)S(1)}, u32[]{:S(2)}, u32[]{:S(2)}) async-start(bf16[8,512,128]{2,1,0:T(8,128)(2,1)} %shard_map.172), calls=%async_computation.1 | async-start | bytes 2097152 | tf_op jit(solution)/shard_map/all_to_all | solution.py:696
  84.1 2.6 %collective-permute-start.17 = (bf16[128,1408]{1,0:T(8,128)(2,1)}, bf16[128,1408]{1,0:T(8,128)(2,1)}, u32[]{:S(2)}, u32[]{:S(2)}) collective-permute-start(bf16[128,1408]{1,0:T(8,128)(2,1)} %bitcast.26), channel_id=1, source_target_pairs={{0,96},{4,100},{8,104},{12,108},{16,112},{20,116},{24,120},{28,124... | collective-permute-start | bytes 1081352 | tf_op jit(solution)/shard_map/ppermute | solution.py:31
  89.0 5.5 %all-to-all-done.1.refs_1_ = bf16[8,512,128]{2,1,0:T(8,128)(2,1)S(1)} async-done(((bf16[8,512,128]{2,1,0:T(8,128)(2,1)}), bf16[8,512,128]{2,1,0:T(8,128)(2,1)S(1)}, u32[]{:S(2)}, u32[]{:S(2)}) %all-to-all-start.1) | async-done | bytes 1048608 | tf_op jit(solution)/shard_map/all_to_all | solution.py:696
  98.8 2.3 %shard_map.173 = (bf16[256,1024]{1,0:T(8,128)(2,1)S(1)}, bf16[256,1024]{1,0:T(8,128)(2,1)S(1)}, bf16[256,1024]{1,0:T(8,128)(2,1)S(1)}, bf16[256,1024]{1,0:T(8,128)(2,1)S(1)}) custom-call(s32[14]{0:T(128)S(1)} %concatenate.3.refs_0_, bf16[8,512,128]{2,1,0:T(8,128)(2,1)S(1)} %all-to-all-done.1.refs_1_, bf16[272,1024]{1,0:T(8,128)(2,1)S(1)} %copy-done.7, ...), custom_call_target="tpu_custom_call" | custom-call | flops 1000000 | bytes 10000 | tf_op jit(solution)/shard_map/pallas_call | solution.py:55
  102.6 1.7 collective-permute-done.20
  104.3 2.5 %collective-permute-start.21 = (bf16[128,1408]{1,0:T(8,128)(2,1)}, bf16[128,1408]{1,0:T(8,128)(2,1)S(1)}, u32[]{:S(2)}, u32[]{:S(2)}) collective-permute-start(bf16[128,1408]{1,0:T(8,128)(2,1)} %bitcast.16.refs_6_), channel_id=1, source_target_pairs={{0,96},{4,100},{8,104},{12,108},{16,112},{20,116},{24,120},{28,124... | collective-permute-start | bytes 1081352 | tf_op jit(solution)/shard_map/ppermute | solution.py:31
  109.8 3.0 %collective-permute-done.19.refs_5_ = bf16[128,1408]{1,0:T(8,128)(2,1)} collective-permute-done((bf16[128,1408]{1,0:T(8,128)(2,1)}, bf16[128,1408]{1,0:T(8,128)(2,1)}, u32[]{:S(2)}, u32[]{:S(2)}) %collective-permute-start.19) | collective-permute-done | bytes 360480 | tf_op jit(solution)/shard_map/ppermute | solution.py:31
  113.6 2.1 %collective-permute-done.21.refs_7_ = bf16[128,1408]{1,0:T(8,128)(2,1)S(1)} collective-permute-done((bf16[128,1408]{1,0:T(8,128)(2,1)}, bf16[128,1408]{1,0:T(8,128)(2,1)S(1)}, u32[]{:S(2)}, u32[]{:S(2)}) %collective-permute-start.21) | collective-permute-done | bytes 360480 | tf_op jit(solution)/shard_map/ppermute | solution.py:31
  115.7 3.0 %collective-permute-start.22 = (bf16[128,1408]{1,0:T(8,128)(2,1)}, bf16[128,1408]{1,0:T(8,128)(2,1)S(1)}, u32[]{:S(2)}, u32[]{:S(2)}) collective-permute-start(bf16[128,1408]{1,0:T(8,128)(2,1)} %bitcast.16.refs_6_), channel_id=1, source_target_pairs={{0,64},{4,68},{8,72},{12,76},{16,80},{20,84},{24,88},{28,92},{32,9... | collective-permute-start | bytes 1081352 | tf_op jit(solution)/shard_map/ppermute | solution.py:31
  118.8 5.1 %collective-permute-done.22.refs_8_ = bf16[128,1408]{1,0:T(8,128)(2,1)S(1)} collective-permute-done((bf16[128,1408]{1,0:T(8,128)(2,1)}, bf16[128,1408]{1,0:T(8,128)(2,1)S(1)}, u32[]{:S(2)}, u32[]{:S(2)}) %collective-permute-start.22) | collective-permute-done | bytes 360480 | tf_op jit(solution)/shard_map/ppermute | solution.py:31
  123.9 4.1 %collective-permute-done.23.refs_9_ = bf16[128,1408]{1,0:T(8,128)(2,1)S(1)} collective-permute-done((bf16[128,1408]{1,0:T(8,128)(2,1)}, bf16[128,1408]{1,0:T(8,128)(2,1)S(1)}, u32[]{:S(2)}, u32[]{:S(2)}) %collective-permute-start.23) | collective-permute-done | bytes 360480 | tf_op jit(solution)/shard_map/ppermute | solution.py:31
  127.9 6.2 %collective-permute-done.26.refs_13_ = bf16[1024,256]{1,0:T(8,128)(2,1)S(1)} collective-permute-done((bf16[1024,256]{1,0:T(8,128)(2,1)S(1)}, bf16[1024,256]{1,0:T(8,128)(2,1)S(1)}, u32[]{:S(2)}, u32[]{:S(2)}) %collective-permute-start.26) | collective-permute-done | bytes 524320 | tf_op jit(solution)/shard_map/ppermute | solution.py:31
  134.2 9.7 %shard_map.179 = (bf16[4,2,256,256]{3,2,1,0:T(8,128)(2,1)S(1)}, bf16[4,2,256,256]{3,2,1,0:T(8,128)(2,1)}) custom-call(s32[14]{0:T(128)S(1)} %concatenate.3.refs_0_, bf16[8,512,128]{2,1,0:T(8,128)(2,1)} %copy-done.1, bf16[128,1408]{1,0:T(8,128)(2,1)S(1)} %bitcast.29, bf16[128,1408]{1,0:T(8,128)(2,1)} %collective-permute-done.17.refs_3_, ...), custom_call_target="tpu_custom_call" | custom-call | flops 1000000 | bytes 10000 | tf_op jit(solution)/shard_map/pallas_call | solution.py:55
  143.9 11.6 %collective-permute-start.27 = (bf16[4,2,256,256]{3,2,1,0:T(8,128)(2,1)}, bf16[4,2,256,256]{3,2,1,0:T(8,128)(2,1)S(1)}, u32[]{:S(2)}, u32[]{:S(2)}) collective-permute-start(bf16[4,2,256,256]{3,2,1,0:T(8,128)(2,1)} %get-tuple-element.49), channel_id=1, source_target_pairs={{0,1},{1,0},{2,3},{3,2},{4,5},{5,4},{6,7},{7,6},{8,9},{9,8},{10,11... | collective-permute-start | bytes 3145736 | tf_op jit(solution)/shard_map/ppermute | solution.py:734
  158.9 2.7 %collective-permute-start.29 = (bf16[2,256,256]{2,1,0:T(8,128)(2,1)S(1)}, bf16[2,256,256]{2,1,0:T(8,128)(2,1)S(1)}, u32[]{:S(2)}, u32[]{:S(2)}) collective-permute-start(bf16[2,256,256]{2,1,0:T(8,128)(2,1)S(1)} %get-tuple-element.52), channel_id=1, source_target_pairs={{0,12},{4,0},{8,4},{12,8},{16,28},{20,16},{24,20},{28,24},{32,44},... | collective-permute-start | bytes 786440 | tf_op jit(solution)/shard_map/ppermute | solution.py:31
  161.5 15.3 %collective-permute-done.28.refs_2_ = bf16[2,256,256]{2,1,0:T(8,128)(2,1)S(1)} collective-permute-done((bf16[2,256,256]{2,1,0:T(8,128)(2,1)S(1)}, bf16[2,256,256]{2,1,0:T(8,128)(2,1)S(1)}, u32[]{:S(2)}, u32[]{:S(2)}) %collective-permute-start.28) | collective-permute-done | bytes 262176 | tf_op jit(solution)/shard_map/ppermute | solution.py:31
  176.8 4.9 %collective-permute-done.30.refs_4_ = bf16[2,256,256]{2,1,0:T(8,128)(2,1)S(1)} collective-permute-done((bf16[2,256,256]{2,1,0:T(8,128)(2,1)S(1)}, bf16[2,256,256]{2,1,0:T(8,128)(2,1)S(1)}, u32[]{:S(2)}, u32[]{:S(2)}) %collective-permute-start.30) | collective-permute-done | bytes 262176 | tf_op jit(solution)/shard_map/ppermute | solution.py:31
  182.4 3.4 %collective-permute-start.31 = (bf16[256,256]{1,0:T(8,128)(2,1)S(1)}, bf16[256,256]{1,0:T(8,128)(2,1)S(1)}, u32[]{:S(2)}, u32[]{:S(2)}) collective-permute-start(bf16[256,256]{1,0:T(8,128)(2,1)S(1)} %get-tuple-element.55), channel_id=1, source_target_pairs={{0,2},{1,3},{2,0},{3,1},{4,6},{5,7},{6,4},{7,5},{8,10},{9,11},{10,... | collective-permute-start | bytes 393224 | tf_op jit(solution)/shard_map/ppermute | solution.py:746
  185.8 5.1 %shard_map.174.refs_8_ = bf16[256,4096]{1,0:T(8,128)(2,1)} custom-call(s32[14]{0:T(128)S(1)} %concatenate.3.refs_0_, bf16[256,512]{1,0:T(8,128)(2,1)S(1)} %get-tuple-element.29.refs_1_, bf16[512,256]{1,0:T(8,128)(2,1)S(1)} %copy-done.19, f32[4,256,16]{2,1,0:T(8,128)S(1)} %copy-done.15, f32[64,256]{1,0:T(8,128)S(1)} %get-tuple-element.32.refs_4_, ...), custom_call_target="tpu_custom_call" | custom-call | flops 1000000 | bytes 10000 | tf_op jit(solution)/shard_map/pallas_call | solution.py:55
  191.0 2.5 %shard_map.175 = bf16[256,4096]{1,0:T(8,128)(2,1)} custom-call(s32[14]{0:T(128)S(1)} %concatenate.3.refs_0_, bf16[256,512]{1,0:T(8,128)(2,1)S(1)} %get-tuple-element.29.refs_1_, bf16[512,256]{1,0:T(8,128)(2,1)S(1)} %copy-done.19, f32[4,256,16]{2,1,0:T(8,128)S(1)} %copy-done.15, ...), custom_call_target="tpu_custom_call", output_to_operand_aliasing={{}: (8, {})} | custom-call | flops 1000000 | bytes 10000 | tf_op jit(solution)/shard_map/pallas_call | solution.py:55
  (122 shorter events, 34.2 us)
Async XLA Ops:
  5.3 6.1 %collective-permute-start.4 = (bf16[3,5120]{1,0:T(4,128)(2,1)S(1)}, bf16[3,5120]{1,0:T(4,128)(2,1)S(1)}, u32[]{:S(2)}, u32[]{:S(2)}) collective-permute-start(bf16[3,5120]{1,0:T(4,128)(2,1)S(1)} %shard_map.167), channel_id=1, source_target_pairs={{124,112},{125,113},{126,114},{127,115}} | collective-permute-start | bytes 92168 | tf_op jit(solution)/shard_map/ppermute | solution.py:594
  6.0 5.5 %collective-permute-start.5 = (bf16[3,5120]{1,0:T(4,128)(2,1)S(1)}, bf16[3,5120]{1,0:T(4,128)(2,1)S(1)}, u32[]{:S(2)}, u32[]{:S(2)}) collective-permute-start(bf16[3,5120]{1,0:T(4,128)(2,1)S(1)} %shard_map.167), channel_id=1, source_target_pairs={{124,116},{125,117},{126,118},{127,119}} | collective-permute-start | bytes 92168 | tf_op jit(solution)/shard_map/ppermute | solution.py:594
  6.7 4.8 %collective-permute-start.6 = (bf16[3,5120]{1,0:T(4,128)(2,1)S(1)}, bf16[3,5120]{1,0:T(4,128)(2,1)S(1)}, u32[]{:S(2)}, u32[]{:S(2)}) collective-permute-start(bf16[3,5120]{1,0:T(4,128)(2,1)S(1)} %shard_map.167), channel_id=1, source_target_pairs={{124,120},{125,121},{126,122},{127,123}} | collective-permute-start | bytes 92168 | tf_op jit(solution)/shard_map/ppermute | solution.py:594
  7.4 5.1 %collective-permute-start = (bf16[3,5120]{1,0:T(4,128)(2,1)S(1)}, bf16[3,5120]{1,0:T(4,128)(2,1)S(1)}, u32[]{:S(2)}, u32[]{:S(2)}) collective-permute-start(bf16[3,5120]{1,0:T(4,128)(2,1)S(1)} %shard_map.167), channel_id=1, source_target_pairs={{0,4},{4,8},{8,12},{12,16},{16,20},{20,24},{24,28},{28,32},{32,36}... | collective-permute-start | bytes 92168 | tf_op jit(solution)/shard_map/ppermute | solution.py:590
  11.6 19.0 %collective-permute-start.7 = (bf16[3,5120]{1,0:T(4,128)(2,1)S(1)}, bf16[3,5120]{1,0:T(4,128)(2,1)S(1)}, u32[]{:S(2)}, u32[]{:S(2)}) collective-permute-start(bf16[3,5120]{1,0:T(4,128)(2,1)S(1)} %select_select_fusion), channel_id=1, source_target_pairs={{112,96},{116,100},{120,104},{124,108},{113,97},{117,101},{121,105... | collective-permute-start | bytes 92168 | tf_op jit(solution)/shard_map/ppermute | solution.py:597
  26.4 36.7 %collective-permute-start.1 = (bf16[272,1024]{1,0:T(8,128)(2,1)}, bf16[272,1024]{1,0:T(8,128)(2,1)S(1)}, u32[]{:S(2)}, u32[]{:S(2)}) collective-permute-start(bf16[272,1024]{1,0:T(8,128)(2,1)} %get-tuple-element.36), channel_id=1, source_target_pairs={{0,12},{4,0},{8,4},{12,8},{16,28},{20,16},{24,20},{28,24},{32,44},... | collective-permute-start | bytes 1671176 | tf_op jit(solution)/shard_map/ppermute | solution.py:31
  29.6 33.6 %collective-permute-start.2 = (bf16[272,1024]{1,0:T(8,128)(2,1)}, bf16[272,1024]{1,0:T(8,128)(2,1)S(1)}, u32[]{:S(2)}, u32[]{:S(2)}) collective-permute-start(bf16[272,1024]{1,0:T(8,128)(2,1)} %get-tuple-element.37), channel_id=1, source_target_pairs={{0,8},{4,12},{8,0},{12,4},{16,24},{20,28},{24,16},{28,20},{32,40},... | collective-permute-start | bytes 1671176 | tf_op jit(solution)/shard_map/ppermute | solution.py:31
  29.9 33.2 %collective-permute-start.3 = (bf16[272,1024]{1,0:T(8,128)(2,1)}, bf16[272,1024]{1,0:T(8,128)(2,1)S(1)}, u32[]{:S(2)}, u32[]{:S(2)}) collective-permute-start(bf16[272,1024]{1,0:T(8,128)(2,1)} %get-tuple-element.38), channel_id=1, source_target_pairs={{0,4},{4,8},{8,12},{12,0},{16,20},{20,24},{24,28},{28,16},{32,36},... | collective-permute-start | bytes 1671176 | tf_op jit(solution)/shard_map/ppermute | solution.py:31
  31.3 2.1 %collective-permute-start.9 = (bf16[3,5120]{1,0:T(4,128)(2,1)S(1)}, bf16[3,5120]{1,0:T(4,128)(2,1)S(1)}, u32[]{:S(2)}, u32[]{:S(2)}) collective-permute-start(bf16[3,5120]{1,0:T(4,128)(2,1)S(1)} %broadcast_select_fusion.refs_1_), channel_id=1, source_target_pairs={{96,32},{100,36},{104,40},{108,44},{112,48},{116,52},{120,56},{124... | collective-permute-start | bytes 92168 | tf_op jit(solution)/shard_map/ppermute | solution.py:604
  32.0 8.6 %collective-permute-start.10 = (bf16[3,5120]{1,0:T(4,128)(2,1)S(1)}, bf16[3,5120]{1,0:T(4,128)(2,1)S(1)}, u32[]{:S(2)}, u32[]{:S(2)}) collective-permute-start(bf16[3,5120]{1,0:T(4,128)(2,1)S(1)} %broadcast_select_fusion.refs_1_), channel_id=1, source_target_pairs={{96,0},{100,4},{104,8},{108,12},{112,16},{116,20},{120,24},{124,28... | collective-permute-start | bytes 92168 | tf_op jit(solution)/shard_map/ppermute | solution.py:604
  45.2 10.1 %collective-permute-start.11 = (bf16[32,1408]{1,0:T(8,128)(2,1)S(1)}, bf16[32,1408]{1,0:T(8,128)(2,1)S(1)}, u32[]{:S(2)}, u32[]{:S(2)}) collective-permute-start(bf16[32,1408]{1,0:T(8,128)(2,1)S(1)} %get-tuple-element.58), channel_id=1, source_target_pairs={{0,12},{4,0},{8,4},{12,8},{16,28},{20,16},{24,20},{28,24},{32,44},... | collective-permute-start | bytes 270344 | tf_op jit(solution)/shard_map/ppermute | solution.py:31
  47.7 10.9 %collective-permute-start.12 = (bf16[32,1408]{1,0:T(8,128)(2,1)S(1)}, bf16[32,1408]{1,0:T(8,128)(2,1)S(1)}, u32[]{:S(2)}, u32[]{:S(2)}) collective-permute-start(bf16[32,1408]{1,0:T(8,128)(2,1)S(1)} %get-tuple-element.57), channel_id=1, source_target_pairs={{0,8},{4,12},{8,0},{12,4},{16,24},{20,28},{24,16},{28,20},{32,40},... | collective-permute-start | bytes 270344 | tf_op jit(solution)/shard_map/ppermute | solution.py:31
  55.3 6.4 %collective-permute-start.13 = (bf16[32,1408]{1,0:T(8,128)(2,1)S(1)}, bf16[32,1408]{1,0:T(8,128)(2,1)S(1)}, u32[]{:S(2)}, u32[]{:S(2)}) collective-permute-start(bf16[32,1408]{1,0:T(8,128)(2,1)S(1)} %get-tuple-element.56), channel_id=1, source_target_pairs={{0,4},{4,8},{8,12},{12,0},{16,20},{20,24},{24,28},{28,16},{32,36},... | collective-permute-start | bytes 270344 | tf_op jit(solution)/shard_map/ppermute | solution.py:31
  80.5 14.0 %all-to-all-start.1 = ((bf16[8,512,128]{2,1,0:T(8,128)(2,1)}), bf16[8,512,128]{2,1,0:T(8,128)(2,1)S(1)}, u32[]{:S(2)}, u32[]{:S(2)}) async-start(bf16[8,512,128]{2,1,0:T(8,128)(2,1)} %shard_map.172), calls=%async_computation.1 | async-start | bytes 2097152 | tf_op jit(solution)/shard_map/all_to_all | solution.py:696
  84.1 18.3 %collective-permute-start.17 = (bf16[128,1408]{1,0:T(8,128)(2,1)}, bf16[128,1408]{1,0:T(8,128)(2,1)}, u32[]{:S(2)}, u32[]{:S(2)}) collective-permute-start(bf16[128,1408]{1,0:T(8,128)(2,1)} %bitcast.26), channel_id=1, source_target_pairs={{0,96},{4,100},{8,104},{12,108},{16,112},{20,116},{24,120},{28,124... | collective-permute-start | bytes 1081352 | tf_op jit(solution)/shard_map/ppermute | solution.py:31
  86.7 17.6 %collective-permute-start.20 = (bf16[4,32,1408]{2,1,0:T(8,128)(2,1)}, bf16[4,32,1408]{2,1,0:T(8,128)(2,1)}, u32[]{:S(2)}, u32[]{:S(2)}) collective-permute-start(bf16[4,32,1408]{2,1,0:T(8,128)(2,1)} %copy-done.20), channel_id=1, source_target_pairs={{0,16},{4,20},{8,24},{12,28},{16,0},{20,4},{24,8},{28,12},{32,48},... | collective-permute-start | bytes 1081352 | tf_op jit(solution)/shard_map/ppermute | solution.py:31
  87.9 20.7 %collective-permute-start.18 = (bf16[128,1408]{1,0:T(8,128)(2,1)}, bf16[128,1408]{1,0:T(8,128)(2,1)}, u32[]{:S(2)}, u32[]{:S(2)}) collective-permute-start(bf16[128,1408]{1,0:T(8,128)(2,1)} %bitcast.27), channel_id=1, source_target_pairs={{0,64},{4,68},{8,72},{12,76},{16,80},{20,84},{24,88},{28,92},{32,9... | collective-permute-start | bytes 1081352 | tf_op jit(solution)/shard_map/ppermute | solution.py:31
  88.4 24.4 %collective-permute-start.19 = (bf16[128,1408]{1,0:T(8,128)(2,1)}, bf16[128,1408]{1,0:T(8,128)(2,1)}, u32[]{:S(2)}, u32[]{:S(2)}) collective-permute-start(bf16[128,1408]{1,0:T(8,128)(2,1)} %bitcast.28), channel_id=1, source_target_pairs={{0,32},{4,36},{8,40},{12,44},{16,48},{20,52},{24,56},{28,60},{32,6... | collective-permute-start | bytes 1081352 | tf_op jit(solution)/shard_map/ppermute | solution.py:31
  101.1 14.6 %collective-permute-start.15 = (bf16[256,1024]{1,0:T(8,128)(2,1)S(1)}, bf16[256,1024]{1,0:T(8,128)(2,1)S(1)}, u32[]{:S(2)}, u32[]{:S(2)}) collective-permute-start(bf16[256,1024]{1,0:T(8,128)(2,1)S(1)} %get-tuple-element.44), channel_id=1, source_target_pairs={{0,12},{4,0},{8,4},{12,8},{16,28},{20,16},{24,20},{28,24},{32,44},... | collective-permute-start | bytes 1572872 | tf_op jit(solution)/shard_map/ppermute | solution.py:31
  102.4 16.4 %collective-permute-start.16 = (bf16[256,1024]{1,0:T(8,128)(2,1)S(1)}, bf16[256,1024]{1,0:T(8,128)(2,1)S(1)}, u32[]{:S(2)}, u32[]{:S(2)}) collective-permute-start(bf16[256,1024]{1,0:T(8,128)(2,1)S(1)} %get-tuple-element.45), channel_id=1, source_target_pairs={{0,4},{4,8},{8,12},{12,0},{16,20},{20,24},{24,28},{28,16},{32,36},... | collective-permute-start | bytes 1572872 | tf_op jit(solution)/shard_map/ppermute | solution.py:31
  104.3 11.4 %collective-permute-start.21 = (bf16[128,1408]{1,0:T(8,128)(2,1)}, bf16[128,1408]{1,0:T(8,128)(2,1)S(1)}, u32[]{:S(2)}, u32[]{:S(2)}) collective-permute-start(bf16[128,1408]{1,0:T(8,128)(2,1)} %bitcast.16.refs_6_), channel_id=1, source_target_pairs={{0,96},{4,100},{8,104},{12,108},{16,112},{20,116},{24,120},{28,124... | collective-permute-start | bytes 1081352 | tf_op jit(solution)/shard_map/ppermute | solution.py:31
  108.6 19.4 %collective-permute-start.24 = (bf16[1024,256]{1,0:T(8,128)(2,1)S(1)}, bf16[1024,256]{1,0:T(8,128)(2,1)S(1)}, u32[]{:S(2)}, u32[]{:S(2)}) collective-permute-start(bf16[1024,256]{1,0:T(8,128)(2,1)S(1)} %shard_map.176), channel_id=1, source_target_pairs={{0,12},{4,0},{8,4},{12,8},{16,28},{20,16},{24,20},{28,24},{32,44},... | collective-permute-start | bytes 1572872 | tf_op jit(solution)/shard_map/ppermute | solution.py:31
  112.8 15.1 %collective-permute-start.25 = (bf16[1024,256]{1,0:T(8,128)(2,1)S(1)}, bf16[1024,256]{1,0:T(8,128)(2,1)S(1)}, u32[]{:S(2)}, u32[]{:S(2)}) collective-permute-start(bf16[1024,256]{1,0:T(8,128)(2,1)S(1)} %shard_map.177), channel_id=1, source_target_pairs={{0,8},{4,12},{8,0},{12,4},{16,24},{20,28},{24,16},{28,20},{32,40},... | collective-permute-start | bytes 1572872 | tf_op jit(solution)/shard_map/ppermute | solution.py:31
  115.7 18.5 %collective-permute-start.26 = (bf16[1024,256]{1,0:T(8,128)(2,1)S(1)}, bf16[1024,256]{1,0:T(8,128)(2,1)S(1)}, u32[]{:S(2)}, u32[]{:S(2)}) collective-permute-start(bf16[1024,256]{1,0:T(8,128)(2,1)S(1)} %shard_map.178), channel_id=1, source_target_pairs={{0,4},{4,8},{8,12},{12,0},{16,20},{20,24},{24,28},{28,16},{32,36},... | collective-permute-start | bytes 1572872 | tf_op jit(solution)/shard_map/ppermute | solution.py:31
  115.7 8.2 %collective-permute-start.22 = (bf16[128,1408]{1,0:T(8,128)(2,1)}, bf16[128,1408]{1,0:T(8,128)(2,1)S(1)}, u32[]{:S(2)}, u32[]{:S(2)}) collective-permute-start(bf16[128,1408]{1,0:T(8,128)(2,1)} %bitcast.16.refs_6_), channel_id=1, source_target_pairs={{0,64},{4,68},{8,72},{12,76},{16,80},{20,84},{24,88},{28,92},{32,9... | collective-permute-start | bytes 1081352 | tf_op jit(solution)/shard_map/ppermute | solution.py:31
  118.7 9.2 %collective-permute-start.23 = (bf16[128,1408]{1,0:T(8,128)(2,1)}, bf16[128,1408]{1,0:T(8,128)(2,1)S(1)}, u32[]{:S(2)}, u32[]{:S(2)}) collective-permute-start(bf16[128,1408]{1,0:T(8,128)(2,1)} %bitcast.16.refs_6_), channel_id=1, source_target_pairs={{0,32},{4,36},{8,40},{12,44},{16,48},{20,52},{24,56},{28,60},{32,6... | collective-permute-start | bytes 1081352 | tf_op jit(solution)/shard_map/ppermute | solution.py:31
  143.9 14.1 %collective-permute-start.27 = (bf16[4,2,256,256]{3,2,1,0:T(8,128)(2,1)}, bf16[4,2,256,256]{3,2,1,0:T(8,128)(2,1)S(1)}, u32[]{:S(2)}, u32[]{:S(2)}) collective-permute-start(bf16[4,2,256,256]{3,2,1,0:T(8,128)(2,1)} %get-tuple-element.49), channel_id=1, source_target_pairs={{0,1},{1,0},{2,3},{3,2},{4,5},{5,4},{6,7},{7,6},{8,9},{9,8},{10,11... | collective-permute-start | bytes 3145736 | tf_op jit(solution)/shard_map/ppermute | solution.py:734
  155.5 35.5 %collective-permute-start.14 = (bf16[256,1024]{1,0:T(8,128)(2,1)S(1)}, bf16[256,1024]{1,0:T(8,128)(2,1)S(1)}, u32[]{:S(2)}, u32[]{:S(2)}) collective-permute-start(bf16[256,1024]{1,0:T(8,128)(2,1)S(1)} %get-tuple-element.42), channel_id=1, source_target_pairs={{0,8},{4,12},{8,0},{12,4},{16,24},{20,28},{24,16},{28,20},{32,40},... | collective-permute-start | bytes 1572872 | tf_op jit(solution)/shard_map/ppermute | solution.py:31
  158.8 18.1 %collective-permute-start.28 = (bf16[2,256,256]{2,1,0:T(8,128)(2,1)S(1)}, bf16[2,256,256]{2,1,0:T(8,128)(2,1)S(1)}, u32[]{:S(2)}, u32[]{:S(2)}) collective-permute-start(bf16[2,256,256]{2,1,0:T(8,128)(2,1)S(1)} %get-tuple-element.51), channel_id=1, source_target_pairs={{0,4},{4,8},{8,12},{12,0},{16,20},{20,24},{24,28},{28,16},{32,36},... | collective-permute-start | bytes 786440 | tf_op jit(solution)/shard_map/ppermute | solution.py:31
  158.9 18.0 %collective-permute-start.29 = (bf16[2,256,256]{2,1,0:T(8,128)(2,1)S(1)}, bf16[2,256,256]{2,1,0:T(8,128)(2,1)S(1)}, u32[]{:S(2)}, u32[]{:S(2)}) collective-permute-start(bf16[2,256,256]{2,1,0:T(8,128)(2,1)S(1)} %get-tuple-element.52), channel_id=1, source_target_pairs={{0,12},{4,0},{8,4},{12,8},{16,28},{20,16},{24,20},{28,24},{32,44},... | collective-permute-start | bytes 786440 | tf_op jit(solution)/shard_map/ppermute | solution.py:31
  161.5 20.2 %collective-permute-start.30 = (bf16[2,256,256]{2,1,0:T(8,128)(2,1)S(1)}, bf16[2,256,256]{2,1,0:T(8,128)(2,1)S(1)}, u32[]{:S(2)}, u32[]{:S(2)}) collective-permute-start(bf16[2,256,256]{2,1,0:T(8,128)(2,1)S(1)} %get-tuple-element.53), channel_id=1, source_target_pairs={{0,8},{4,12},{8,0},{12,4},{16,24},{20,28},{24,16},{28,20},{32,40},... | collective-permute-start | bytes 786440 | tf_op jit(solution)/shard_map/ppermute | solution.py:31
  182.4 11.1 %collective-permute-start.31 = (bf16[256,256]{1,0:T(8,128)(2,1)S(1)}, bf16[256,256]{1,0:T(8,128)(2,1)S(1)}, u32[]{:S(2)}, u32[]{:S(2)}) collective-permute-start(bf16[256,256]{1,0:T(8,128)(2,1)S(1)} %get-tuple-element.55), channel_id=1, source_target_pairs={{0,2},{1,3},{2,0},{3,1},{4,6},{5,7},{6,4},{7,5},{8,10},{9,11},{10,... | collective-permute-start | bytes 393224 | tf_op jit(solution)/shard_map/ppermute | solution.py:746
  (33 other events, 499.2 us)

commit v3 on v2

--- a/solution.py
+++ b/solution.py
@@ -14,7 +14,7 @@
 X, Z, Y = 4, 2, 4
 F32 = jnp.float32
 BF16 = jnp.bfloat16
-VMEM_BYTES = 48 * 2**20
+VMEM_BYTES = 24 * 2**20
 
 
 def place(x, z, y):
@@ -66,7 +66,7 @@
         input_output_aliases=aliases,
         compiler_params=pltpu.CompilerParams(vmem_limit_bytes=VMEM_BYTES),
         cost_estimate=pl.CostEstimate(
-            flops=10**6, bytes_accessed=10**4, transcendentals=0
+            flops=4 * 10**9, bytes_accessed=10**4, transcendentals=0
         ),
     )(ids, *[split(entry)[0] for entry in ins], *extra)
 

time: 195 us -> 190 us (0.974)
  blocking collectives: 14.6 us -> 0 us
  starting transfers between devices: 56.8 us -> 63.5 us
  waiting for transfers between devices: 66.4 us -> 71 us
  Pallas kernels: 41.5 us -> 39 us
    all_to_all x1 -> x0, blocking collectives: 14.6 us -> none  [shards(): lax.all_to_all(totals, 'ctx', 0, 0, tiled=True, axis_index_groups=groups)]
    all_to_all x0 -> x1, starting transfers between devices: none -> 9.31 us  [shards(): lax.all_to_all(totals, 'ctx', 0, 0, tiled=True, axis_index_groups=groups)]
    ppermute x22, waiting for transfers between devices: 52 us -> 60.8 us  [shifted(): return lax.ppermute(value, 'ctx', pairs)]
    ppermute x3, waiting for transfers between devices: 7.18 us -> 0.01 us  [shards(): lax.ppermute(moved, 'ctx', [(place(X - 1, z, y), place(X - 1 - step, z, y...]
    all_to_all x0 -> x1, waiting for transfers between devices: none -> 5.89 us  [shards(): lax.all_to_all(totals, 'ctx', 0, 0, tiled=True, axis_index_groups=groups)]
    ppermute x22, starting transfers between devices: 28.8 us -> 23.3 us  [shifted(): return lax.ppermute(value, 'ctx', pairs)]
    all_to_all x1, waiting for transfers between devices: 5.53 us -> 1.64 us  [shards(): lax.all_to_all(back, 'ctx', 0, 0, tiled=True, axis_index_groups=groups)]
    ppermute x1, starting transfers between devices: 11.6 us -> 14.4 us  [shards(): other = lax.ppermute(send, 'head', [(i, i ^ 1) for i in range(4)])]
  transfers between devices with their start and end apart: 33 -> 34, of which waited for: 13 -> 14; matrix products, arithmetic and copies ran while one was open for 0% -> 0% of each run, Pallas kernels for 14% -> 14%
where the time goes in v3:
time: 190 us; the launch traced here: 188 us
  waiting for transfers between devices  71 us (37%)
  starting transfers between devices  63.5 us (33%)
  Pallas kernels  39 us (21%)
  local copies, waits for them, and re-layouts  12.8 us (7%)
  between operations  2.05 us (1%)
    ppermute x22, waiting for transfers between devices, shifted(): return lax.ppermute(value, 'ctx', pairs)  60.8 us
    pallas_call x16, Pallas kernels, call(): pl.pallas_call(body, grid_spec=pltpu.PrefetchScalarGridSpec(num_scalar_pr...  39 us
    ppermute x22, starting transfers between devices, shifted(): return lax.ppermute(value, 'ctx', pairs)  23.3 us
    ppermute x1, starting transfers between devices, shards(): other = lax.ppermute(send, 'head', [(i, i ^ 1) for i in range(4)])  14.4 us
    unnamed x81, local copies, waits for them, and re-layouts  12 us
    all_to_all x1, starting transfers between devices, shards(): lax.all_to_all(totals, 'ctx', 0, 0, tiled=True, axis_index_groups=groups)  9.31 us
    all_to_all x1, waiting for transfers between devices, shards(): lax.all_to_all(totals, 'ctx', 0, 0, tiled=True, axis_index_groups=groups)  5.89 us
    ppermute x1, starting transfers between devices, shards(): rim = lax.ppermute(tails, 'ctx', [(i, i + 1) for i in range(devices - 1)])  4.03 us
  transfers between devices with their start and end apart: 34, of which 14 were waited for; matrix products, arithmetic and copies ran while one was open for 0% of the time, Pallas kernels for 14%

profile of v3, /device:TPU:1, one launch (start us, length us, event | category | flops | bytes accessed | tf_op | source)
XLA Modules:
  0.0 188.4 jit_solution(2073472814394952552)
XLA Ops:
  8.2 4.0 %collective-permute-start = (bf16[3,5120]{1,0:T(4,128)(2,1)S(1)}, bf16[3,5120]{1,0:T(4,128)(2,1)S(1)}, u32[]{:S(2)}, u32[]{:S(2)}) collective-permute-start(bf16[3,5120]{1,0:T(4,128)(2,1)S(1)} %shard_map.167), channel_id=1, source_target_pairs={{0,4},{4,8},{8,12},{12,16},{16,20},{20,24},{24,28},{28,32},{32,36}... | collective-permute-start | bytes 92168 | tf_op jit(solution)/shard_map/ppermute | solution.py:590
  15.3 8.4 %shard_map.168 = (bf16[256,512]{1,0:T(8,128)(2,1)S(1)}, bf16[512,256]{1,0:T(8,128)(2,1)S(1)}, f32[4,256,16]{2,1,0:T(8,128)S(1)}, f32[64,256]{1,0:T(8,128)S(1)}, ...) custom-call(s32[14]{0:T(128)S(1)} %concatenate.3.refs_0_, ...), custom_call_target="tpu_custom_call" | custom-call | flops 4000000000 | bytes 10000 | tf_op jit(solution)/shard_map/pallas_call | solution.py:55
  27.1 2.7 %collective-permute-start.1 = (bf16[272,1024]{1,0:T(8,128)(2,1)S(1)}, bf16[272,1024]{1,0:T(8,128)(2,1)S(1)}, u32[]{:S(2)}, u32[]{:S(2)}) collective-permute-start(bf16[272,1024]{1,0:T(8,128)(2,1)S(1)} %get-tuple-element.36), channel_id=1, source_target_pairs={{0,12},{4,0},{8,4},{12,8},{16,28},{20,16},{24,20},{28,24},{32,44},... | collective-permute-start | bytes 1671176 | tf_op jit(solution)/shard_map/ppermute | solution.py:31
  30.6 2.5 %shard_map.169 = bf16[4,32,1408]{2,1,0:T(8,128)(2,1)S(1)} custom-call(s32[14]{0:T(128)S(1)} %concatenate.3.refs_0_, bf16[3,5120]{1,0:T(4,128)(2,1)S(1)} %broadcast_select_fusion.refs_1_, bf16[3,5120]{1,0:T(4,128)(2,1)S(1)} %collective-permute-done.8.refs_2_, bf16[3,5120]{1,0:T(4,128)(2,1)S(1)} %collective-permute-done.9.refs_3_, ...), custom_call_target="tpu_custom_call" | custom-call | flops 4000000000 | bytes 10000 | tf_op jit(solution)/shard_map/pallas_call | solution.py:55
  33.2 2.3 %collective-permute-start.11 = (bf16[32,1408]{1,0:T(8,128)(2,1)S(1)}, bf16[32,1408]{1,0:T(8,128)(2,1)S(1)}, u32[]{:S(2)}, u32[]{:S(2)}) collective-permute-start(bf16[32,1408]{1,0:T(8,128)(2,1)S(1)} %get-tuple-element.58), channel_id=1, source_target_pairs={{0,12},{4,0},{8,4},{12,8},{16,28},{20,16},{24,20},{28,24},{32,44},... | collective-permute-start | bytes 270344 | tf_op jit(solution)/shard_map/ppermute | solution.py:31
  36.9 18.6 %collective-permute-done.11.refs_2_ = bf16[32,1408]{1,0:T(8,128)(2,1)S(1)} collective-permute-done((bf16[32,1408]{1,0:T(8,128)(2,1)S(1)}, bf16[32,1408]{1,0:T(8,128)(2,1)S(1)}, u32[]{:S(2)}, u32[]{:S(2)}) %collective-permute-start.11) | collective-permute-done | bytes 90144 | tf_op jit(solution)/shard_map/ppermute | solution.py:31
  55.5 2.4 %collective-permute-done.12.refs_3_ = bf16[32,1408]{1,0:T(8,128)(2,1)S(1)} collective-permute-done((bf16[32,1408]{1,0:T(8,128)(2,1)S(1)}, bf16[32,1408]{1,0:T(8,128)(2,1)S(1)}, u32[]{:S(2)}, u32[]{:S(2)}) %collective-permute-start.12) | collective-permute-done | bytes 90144 | tf_op jit(solution)/shard_map/ppermute | solution.py:31
  57.8 3.4 %collective-permute-done.13.refs_4_ = bf16[32,1408]{1,0:T(8,128)(2,1)S(1)} collective-permute-done((bf16[32,1408]{1,0:T(8,128)(2,1)S(1)}, bf16[32,1408]{1,0:T(8,128)(2,1)S(1)}, u32[]{:S(2)}, u32[]{:S(2)}) %collective-permute-start.13) | collective-permute-done | bytes 90144 | tf_op jit(solution)/shard_map/ppermute | solution.py:31
  61.9 1.9 %shard_map.171 = (bf16[8,272,128]{2,1,0:T(8,128)(2,1)}, f32[8,128]{1,0:T(8,128)S(1)}) custom-call(s32[14]{0:T(128)S(1)} %concatenate.3.refs_0_, bf16[272,1024]{1,0:T(8,128)(2,1)S(1)} %get-tuple-element.35.refs_1_.refs_2_, bf16[272,1024]{1,0:T(8,128)(2,1)S(1)} %collective-permute-done.1.refs_2_.refs_3_, ...), custom_call_target="tpu_custom_call" | custom-call | flops 4000000000 | bytes 10000 | tf_op jit(solution)/shard_map/pallas_call | solution.py:55
  63.8 9.3 %all-to-all-start = ((bf16[8,272,128]{2,1,0:T(8,128)(2,1)}), bf16[8,272,128]{2,1,0:T(8,128)(2,1)S(1)}, u32[]{:S(2)}, u32[]{:S(2)}) async-start(bf16[8,272,128]{2,1,0:T(8,128)(2,1)} %get-tuple-element.41), calls=%async_computation | async-start | bytes 1114112 | tf_op jit(solution)/shard_map/all_to_all | solution.py:694
  74.6 5.9 %all-to-all-done.refs_1_ = bf16[8,272,128]{2,1,0:T(8,128)(2,1)S(1)} async-done(((bf16[8,272,128]{2,1,0:T(8,128)(2,1)}), bf16[8,272,128]{2,1,0:T(8,128)(2,1)S(1)}, u32[]{:S(2)}, u32[]{:S(2)}) %all-to-all-start) | async-done | bytes 557088 | tf_op jit(solution)/shard_map/all_to_all | solution.py:694
  80.5 1.7 shard_map.172
  82.1 3.7 %all-to-all-start.1 = ((bf16[8,512,128]{2,1,0:T(8,128)(2,1)}), bf16[8,512,128]{2,1,0:T(8,128)(2,1)S(1)}, u32[]{:S(2)}, u32[]{:S(2)}) async-start(bf16[8,512,128]{2,1,0:T(8,128)(2,1)} %shard_map.172), calls=%async_computation.1 | async-start | bytes 2097152 | tf_op jit(solution)/shard_map/all_to_all | solution.py:696
  85.8 2.6 %collective-permute-start.17 = (bf16[128,1408]{1,0:T(8,128)(2,1)S(1)}, bf16[128,1408]{1,0:T(8,128)(2,1)}, u32[]{:S(2)}, u32[]{:S(2)}) collective-permute-start(bf16[128,1408]{1,0:T(8,128)(2,1)S(1)} %bitcast.26), channel_id=1, source_target_pairs={{0,96},{4,100},{8,104},{12,108},{16,112},{20,116},{24,120},{28,124... | collective-permute-start | bytes 1081352 | tf_op jit(solution)/shard_map/ppermute | solution.py:31
  89.6 2.1 %collective-permute-start.21 = (bf16[128,1408]{1,0:T(8,128)(2,1)}, bf16[128,1408]{1,0:T(8,128)(2,1)}, u32[]{:S(2)}, u32[]{:S(2)}) collective-permute-start(bf16[128,1408]{1,0:T(8,128)(2,1)} %bitcast.16.refs_6_), channel_id=1, source_target_pairs={{0,96},{4,100},{8,104},{12,108},{16,112},{20,116},{24,120},{28,124... | collective-permute-start | bytes 1081352 | tf_op jit(solution)/shard_map/ppermute | solution.py:31
  94.4 1.6 all-to-all-done.1.refs_1_
  100.3 2.3 %shard_map.173 = (bf16[256,1024]{1,0:T(8,128)(2,1)S(1)}, bf16[256,1024]{1,0:T(8,128)(2,1)S(1)}, bf16[256,1024]{1,0:T(8,128)(2,1)S(1)}, bf16[256,1024]{1,0:T(8,128)(2,1)S(1)}) custom-call(s32[14]{0:T(128)S(1)} %concatenate.3.refs_0_, bf16[8,512,128]{2,1,0:T(8,128)(2,1)S(1)} %all-to-all-done.1.refs_1_, bf16[272,1024]{1,0:T(8,128)(2,1)S(1)} %copy-done.35, ...), custom_call_target="tpu_custom_call" | custom-call | flops 4000000000 | bytes 10000 | tf_op jit(solution)/shard_map/pallas_call | solution.py:55
  106.2 4.8 %collective-permute-done.19.refs_5_ = bf16[128,1408]{1,0:T(8,128)(2,1)} collective-permute-done((bf16[128,1408]{1,0:T(8,128)(2,1)S(1)}, bf16[128,1408]{1,0:T(8,128)(2,1)}, u32[]{:S(2)}, u32[]{:S(2)}) %collective-permute-start.19) | collective-permute-done | bytes 360480 | tf_op jit(solution)/shard_map/ppermute | solution.py:31
  111.0 5.8 %collective-permute-done.21.refs_7_ = bf16[128,1408]{1,0:T(8,128)(2,1)} collective-permute-done((bf16[128,1408]{1,0:T(8,128)(2,1)}, bf16[128,1408]{1,0:T(8,128)(2,1)}, u32[]{:S(2)}, u32[]{:S(2)}) %collective-permute-start.21) | collective-permute-done | bytes 360480 | tf_op jit(solution)/shard_map/ppermute | solution.py:31
  116.9 3.0 %collective-permute-start.22 = (bf16[128,1408]{1,0:T(8,128)(2,1)}, bf16[128,1408]{1,0:T(8,128)(2,1)S(1)}, u32[]{:S(2)}, u32[]{:S(2)}) collective-permute-start(bf16[128,1408]{1,0:T(8,128)(2,1)} %bitcast.16.refs_6_), channel_id=1, source_target_pairs={{0,64},{4,68},{8,72},{12,76},{16,80},{20,84},{24,88},{28,92},{32,9... | collective-permute-start | bytes 1081352 | tf_op jit(solution)/shard_map/ppermute | solution.py:31
  119.9 5.1 %collective-permute-done.22.refs_8_ = bf16[128,1408]{1,0:T(8,128)(2,1)S(1)} collective-permute-done((bf16[128,1408]{1,0:T(8,128)(2,1)}, bf16[128,1408]{1,0:T(8,128)(2,1)S(1)}, u32[]{:S(2)}, u32[]{:S(2)}) %collective-permute-start.22) | collective-permute-done | bytes 360480 | tf_op jit(solution)/shard_map/ppermute | solution.py:31
  125.0 4.1 %collective-permute-done.23.refs_9_ = bf16[128,1408]{1,0:T(8,128)(2,1)S(1)} collective-permute-done((bf16[128,1408]{1,0:T(8,128)(2,1)}, bf16[128,1408]{1,0:T(8,128)(2,1)S(1)}, u32[]{:S(2)}, u32[]{:S(2)}) %collective-permute-start.23) | collective-permute-done | bytes 360480 | tf_op jit(solution)/shard_map/ppermute | solution.py:31
  129.1 1.9 %collective-permute-done.26.refs_13_ = bf16[1024,256]{1,0:T(8,128)(2,1)S(1)} collective-permute-done((bf16[1024,256]{1,0:T(8,128)(2,1)S(1)}, bf16[1024,256]{1,0:T(8,128)(2,1)S(1)}, u32[]{:S(2)}, u32[]{:S(2)}) %collective-permute-start.26) | collective-permute-done | bytes 524320 | tf_op jit(solution)/shard_map/ppermute | solution.py:31
  131.0 8.4 %shard_map.179 = (bf16[4,2,256,256]{3,2,1,0:T(8,128)(2,1)S(1)}, bf16[4,2,256,256]{3,2,1,0:T(8,128)(2,1)S(1)}) custom-call(s32[14]{0:T(128)S(1)} %concatenate.3.refs_0_, bf16[8,512,128]{2,1,0:T(8,128)(2,1)S(1)} %all-to-all-done.1.refs_1_, bf16[128,1408]{1,0:T(8,128)(2,1)S(1)} %bitcast.29, bf16[128,1408]{1,0:T(8,128)(2,1)} %collective-permute-done.17.refs_3_, ...), custom_call_target="tpu_custom_call" | custom-call | flops 4000000000 | bytes 10000 | tf_op jit(solution)/shard_map/pallas_call | solution.py:55
  139.4 14.4 %collective-permute-start.27 = (bf16[4,2,256,256]{3,2,1,0:T(8,128)(2,1)S(1)}, bf16[4,2,256,256]{3,2,1,0:T(8,128)(2,1)S(1)}, u32[]{:S(2)}, u32[]{:S(2)}) collective-permute-start(bf16[4,2,256,256]{3,2,1,0:T(8,128)(2,1)S(1)} %get-tuple-element.49), channel_id=1, source_target_pairs={{0,1},{1,0},{2,3},{3,2},{4,5},{5,4},{6,7},{7,6},{8,9},{9,8},{10,11... | collective-permute-start | bytes 3145736 | tf_op jit(solution)/shard_map/ppermute | solution.py:734
  153.9 2.3 %collective-permute-done.27.refs_2_ = bf16[4,2,256,256]{3,2,1,0:T(8,128)(2,1)S(1)} collective-permute-done((bf16[4,2,256,256]{3,2,1,0:T(8,128)(2,1)S(1)}, bf16[4,2,256,256]{3,2,1,0:T(8,128)(2,1)S(1)}, u32[]{:S(2)}, u32[]{:S(2)}) %collective-permute-start.27) | collective-permute-done | bytes 1048608 | tf_op jit(solution)/shard_map/ppermute | solution.py:734
  157.1 2.7 %collective-permute-start.29 = (bf16[2,256,256]{2,1,0:T(8,128)(2,1)S(1)}, bf16[2,256,256]{2,1,0:T(8,128)(2,1)S(1)}, u32[]{:S(2)}, u32[]{:S(2)}) collective-permute-start(bf16[2,256,256]{2,1,0:T(8,128)(2,1)S(1)} %get-tuple-element.52), channel_id=1, source_target_pairs={{0,12},{4,0},{8,4},{12,8},{16,28},{20,16},{24,20},{28,24},{32,44},... | collective-permute-start | bytes 786440 | tf_op jit(solution)/shard_map/ppermute | solution.py:31
  159.8 5.6 %shard_map.174.refs_8_ = bf16[256,4096]{1,0:T(8,128)(2,1)} custom-call(s32[14]{0:T(128)S(1)} %concatenate.3.refs_0_, bf16[256,512]{1,0:T(8,128)(2,1)S(1)} %copy-done.31, bf16[512,256]{1,0:T(8,128)(2,1)S(1)} %copy-done.33, f32[4,256,16]{2,1,0:T(8,128)S(1)} %copy-done.29, f32[64,256]{1,0:T(8,128)S(1)} %copy-done.39, bf16[272,128]{1,0:T(8,128)(2,1)S(1)} %copy-done.37, ...), custom_call_target="tpu_custom_call" | custom-call | flops 4000000000 | bytes 10000 | tf_op jit(solution)/shard_map/pallas_call | solution.py:55
  165.4 9.8 %collective-permute-done.28.refs_2_ = bf16[2,256,256]{2,1,0:T(8,128)(2,1)S(1)} collective-permute-done((bf16[2,256,256]{2,1,0:T(8,128)(2,1)S(1)}, bf16[2,256,256]{2,1,0:T(8,128)(2,1)S(1)}, u32[]{:S(2)}, u32[]{:S(2)}) %collective-permute-start.28) | collective-permute-done | bytes 262176 | tf_op jit(solution)/shard_map/ppermute | solution.py:31
  175.2 4.9 %collective-permute-done.30.refs_4_ = bf16[2,256,256]{2,1,0:T(8,128)(2,1)S(1)} collective-permute-done((bf16[2,256,256]{2,1,0:T(8,128)(2,1)S(1)}, bf16[2,256,256]{2,1,0:T(8,128)(2,1)S(1)}, u32[]{:S(2)}, u32[]{:S(2)}) %collective-permute-start.30) | collective-permute-done | bytes 262176 | tf_op jit(solution)/shard_map/ppermute | solution.py:31
  180.8 3.4 %collective-permute-start.31 = (bf16[256,256]{1,0:T(8,128)(2,1)S(1)}, bf16[256,256]{1,0:T(8,128)(2,1)S(1)}, u32[]{:S(2)}, u32[]{:S(2)}) collective-permute-start(bf16[256,256]{1,0:T(8,128)(2,1)S(1)} %get-tuple-element.55), channel_id=1, source_target_pairs={{0,2},{1,3},{2,0},{3,1},{4,6},{5,7},{6,4},{7,5},{8,10},{9,11},{10,... | collective-permute-start | bytes 393224 | tf_op jit(solution)/shard_map/ppermute | solution.py:746
  184.2 2.7 %shard_map.175 = bf16[256,4096]{1,0:T(8,128)(2,1)} custom-call(s32[14]{0:T(128)S(1)} %concatenate.3.refs_0_, bf16[256,512]{1,0:T(8,128)(2,1)S(1)} %copy-done.31, bf16[512,256]{1,0:T(8,128)(2,1)S(1)} %copy-done.33, f32[4,256,16]{2,1,0:T(8,128)S(1)} %copy-done.29, f32[64,256]{1,0:T(8,128)S(1)} %copy-done.39, ...), custom_call_target="tpu_custom_call", output_to_operand_aliasing={{}: (8, {})} | custom-call | flops 4000000000 | bytes 10000 | tf_op jit(solution)/shard_map/pallas_call | solution.py:55
  (139 shorter events, 32.0 us)
Async XLA Ops:
  5.3 2.2 %collective-permute-start.4 = (bf16[3,5120]{1,0:T(4,128)(2,1)S(1)}, bf16[3,5120]{1,0:T(4,128)(2,1)S(1)}, u32[]{:S(2)}, u32[]{:S(2)}) collective-permute-start(bf16[3,5120]{1,0:T(4,128)(2,1)S(1)} %shard_map.167), channel_id=1, source_target_pairs={{124,112},{125,113},{126,114},{127,115}} | collective-permute-start | bytes 92168 | tf_op jit(solution)/shard_map/ppermute | solution.py:594
  7.6 4.9 %collective-permute-start.7 = (bf16[3,5120]{1,0:T(4,128)(2,1)S(1)}, bf16[3,5120]{1,0:T(4,128)(2,1)S(1)}, u32[]{:S(2)}, u32[]{:S(2)}) collective-permute-start(bf16[3,5120]{1,0:T(4,128)(2,1)S(1)} %select_select_fusion), channel_id=1, source_target_pairs={{112,96},{116,100},{120,104},{124,108},{113,97},{117,101},{121,105... | collective-permute-start | bytes 92168 | tf_op jit(solution)/shard_map/ppermute | solution.py:597
  8.2 6.9 %collective-permute-start = (bf16[3,5120]{1,0:T(4,128)(2,1)S(1)}, bf16[3,5120]{1,0:T(4,128)(2,1)S(1)}, u32[]{:S(2)}, u32[]{:S(2)}) collective-permute-start(bf16[3,5120]{1,0:T(4,128)(2,1)S(1)} %shard_map.167), channel_id=1, source_target_pairs={{0,4},{4,8},{8,12},{12,16},{16,20},{20,24},{24,28},{28,32},{32,36}... | collective-permute-start | bytes 92168 | tf_op jit(solution)/shard_map/ppermute | solution.py:590
  12.5 17.7 %collective-permute-start.8 = (bf16[3,5120]{1,0:T(4,128)(2,1)S(1)}, bf16[3,5120]{1,0:T(4,128)(2,1)S(1)}, u32[]{:S(2)}, u32[]{:S(2)}) collective-permute-start(bf16[3,5120]{1,0:T(4,128)(2,1)S(1)} %broadcast_select_fusion.refs_1_), channel_id=1, source_target_pairs={{96,64},{100,68},{104,72},{108,76},{112,80},{116,84},{120,88},{124... | collective-permute-start | bytes 92168 | tf_op jit(solution)/shard_map/ppermute | solution.py:604
  13.2 17.4 %collective-permute-start.9 = (bf16[3,5120]{1,0:T(4,128)(2,1)S(1)}, bf16[3,5120]{1,0:T(4,128)(2,1)S(1)}, u32[]{:S(2)}, u32[]{:S(2)}) collective-permute-start(bf16[3,5120]{1,0:T(4,128)(2,1)S(1)} %broadcast_select_fusion.refs_1_), channel_id=1, source_target_pairs={{96,32},{100,36},{104,40},{108,44},{112,48},{116,52},{120,56},{124... | collective-permute-start | bytes 92168 | tf_op jit(solution)/shard_map/ppermute | solution.py:604
  13.9 16.7 %collective-permute-start.10 = (bf16[3,5120]{1,0:T(4,128)(2,1)S(1)}, bf16[3,5120]{1,0:T(4,128)(2,1)S(1)}, u32[]{:S(2)}, u32[]{:S(2)}) collective-permute-start(bf16[3,5120]{1,0:T(4,128)(2,1)S(1)} %broadcast_select_fusion.refs_1_), channel_id=1, source_target_pairs={{96,0},{100,4},{104,8},{108,12},{112,16},{116,20},{120,24},{124,28... | collective-permute-start | bytes 92168 | tf_op jit(solution)/shard_map/ppermute | solution.py:604
  27.1 34.7 %collective-permute-start.1 = (bf16[272,1024]{1,0:T(8,128)(2,1)S(1)}, bf16[272,1024]{1,0:T(8,128)(2,1)S(1)}, u32[]{:S(2)}, u32[]{:S(2)}) collective-permute-start(bf16[272,1024]{1,0:T(8,128)(2,1)S(1)} %get-tuple-element.36), channel_id=1, source_target_pairs={{0,12},{4,0},{8,4},{12,8},{16,28},{20,16},{24,20},{28,24},{32,44},... | collective-permute-start | bytes 1671176 | tf_op jit(solution)/shard_map/ppermute | solution.py:31
  29.8 32.0 %collective-permute-start.2 = (bf16[272,1024]{1,0:T(8,128)(2,1)S(1)}, bf16[272,1024]{1,0:T(8,128)(2,1)S(1)}, u32[]{:S(2)}, u32[]{:S(2)}) collective-permute-start(bf16[272,1024]{1,0:T(8,128)(2,1)S(1)} %get-tuple-element.37), channel_id=1, source_target_pairs={{0,8},{4,12},{8,0},{12,4},{16,24},{20,28},{24,16},{28,20},{32,40},... | collective-permute-start | bytes 1671176 | tf_op jit(solution)/shard_map/ppermute | solution.py:31
  30.2 31.7 %collective-permute-start.3 = (bf16[272,1024]{1,0:T(8,128)(2,1)S(1)}, bf16[272,1024]{1,0:T(8,128)(2,1)S(1)}, u32[]{:S(2)}, u32[]{:S(2)}) collective-permute-start(bf16[272,1024]{1,0:T(8,128)(2,1)S(1)} %get-tuple-element.38), channel_id=1, source_target_pairs={{0,4},{4,8},{8,12},{12,0},{16,20},{20,24},{24,28},{28,16},{32,36},... | collective-permute-start | bytes 1671176 | tf_op jit(solution)/shard_map/ppermute | solution.py:31
  33.2 22.3 %collective-permute-start.11 = (bf16[32,1408]{1,0:T(8,128)(2,1)S(1)}, bf16[32,1408]{1,0:T(8,128)(2,1)S(1)}, u32[]{:S(2)}, u32[]{:S(2)}) collective-permute-start(bf16[32,1408]{1,0:T(8,128)(2,1)S(1)} %get-tuple-element.58), channel_id=1, source_target_pairs={{0,12},{4,0},{8,4},{12,8},{16,28},{20,16},{24,20},{28,24},{32,44},... | collective-permute-start | bytes 270344 | tf_op jit(solution)/shard_map/ppermute | solution.py:31
  35.5 22.3 %collective-permute-start.12 = (bf16[32,1408]{1,0:T(8,128)(2,1)S(1)}, bf16[32,1408]{1,0:T(8,128)(2,1)S(1)}, u32[]{:S(2)}, u32[]{:S(2)}) collective-permute-start(bf16[32,1408]{1,0:T(8,128)(2,1)S(1)} %get-tuple-element.57), channel_id=1, source_target_pairs={{0,8},{4,12},{8,0},{12,4},{16,24},{20,28},{24,16},{28,20},{32,40},... | collective-permute-start | bytes 270344 | tf_op jit(solution)/shard_map/ppermute | solution.py:31
  55.5 5.8 %collective-permute-start.13 = (bf16[32,1408]{1,0:T(8,128)(2,1)S(1)}, bf16[32,1408]{1,0:T(8,128)(2,1)S(1)}, u32[]{:S(2)}, u32[]{:S(2)}) collective-permute-start(bf16[32,1408]{1,0:T(8,128)(2,1)S(1)} %get-tuple-element.56), channel_id=1, source_target_pairs={{0,4},{4,8},{8,12},{12,0},{16,20},{20,24},{24,28},{28,16},{32,36},... | collective-permute-start | bytes 270344 | tf_op jit(solution)/shard_map/ppermute | solution.py:31
  63.8 16.7 %all-to-all-start = ((bf16[8,272,128]{2,1,0:T(8,128)(2,1)}), bf16[8,272,128]{2,1,0:T(8,128)(2,1)S(1)}, u32[]{:S(2)}, u32[]{:S(2)}) async-start(bf16[8,272,128]{2,1,0:T(8,128)(2,1)} %get-tuple-element.41), calls=%async_computation | async-start | bytes 1114112 | tf_op jit(solution)/shard_map/all_to_all | solution.py:694
  73.1 16.5 %collective-permute-start.20 = (bf16[4,32,1408]{2,1,0:T(8,128)(2,1)S(1)}, bf16[4,32,1408]{2,1,0:T(8,128)(2,1)}, u32[]{:S(2)}, u32[]{:S(2)}) collective-permute-start(bf16[4,32,1408]{2,1,0:T(8,128)(2,1)S(1)} %get-tuple-element.46), channel_id=1, source_target_pairs={{0,16},{4,20},{8,24},{12,28},{16,0},{20,4},{24,8},{28,12},{32,48},... | collective-permute-start | bytes 1081352 | tf_op jit(solution)/shard_map/ppermute | solution.py:31
  82.1 14.0 %all-to-all-start.1 = ((bf16[8,512,128]{2,1,0:T(8,128)(2,1)}), bf16[8,512,128]{2,1,0:T(8,128)(2,1)S(1)}, u32[]{:S(2)}, u32[]{:S(2)}) async-start(bf16[8,512,128]{2,1,0:T(8,128)(2,1)} %shard_map.172), calls=%async_computation.1 | async-start | bytes 2097152 | tf_op jit(solution)/shard_map/all_to_all | solution.py:696
  85.8 17.0 %collective-permute-start.17 = (bf16[128,1408]{1,0:T(8,128)(2,1)S(1)}, bf16[128,1408]{1,0:T(8,128)(2,1)}, u32[]{:S(2)}, u32[]{:S(2)}) collective-permute-start(bf16[128,1408]{1,0:T(8,128)(2,1)S(1)} %bitcast.26), channel_id=1, source_target_pairs={{0,96},{4,100},{8,104},{12,108},{16,112},{20,116},{24,120},{28,124... | collective-permute-start | bytes 1081352 | tf_op jit(solution)/shard_map/ppermute | solution.py:31
  88.4 16.3 %collective-permute-start.18 = (bf16[128,1408]{1,0:T(8,128)(2,1)S(1)}, bf16[128,1408]{1,0:T(8,128)(2,1)}, u32[]{:S(2)}, u32[]{:S(2)}) collective-permute-start(bf16[128,1408]{1,0:T(8,128)(2,1)S(1)} %bitcast.27), channel_id=1, source_target_pairs={{0,64},{4,68},{8,72},{12,76},{16,80},{20,84},{24,88},{28,92},{32,9... | collective-permute-start | bytes 1081352 | tf_op jit(solution)/shard_map/ppermute | solution.py:31
  89.0 22.1 %collective-permute-start.19 = (bf16[128,1408]{1,0:T(8,128)(2,1)S(1)}, bf16[128,1408]{1,0:T(8,128)(2,1)}, u32[]{:S(2)}, u32[]{:S(2)}) collective-permute-start(bf16[128,1408]{1,0:T(8,128)(2,1)S(1)} %bitcast.28), channel_id=1, source_target_pairs={{0,32},{4,36},{8,40},{12,44},{16,48},{20,52},{24,56},{28,60},{32,6... | collective-permute-start | bytes 1081352 | tf_op jit(solution)/shard_map/ppermute | solution.py:31
  89.6 27.3 %collective-permute-start.21 = (bf16[128,1408]{1,0:T(8,128)(2,1)}, bf16[128,1408]{1,0:T(8,128)(2,1)}, u32[]{:S(2)}, u32[]{:S(2)}) collective-permute-start(bf16[128,1408]{1,0:T(8,128)(2,1)} %bitcast.16.refs_6_), channel_id=1, source_target_pairs={{0,96},{4,100},{8,104},{12,108},{16,112},{20,116},{24,120},{28,124... | collective-permute-start | bytes 1081352 | tf_op jit(solution)/shard_map/ppermute | solution.py:31
  102.6 14.2 %collective-permute-start.15 = (bf16[256,1024]{1,0:T(8,128)(2,1)S(1)}, bf16[256,1024]{1,0:T(8,128)(2,1)S(1)}, u32[]{:S(2)}, u32[]{:S(2)}) collective-permute-start(bf16[256,1024]{1,0:T(8,128)(2,1)S(1)} %get-tuple-element.44), channel_id=1, source_target_pairs={{0,12},{4,0},{8,4},{12,8},{16,28},{20,16},{24,20},{28,24},{32,44},... | collective-permute-start | bytes 1572872 | tf_op jit(solution)/shard_map/ppermute | solution.py:31
  102.8 17.1 %collective-permute-start.16 = (bf16[256,1024]{1,0:T(8,128)(2,1)S(1)}, bf16[256,1024]{1,0:T(8,128)(2,1)S(1)}, u32[]{:S(2)}, u32[]{:S(2)}) collective-permute-start(bf16[256,1024]{1,0:T(8,128)(2,1)S(1)} %get-tuple-element.45), channel_id=1, source_target_pairs={{0,4},{4,8},{8,12},{12,0},{16,20},{20,24},{24,28},{28,16},{32,36},... | collective-permute-start | bytes 1572872 | tf_op jit(solution)/shard_map/ppermute | solution.py:31
  104.8 24.3 %collective-permute-start.24 = (bf16[1024,256]{1,0:T(8,128)(2,1)S(1)}, bf16[1024,256]{1,0:T(8,128)(2,1)S(1)}, u32[]{:S(2)}, u32[]{:S(2)}) collective-permute-start(bf16[1024,256]{1,0:T(8,128)(2,1)S(1)} %copy-done.15), channel_id=1, source_target_pairs={{0,12},{4,0},{8,4},{12,8},{16,28},{20,16},{24,20},{28,24},{32,44},... | collective-permute-start | bytes 1572872 | tf_op jit(solution)/shard_map/ppermute | solution.py:31
  111.0 18.1 %collective-permute-start.25 = (bf16[1024,256]{1,0:T(8,128)(2,1)S(1)}, bf16[1024,256]{1,0:T(8,128)(2,1)S(1)}, u32[]{:S(2)}, u32[]{:S(2)}) collective-permute-start(bf16[1024,256]{1,0:T(8,128)(2,1)S(1)} %copy-done.13), channel_id=1, source_target_pairs={{0,8},{4,12},{8,0},{12,4},{16,24},{20,28},{24,16},{28,20},{32,40},... | collective-permute-start | bytes 1572872 | tf_op jit(solution)/shard_map/ppermute | solution.py:31
  116.9 14.2 %collective-permute-start.26 = (bf16[1024,256]{1,0:T(8,128)(2,1)S(1)}, bf16[1024,256]{1,0:T(8,128)(2,1)S(1)}, u32[]{:S(2)}, u32[]{:S(2)}) collective-permute-start(bf16[1024,256]{1,0:T(8,128)(2,1)S(1)} %shard_map.178), channel_id=1, source_target_pairs={{0,4},{4,8},{8,12},{12,0},{16,20},{20,24},{24,28},{28,16},{32,36},... | collective-permute-start | bytes 1572872 | tf_op jit(solution)/shard_map/ppermute | solution.py:31
  116.9 8.1 %collective-permute-start.22 = (bf16[128,1408]{1,0:T(8,128)(2,1)}, bf16[128,1408]{1,0:T(8,128)(2,1)S(1)}, u32[]{:S(2)}, u32[]{:S(2)}) collective-permute-start(bf16[128,1408]{1,0:T(8,128)(2,1)} %bitcast.16.refs_6_), channel_id=1, source_target_pairs={{0,64},{4,68},{8,72},{12,76},{16,80},{20,84},{24,88},{28,92},{32,9... | collective-permute-start | bytes 1081352 | tf_op jit(solution)/shard_map/ppermute | solution.py:31
  119.9 9.2 %collective-permute-start.23 = (bf16[128,1408]{1,0:T(8,128)(2,1)}, bf16[128,1408]{1,0:T(8,128)(2,1)S(1)}, u32[]{:S(2)}, u32[]{:S(2)}) collective-permute-start(bf16[128,1408]{1,0:T(8,128)(2,1)} %bitcast.16.refs_6_), channel_id=1, source_target_pairs={{0,32},{4,36},{8,40},{12,44},{16,48},{20,52},{24,56},{28,60},{32,6... | collective-permute-start | bytes 1081352 | tf_op jit(solution)/shard_map/ppermute | solution.py:31
  139.4 16.7 %collective-permute-start.27 = (bf16[4,2,256,256]{3,2,1,0:T(8,128)(2,1)S(1)}, bf16[4,2,256,256]{3,2,1,0:T(8,128)(2,1)S(1)}, u32[]{:S(2)}, u32[]{:S(2)}) collective-permute-start(bf16[4,2,256,256]{3,2,1,0:T(8,128)(2,1)S(1)} %get-tuple-element.49), channel_id=1, source_target_pairs={{0,1},{1,0},{2,3},{3,2},{4,5},{5,4},{6,7},{7,6},{8,9},{9,8},{10,11... | collective-permute-start | bytes 3145736 | tf_op jit(solution)/shard_map/ppermute | solution.py:734
  153.9 30.3 %collective-permute-start.14 = (bf16[256,1024]{1,0:T(8,128)(2,1)S(1)}, bf16[256,1024]{1,0:T(8,128)(2,1)S(1)}, u32[]{:S(2)}, u32[]{:S(2)}) collective-permute-start(bf16[256,1024]{1,0:T(8,128)(2,1)S(1)} %get-tuple-element.42), channel_id=1, source_target_pairs={{0,8},{4,12},{8,0},{12,4},{16,24},{20,28},{24,16},{28,20},{32,40},... | collective-permute-start | bytes 1572872 | tf_op jit(solution)/shard_map/ppermute | solution.py:31
  157.0 18.2 %collective-permute-start.28 = (bf16[2,256,256]{2,1,0:T(8,128)(2,1)S(1)}, bf16[2,256,256]{2,1,0:T(8,128)(2,1)S(1)}, u32[]{:S(2)}, u32[]{:S(2)}) collective-permute-start(bf16[2,256,256]{2,1,0:T(8,128)(2,1)S(1)} %get-tuple-element.51), channel_id=1, source_target_pairs={{0,4},{4,8},{8,12},{12,0},{16,20},{20,24},{24,28},{28,16},{32,36},... | collective-permute-start | bytes 786440 | tf_op jit(solution)/shard_map/ppermute | solution.py:31
  157.1 18.1 %collective-permute-start.29 = (bf16[2,256,256]{2,1,0:T(8,128)(2,1)S(1)}, bf16[2,256,256]{2,1,0:T(8,128)(2,1)S(1)}, u32[]{:S(2)}, u32[]{:S(2)}) collective-permute-start(bf16[2,256,256]{2,1,0:T(8,128)(2,1)S(1)} %get-tuple-element.52), channel_id=1, source_target_pairs={{0,12},{4,0},{8,4},{12,8},{16,28},{20,16},{24,20},{28,24},{32,44},... | collective-permute-start | bytes 786440 | tf_op jit(solution)/shard_map/ppermute | solution.py:31
  159.7 20.4 %collective-permute-start.30 = (bf16[2,256,256]{2,1,0:T(8,128)(2,1)S(1)}, bf16[2,256,256]{2,1,0:T(8,128)(2,1)S(1)}, u32[]{:S(2)}, u32[]{:S(2)}) collective-permute-start(bf16[2,256,256]{2,1,0:T(8,128)(2,1)S(1)} %get-tuple-element.53), channel_id=1, source_target_pairs={{0,8},{4,12},{8,0},{12,4},{16,24},{20,28},{24,16},{28,20},{32,40},... | collective-permute-start | bytes 786440 | tf_op jit(solution)/shard_map/ppermute | solution.py:31
  180.8 6.4 %collective-permute-start.31 = (bf16[256,256]{1,0:T(8,128)(2,1)S(1)}, bf16[256,256]{1,0:T(8,128)(2,1)S(1)}, u32[]{:S(2)}, u32[]{:S(2)}) collective-permute-start(bf16[256,256]{1,0:T(8,128)(2,1)S(1)} %get-tuple-element.55), channel_id=1, source_target_pairs={{0,2},{1,3},{2,0},{3,1},{4,6},{5,7},{6,4},{7,5},{8,10},{9,11},{10,... | collective-permute-start | bytes 393224 | tf_op jit(solution)/shard_map/ppermute | solution.py:746
  (42 other events, 270.5 us)
